TPU v7x, 128 devices: a whole 4x4x4 slice. The times are simulated.
128 devices in a mesh: gx: 4 (over y_hi, core), gy: 4 (over z), ta: 8 (over x, y_lo).
Axes of the slice: x: 4, y: 4 (y_hi: 2, y_lo: 2; y = y_hi * 2 + y_lo), z: 4, core: 2. Of those that a mesh axis runs over, the one named last changes fastest.
Arguments:
- features: bfloat16 [32, 16, 16, 128, 256], P('ta', 'gx', 'gy'), may hold values from -6 to 6
- neighbours: int32 [16, 16, 4], P('gx', 'gy'), may hold values from 0 to 8, as said below
- adjacency: int32 [16, 16, 4, 128, 128], P('gx', 'gy'), may hold values 0 or 1
- w_space: bfloat16 [256, 256], replicated, may hold values from -0.375 to 0.375
- w_time: bfloat16 [3, 256, 256], replicated, may hold values from -0.21875 to 0.21875
- cotangent: bfloat16 [32, 16, 16, 128, 256], P('ta', 'gx', 'gy'), may hold values from -6 to 6
Outputs:
- updated: bfloat16 [32, 16, 16, 128, 256], P('ta', 'gx', 'gy')
- grad_space: float32 [256, 256], replicated
- grad_time: float32 [3, 256, 256], replicated
Inputs may be any that keep to these rules, and one draw needn't show every extreme that they name: `neighbours`: the 4 codes of a tile are distinct; code c names the tile c // 3 - 1 tiles away along x and c % 3 - 1 tiles away along y, periodically.
All inputs are finite; a program needn't handle non-finite values. No bound on the sum of `adjacency` on one device may be relied on, other than what follows from the above.
Results may differ from a plain program's by a relative error of at most 0.0068.
Values may be sent and summed in bfloat16 or wider, within the bound.
No kernel may reach another device: no remote copies, remote signals or barrier semaphores. Data moves between devices by JAX's collectives and lax.ppermute only.
A program may use at most 128 MiB of HBM per device.

v0:
```python
import math

import jax
import jax.numpy as jnp
from jax import lax
from jax.sharding import PartitionSpec as P


def with_halo(block, sides, width):
    for axis, dim in sides:
        count = lax.axis_size(axis)
        forward = [(i, i + 1) for i in range(count - 1)]
        forward.append((count - 1, 0))
        backward = [(target, source) for source, target in forward]
        low = lax.ppermute(
            lax.slice_in_dim(block, block.shape[dim] - width, None, axis=dim), axis, forward
        )
        high = lax.ppermute(lax.slice_in_dim(block, 0, width, axis=dim), axis, backward)
        block = jnp.concatenate([low, block, high], axis=dim)
    return block


def from_behind(block, axis, distance):
    devices = range(lax.axis_size(axis))
    route = [(i - distance, i) for i in devices if i - distance in devices]
    return lax.ppermute(block, axis, route)


def shards(features, neighbours, adjacency, w_space, w_time, cotangent):
    frames, tiles_x, tiles_y, lipids, feat_width = features.shape
    tap_count = w_time.shape[0]
    slot_count = neighbours.shape[2]
    behind = tap_count - 1
    tile_count = tiles_x * tiles_y
    row_count = tile_count * lipids
    extended = with_halo(features, (("gx", 1), ("gy", 2)), 1)
    flat_tiles = extended.reshape(frames, (tiles_x + 2) * (tiles_y + 2), lipids, feat_width)
    along_x = jnp.arange(tiles_x, dtype=jnp.int32)[:, None]
    along_y = jnp.arange(tiles_y, dtype=jnp.int32)[None, :]
    summed = jnp.zeros((frames, tile_count, lipids, feat_width), jnp.float32)
    for slot_pos in range(slot_count):
        offset_code = neighbours[:, :, slot_pos]
        source_index = (
            (along_x + offset_code // 3) * (tiles_y + 2) + along_y + offset_code % 3
        ).reshape(-1)
        picked = jnp.take(flat_tiles, source_index, axis=1)
        lipid_mask = (
            adjacency[:, :, slot_pos].reshape(tile_count, lipids, lipids).astype(jnp.bfloat16)
        )
        summed = summed + jnp.einsum(
            "tij,ftjc->ftic", lipid_mask, picked, preferred_element_type=jnp.float32
        )
    aggregate = (0.18 * summed).astype(jnp.bfloat16).reshape(frames * row_count, feat_width)
    projected = jnp.dot(aggregate, w_space, preferred_element_type=jnp.float32).astype(jnp.bfloat16)
    projected = projected.reshape(frames, row_count, feat_width)
    mixed = jnp.zeros((frames, row_count, feat_width), jnp.float32)
    blank = jnp.zeros((behind, row_count, feat_width), jnp.bfloat16)
    padded = jnp.concatenate([blank, projected, blank], axis=0)
    for offset in range(tap_count):
        window = padded[behind - offset : behind - offset + frames].reshape(-1, feat_width)
        mixed = mixed + jnp.dot(window, w_time[offset], preferred_element_type=jnp.float32).reshape(
            frames, row_count, feat_width
        )
    partial_terms = jnp.zeros((behind, row_count, feat_width), jnp.float32)
    for offset in range(1, tap_count):
        window = padded[behind + frames - offset : behind + frames - offset + behind].reshape(
            -1, feat_width
        )
        partial_terms = partial_terms + jnp.dot(
            window, w_time[offset], preferred_element_type=jnp.float32
        ).reshape(behind, row_count, feat_width)
    carried = from_behind(partial_terms, "ta", 1)
    mixed = mixed + jnp.concatenate(
        [carried, jnp.zeros((frames - behind, row_count, feat_width), jnp.float32)], axis=0
    )
    sigmoid_z = jax.nn.sigmoid(mixed)
    own = features.reshape(frames, row_count, feat_width).astype(jnp.float32)
    updated = (own + mixed * sigmoid_z).astype(jnp.bfloat16).reshape(features.shape)
    grad_in = cotangent.reshape(frames, row_count, feat_width).astype(jnp.float32)
    grad_mixed = (grad_in * sigmoid_z * (1.0 + mixed * (1.0 - sigmoid_z))).astype(jnp.bfloat16)
    next_grads = from_behind(grad_mixed[:behind], "ta", -1)
    joined = jnp.concatenate([grad_mixed, next_grads], axis=0)
    proj_rows = projected.reshape(-1, feat_width)
    contract = (((0,), (0,)), ((), ()))
    row_scale = 1.0 / math.sqrt(
        frames * row_count * lax.axis_size("gx") * lax.axis_size("gy") * lax.axis_size("ta")
    )
    parts = []
    for offset in range(tap_count):
        later = joined[offset : offset + frames].reshape(-1, feat_width)
        parts.append(
            lax.dot_general(proj_rows, later, contract, preferred_element_type=jnp.float32)
        )
    grad_proj = jnp.zeros((frames * row_count, feat_width), jnp.float32)
    for offset in range(tap_count):
        later = joined[offset : offset + frames].reshape(-1, feat_width)
        grad_proj = grad_proj + jnp.dot(later, w_time[offset].T, preferred_element_type=jnp.float32)
    grad_proj = grad_proj.astype(jnp.bfloat16)
    grad_space, grad_time = lax.psum(
        (
            lax.dot_general(aggregate, grad_proj, contract, preferred_element_type=jnp.float32),
            jnp.stack(parts),
        ),
        ("gx", "gy", "ta"),
    )
    return (updated, grad_space * row_scale, grad_time * row_scale)


def solution(mesh):
    in_specs = (
        P("ta", "gx", "gy", None, None),
        P("gx", "gy", None),
        P("gx", "gy", None, None, None),
        P(),
        P(),
        P("ta", "gx", "gy", None, None),
    )
    out_specs = (P("ta", "gx", "gy", None, None), P(), P())
    return jax.shard_map(shards, mesh=mesh, in_specs=in_specs, out_specs=out_specs, check_vma=False)
```

profile of v0, /device:TPU:1, one launch (start us, length us, event | category | flops | bytes accessed | tf_op | source)
XLA Modules:
  0.0 478.1 jit_solution(4176581645567628972)
XLA Ops:
  7.2 1.8 fusion.64
  9.1 4.4 collective-permute-start
  13.5 22.5 %collective-permute-done = bf16[4,1,4,128,256]{4,3,2,1,0:T(8,128)(2,1)S(1)} collective-permute-done((bf16[4,1,4,128,256]{4,3,2,1,0:T(8,128)(2,1)S(1)}, bf16[4,1,4,128,256]{4,3,2,1,0:T(8,128)(2,1)S(1)}, u32[]{:S(2)}, u32[]{:S(2)}) %collective-permute-start) | collective-permute-done | bytes 1048608 | tf_op jit(solution)/shard_map/ppermute | solution.py:15
  36.1 0.5 constant_dynamic-update-slice_fusion.1
  36.6 0.3 collective-permute-done.1
  36.9 2.7 copy-done.4
  39.6 1.9 fusion.63
  41.5 1.7 collective-permute-start.2
  43.2 2.1 collective-permute-start.3
  45.5 0.4 fusion.54
  46.3 0.7 divide_reduce_fusion
  47.7 2.8 convert.11
  50.6 1.1 fusion.65
  51.7 28.7 %collective-permute-done.2 = bf16[4,6,1,128,256]{4,3,2,1,0:T(8,128)(2,1)S(1)} collective-permute-done((bf16[4,6,1,128,256]{4,3,2,1,0:T(8,128)(2,1)}, bf16[4,6,1,128,256]{4,3,2,1,0:T(8,128)(2,1)S(1)}, u32[]{:S(2)}, u32[]{:S(2)}) %collective-permute-start.2) | collective-permute-done | bytes 1572896 | tf_op jit(solution)/shard_map/ppermute | solution.py:15
  80.4 5.7 %pad_maximum_fusion = bf16[4,6,6,128,256]{4,3,2,1,0:T(8,128)(2,1)} fusion(bf16[4,6,1,128,256]{4,3,2,1,0:T(8,128)(2,1)} %collective-permute-done.3, bf16[4,6,4,128,256]{4,3,2,1,0:T(8,128)(2,1)S(1)} %copy-done.5, bf16[4,6,1,128,256]{4,3,2,1,0:T(8,128)(2,1)S(1)} %collective-permute-done.2), kind=kLoop, calls=%fused_computation.8 | loop fusion | flops 9437184 | bytes 18874368 | tf_op jit(solution)/shard_map/concatenate | solution.py:19
  86.1 6.4 %gather_fusion.3 = bf16[16,4,128,256]{3,2,1,0:T(8,128)(2,1)} fusion(bf16[4,36,128,256]{3,2,1,0:T(8,128)(2,1)} %bitcast.110, s32[1024]{0:T(1024)S(1)} %get-tuple-element.44), kind=kCustom, calls=%fused_computation.3.clone | custom fusion | bytes 8388672 | tf_op jit(solution)/shard_map/jit(_take)/gather | solution.py:46
  92.5 6.5 %gather_fusion.2 = bf16[16,4,128,256]{3,2,1,0:T(8,128)(2,1)} fusion(bf16[4,36,128,256]{3,2,1,0:T(8,128)(2,1)} %bitcast.111, s32[1024]{0:T(1024)S(1)} %get-tuple-element.45), kind=kCustom, calls=%fused_computation.2.clone | custom fusion | bytes 8388672 | tf_op jit(solution)/shard_map/jit(_take)/gather | solution.py:46
  99.0 6.6 %gather_fusion.1 = bf16[16,4,128,256]{3,2,1,0:T(8,128)(2,1)} fusion(bf16[4,36,128,256]{3,2,1,0:T(8,128)(2,1)} %bitcast.112, s32[1024]{0:T(1024)S(1)} %get-tuple-element.46), kind=kCustom, calls=%fused_computation.1.clone | custom fusion | bytes 8388672 | tf_op jit(solution)/shard_map/jit(_take)/gather | solution.py:46
  105.6 6.5 %gather_fusion = bf16[16,4,128,256]{3,2,1,0:T(8,128)(2,1)} fusion(bf16[4,36,128,256]{3,2,1,0:T(8,128)(2,1)} %bitcast.113, s32[1024]{0:T(1024)S(1)} %get-tuple-element.47), kind=kCustom, calls=%fused_computation.clone | custom fusion | bytes 8388672 | tf_op jit(solution)/shard_map/jit(_take)/gather | solution.py:46
  112.1 3.8 fusion.8
  115.9 4.5 fusion.12
  120.5 4.5 fusion.10
  125.0 10.2 %fusion.5 = bf16[4,16,128,256]{3,2,0,1:T(8,128)(2,1)} fusion(f32[16,4,256,128]{2,3,1,0:T(8,128)S(1)} %fusion.8, f32[16,4,256,128]{2,3,1,0:T(8,128)} %fusion.12, f32[16,4,256,128]{2,3,1,0:T(8,128)} %fusion.10, bf16[16,128,128,1]{2,1,3,0:T(8,128)(2,1)S(1)} %bitcast.119, bf16[16,4,128,256]{3,2,1,0:T(8,128)(2,1)} %gather_fusion.3, ...), kind=kOutput, calls=%fused_computation.20 | convolution fusion | flops 549453824 | bytes 34078736 | tf_op jit(solution)/shard_map/tij,ftjc->ftic/dot_general | solution.py:50
  135.2 2.5 copy.9
  137.7 1.2 convolution_convert_fusion
  138.9 0.6 copy-done.3
  139.7 0.9 copy-done.9
  140.6 0.7 fusion.29
  141.3 0.7 convolution_add_fusion.2
  142.0 4.1 collective-permute-start.4
  146.2 4.5 fusion.35
  150.6 4.5 fusion.38
  155.1 78.7 %collective-permute-done.4 = f32[2,2048,256]{2,1,0:T(8,128)} collective-permute-done((f32[2,2048,256]{2,1,0:T(8,128)S(1)}, f32[2,2048,256]{2,1,0:T(8,128)}, u32[]{:S(2)}, u32[]{:S(2)}) %collective-permute-start.4) | collective-permute-done | bytes 4194336 | tf_op jit(solution)/shard_map/ppermute | solution.py:26
  233.8 14.0 %fusion.2 = (bf16[4,2048,256]{2,1,0:T(8,128)(2,1)S(1)}, bf16[4,2048,256]{2,1,0:T(8,128)(2,1)}) fusion(bf16[4,4,4,128,256]{4,3,2,1,0:T(8,128)(2,1)} %param.13, bf16[4,4,4,128,256]{4,3,2,1,0:T(8,128)(2,1)} %param.8, f32[2,2048,256]{2,1,0:T(8,128)} %collective-permute-done.4, bf16[4,2048,256]{2,1,0:T(8,128)(2,1)S(1)} %bitcast.105, ...), kind=kOutput, calls=%fused_computation.11 | convolution fusion | flops 572522496 | bytes 42074112 | tf_op jit(solution)/shard_map/dot_general | solution.py:61
  247.9 1.3 collective-permute-start.5
  249.2 1.3 fusion.40
  250.5 1.3 convolution_bitcast_fusion.2
  251.8 45.1 %collective-permute-done.5 = bf16[2,2048,256]{2,1,0:T(8,128)(2,1)S(1)} collective-permute-done((bf16[2,2048,256]{2,1,0:T(8,128)(2,1)S(1)}, bf16[2,2048,256]{2,1,0:T(8,128)(2,1)S(1)}, u32[]{:S(2)}, u32[]{:S(2)}) %collective-permute-start.5) | collective-permute-done | bytes 2097184 | tf_op jit(solution)/shard_map/ppermute | solution.py:26
  296.9 0.8 pad_maximum_fusion.1
  297.8 1.3 convolution_bitcast_fusion.1
  299.1 0.7 copy-done.2
  299.8 1.3 convolution_bitcast_fusion
  301.1 4.5 convolution_add_fusion.1
  305.6 9.1 %fusion.28 = f32[256,256]{1,0:T(8,128)} fusion(bf16[8192,256]{1,0:T(8,128)(2,1)} %bitcast.117, f32[8192,256]{1,0:T(8,128)} %convolution_add_fusion.1, bf16[8192,256]{1,0:T(8,128)(2,1)} %bitcast.115, bf16[3,256,256]{2,1,0:T(8,128)(2,1)S(1)} %copy-done.9), kind=kOutput, calls=%fused_computation.47 | convolution fusion | flops 2151677952 | bytes 17170432 | tf_op jit(solution)/shard_map/dot_general | solution.py:101
  314.7 0.9 pad_maximum_fusion.2
  315.7 151.8 %all-reduce.6.cloned.1.call-done = (f32[256,256]{1,0:T(8,128)}, f32[3,256,256]{2,1,0:T(8,128)}) async-done(((f32[256,256]{1,0:T(8,128)}, f32[3,256,256]{2,1,0:T(8,128)}), (f32[256,256]{1,0:T(8,128)}, f32[3,256,256]{2,1,0:T(8,128)})) %all-reduce.6.cloned.1.call-update) | async-done | bytes 1048592 | tf_op jit(solution)/shard_map/psum | solution.py:99
  467.5 1.7 broadcast_multiply_fusion.1
  469.1 2.1 broadcast_multiply_fusion
  (47 shorter events, 1.8 us)
Async XLA Ops:
  7.2 130.5 %copy-start = (bf16[256,256]{1,0:T(8,128)(2,1)S(1)}, bf16[256,256]{1,0:T(8,128)(2,1)}, u32[]{:S(2)}) copy-start(bf16[256,256]{1,0:T(8,128)(2,1)} %param.11) | copy-start | bytes 393220
  7.2 460.3 %all-reduce.6.cloned.1.call-start = ((), (), s32[]{:S(2)}) async-start(), calls=%async_computation | async-start | bytes 2097152 | tf_op jit(solution)/shard_map/psum | solution.py:99
  7.2 28.8 %copy-start.8 = (bf16[4,4,4,128,256]{4,3,2,1,0:T(8,128)(2,1)S(1)}, bf16[4,4,4,128,256]{4,3,2,1,0:T(8,128)(2,1)}, u32[]{:S(2)}) copy-start(bf16[4,4,4,128,256]{4,3,2,1,0:T(8,128)(2,1)} %param.8) | copy-start | bytes 12582916
  9.1 26.9 %collective-permute-start = (bf16[4,1,4,128,256]{4,3,2,1,0:T(8,128)(2,1)S(1)}, bf16[4,1,4,128,256]{4,3,2,1,0:T(8,128)(2,1)S(1)}, u32[]{:S(2)}, u32[]{:S(2)}) collective-permute-start(bf16[4,1,4,128,256]{4,3,2,1,0:T(8,128)(2,1)S(1)} %get-tuple-element.33), channel_id=1, source_target_pairs={{0,32},{32,64},{64,96},{96,0},{1,33},{33,65},{65,97},{97,1},{2,34}... | collective-permute-start | bytes 3145736 | tf_op jit(solution)/shard_map/ppermute | solution.py:15
  13.5 23.4 %collective-permute-start.1 = (bf16[4,1,4,128,256]{4,3,2,1,0:T(8,128)(2,1)S(1)}, bf16[4,1,4,128,256]{4,3,2,1,0:T(8,128)(2,1)S(1)}, u32[]{:S(2)}, u32[]{:S(2)}) collective-permute-start(bf16[4,1,4,128,256]{4,3,2,1,0:T(8,128)(2,1)S(1)} %get-tuple-element.32), channel_id=1, source_target_pairs={{32,0},{64,32},{96,64},{0,96},{33,1},{65,33},{97,65},{1,97},{34,2}... | collective-permute-start | bytes 3145736 | tf_op jit(solution)/shard_map/ppermute | solution.py:18
  36.6 8.9 %copy-start.11 = (s32[4,4,4]{2,1,0:T(4,128)S(1)}, s32[4,4,4]{2,1,0:T(4,128)}, u32[]{:S(2)}) copy-start(s32[4,4,4]{2,1,0:T(4,128)} %param.9) | copy-start | bytes 772
  36.9 2.7 copy-start.4
  41.5 38.9 %collective-permute-start.2 = (bf16[4,6,1,128,256]{4,3,2,1,0:T(8,128)(2,1)}, bf16[4,6,1,128,256]{4,3,2,1,0:T(8,128)(2,1)S(1)}, u32[]{:S(2)}, u32[]{:S(2)}) collective-permute-start(bf16[4,6,1,128,256]{4,3,2,1,0:T(8,128)(2,1)} %get-tuple-element.30), channel_id=1, source_target_pairs={{0,8},{8,16},{16,24},{24,0},{1,9},{9,17},{17,25},{25,1},{2,10},{10... | collective-permute-start | bytes 4718600 | tf_op jit(solution)/shard_map/ppermute | solution.py:15
  43.2 37.2 %collective-permute-start.3 = (bf16[4,6,1,128,256]{4,3,2,1,0:T(8,128)(2,1)}, bf16[4,6,1,128,256]{4,3,2,1,0:T(8,128)(2,1)}, u32[]{:S(2)}, u32[]{:S(2)}) collective-permute-start(bf16[4,6,1,128,256]{4,3,2,1,0:T(8,128)(2,1)} %get-tuple-element.31), channel_id=1, source_target_pairs={{8,0},{16,8},{24,16},{0,24},{9,1},{17,9},{25,17},{1,25},{10,2},{18... | collective-permute-start | bytes 4718600 | tf_op jit(solution)/shard_map/ppermute | solution.py:18
  47.6 32.7 %copy-start.5 = (bf16[4,6,4,128,256]{4,3,2,1,0:T(8,128)(2,1)S(1)}, bf16[4,6,4,128,256]{4,3,2,1,0:T(8,128)(2,1)}, u32[]{:S(2)}) copy-start(bf16[4,6,4,128,256]{4,3,2,1,0:T(8,128)(2,1)} %copy-done.4) | copy-start | bytes 18874372
  112.1 3.8 copy-start.7
  112.1 3.8 copy-start.10
  115.9 4.6 copy-start.6
  137.7 1.9 copy-start.3
  139.6 1.0 copy-start.9
  142.0 91.8 %collective-permute-start.4 = (f32[2,2048,256]{2,1,0:T(8,128)S(1)}, f32[2,2048,256]{2,1,0:T(8,128)}, u32[]{:S(2)}, u32[]{:S(2)}) collective-permute-start(f32[2,2048,256]{2,1,0:T(8,128)S(1)} %convolution_add_fusion.2), channel_id=1, source_target_pairs={{0,1},{1,2},{2,3},{3,4},{4,5},{5,6},{6,7},{8,9},{9,10},{10,11},{11... | collective-permute-start | bytes 12582920 | tf_op jit(solution)/shard_map/ppermute | solution.py:26
  247.9 49.0 %collective-permute-start.5 = (bf16[2,2048,256]{2,1,0:T(8,128)(2,1)S(1)}, bf16[2,2048,256]{2,1,0:T(8,128)(2,1)S(1)}, u32[]{:S(2)}, u32[]{:S(2)}) collective-permute-start(bf16[2,2048,256]{2,1,0:T(8,128)(2,1)S(1)} %slice.118), channel_id=1, source_target_pairs={{1,0},{2,1},{3,2},{4,3},{5,4},{6,5},{7,6},{9,8},{10,9},{11,10},{12... | collective-permute-start | bytes 6291464 | tf_op jit(solution)/shard_map/ppermute | solution.py:26
  297.8 2.0 copy-start.2
  305.6 165.6 %copy-start.1 = (bf16[256,256]{1,0:T(8,128)(2,1)S(1)}, bf16[256,256]{1,0:T(8,128)(2,1)}, u32[]{:S(2)}) copy-start(bf16[256,256]{1,0:T(8,128)(2,1)} %param.11) | copy-start | bytes 393220
Sparse Core Ops, SparseCore 0:
  315.8 151.6 all-reduce.5
where the time goes:
time: 479 us; the launch traced here: 478 us
  waiting for transfers between devices  327 us (68%)
  matrix products  67.5 us (14%)
  local copies, waits for them, and re-layouts  40.2 us (8%)
  other arithmetic  15.3 us (3%)
  between operations  14.3 us (3%)
  starting transfers between devices  13.7 us (3%)
    psum x1, waiting for transfers between devices, shards(): lax.psum((lax.dot_general(aggregate, grad_proj, contract, preferred_eleme...  152 us
    ppermute x2, waiting for transfers between devices, from_behind(): return lax.ppermute(block, axis, route)  124 us
    ppermute x2, waiting for transfers between devices, with_halo(): lax.ppermute(lax.slice_in_dim(block, block.shape[dim] - width, None, axis...  51.2 us
    gather x4, local copies, waits for them, and re-layouts, shards(): picked = jnp.take(flat_tiles, source_index, axis=1)  25.9 us
    dot_general x5, matrix products, shards(): jnp.dot(window, w_time[offset], preferred_element_type=jnp.float32)  24.4 us
    dot_general x4, matrix products, shards(): jnp.einsum('tij,ftjc->ftic', lipid_mask, picked, preferred_element_type=j...  23.1 us
  transfers between devices with their start and end apart: 7, of which 6 were waited for; matrix products, arithmetic and copies ran while one was open for 4% of the time, Pallas kernels for 0%

commit v1 on v0

v1 whole, which is shorter than its diff:
```python
import functools
import math

import jax
import jax.numpy as jnp
import numpy as np
from jax import lax
from jax.experimental import pallas as pl
from jax.experimental.pallas import tpu as pltpu
from jax.sharding import Mesh
from jax.sharding import PartitionSpec as P

BF16 = jnp.bfloat16
F32 = jnp.float32
GX = ("yh", "core")
EVERY = ("yh", "core", "gy", "ta")


def ring(count, step):
    return [(i, (i + step) % count) for i in range(count)]


def whole_vmem():
    return pl.BlockSpec(memory_space=pltpu.VMEM)


def prep_kernel(adj_ref, ws_ref, wt_ref, mask_ref, v_ref):
    slots, lipids = adj_ref.shape[1], adj_ref.shape[2]
    width = ws_ref.shape[1]
    for k in range(slots):
        mask_ref[0, :, k * lipids : (k + 1) * lipids] = (
            adj_ref[0, k].astype(F32).astype(BF16)
        )

    @pl.when(pl.program_id(0) == 0)
    def _():
        for j in range(wt_ref.shape[0]):
            v_ref[j * width : (j + 1) * width, :] = jnp.dot(
                ws_ref[...], wt_ref[j], preferred_element_type=F32
            ).astype(BF16)


def prep(adjacency, w_space, w_time):
    tiles, slots, lipids, _ = adjacency.shape
    taps, width, _ = w_time.shape
    return pl.pallas_call(
        prep_kernel,
        grid=(tiles,),
        in_specs=[
            pl.BlockSpec((1, slots, lipids, lipids), lambda i: (i, 0, 0, 0)),
            pl.BlockSpec((width, width), lambda i: (0, 0)),
            pl.BlockSpec((taps, width, width), lambda i: (0, 0, 0)),
        ],
        out_specs=[
            pl.BlockSpec((1, lipids, slots * lipids), lambda i: (i, 0, 0)),
            pl.BlockSpec((taps * width, width), lambda i: (0, 0)),
        ],
        out_shape=[
            jax.ShapeDtypeStruct((tiles, lipids, slots * lipids), BF16),
            jax.ShapeDtypeStruct((taps * width, width), BF16),
        ],
        cost_estimate=pl.CostEstimate(
            flops=2 * taps * width**3, bytes_accessed=8 << 20, transcendentals=0
        ),
        name="prep",
    )(adjacency, w_space, w_time)


def agg_kernel(
    first, codes, feat, xlo, xhi, ylo, yhi, clo, chi, mask_ref, out_ref, ext, sems
):
    frames, nx, ny = out_ref.shape[:3]
    own = feat.at[pl.ds(first, frames)]
    moves = [
        (own, ext.at[:, 1 : nx + 1, 1 : ny + 1]),
        (xlo, ext.at[:, 0:1, 1 : ny + 1]),
        (xhi, ext.at[:, nx + 1 : nx + 2, 1 : ny + 1]),
        (ylo, ext.at[:, 1 : nx + 1, 0:1]),
        (yhi, ext.at[:, 1 : nx + 1, ny + 1 : ny + 2]),
        (clo.at[:, 0:1], ext.at[:, 0:1, 0:1]),
        (clo.at[:, 1:2], ext.at[:, nx + 1 : nx + 2, 0:1]),
        (chi.at[:, 0:1], ext.at[:, 0:1, ny + 1 : ny + 2]),
        (chi.at[:, 1:2], ext.at[:, nx + 1 : nx + 2, ny + 1 : ny + 2]),
    ]
    copies = [
        pltpu.make_async_copy(src, dst, sems.at[i]) for i, (src, dst) in enumerate(moves)
    ]
    for copy in copies:
        copy.start()
    for copy in copies:
        copy.wait()
    slots = mask_ref.shape[2] // mask_ref.shape[1]
    for x in range(nx):
        for y in range(ny):
            tile = x * ny + y
            places = []
            for k in range(slots):
                code = codes[tile * slots + k]
                places.append((x + lax.div(code, 3), y + lax.rem(code, 3)))
            mask = mask_ref[tile]
            for f in range(frames):
                source = jnp.concatenate([ext[f, sx, sy] for sx, sy in places], axis=0)
                summed = jnp.dot(mask, source, preferred_element_type=F32)
                out_ref[f, x, y] = (0.18 * summed).astype(BF16)


def aggregate(first, frames, codes, features, halo, mask):
    _, nx, ny, lipids, width = features.shape
    anywhere = pl.BlockSpec(memory_space=pl.ANY)
    flops = 2 * frames * nx * ny * lipids * mask.shape[2] * width
    return pl.pallas_call(
        functools.partial(agg_kernel, first),
        in_specs=[pl.BlockSpec(memory_space=pltpu.SMEM)] + [anywhere] * 7 + [whole_vmem()],
        out_specs=whole_vmem(),
        out_shape=jax.ShapeDtypeStruct((frames, nx, ny, lipids, width), BF16),
        scratch_shapes=[
            pltpu.VMEM((frames, nx + 2, ny + 2, lipids, width), BF16),
            pltpu.SemaphoreType.DMA((9,)),
        ],
        compiler_params=pltpu.CompilerParams(vmem_limit_bytes=40 << 20),
        cost_estimate=pl.CostEstimate(
            flops=flops, bytes_accessed=12 << 20, transcendentals=0
        ),
        name="aggregate",
    )(codes, features, *halo, mask)


def mix_kernel(p_ref, q_ref, feat_ref, cot_ref, v_ref, *rest):
    *given, up_ref, g_ref = rest

    @pl.when(pl.program_id(0) == 0)
    def _():
        g_ref[...] = given[0][...] if given else jnp.zeros_like(g_ref)

    before = [p_ref[0], p_ref[1], q_ref[0], q_ref[1]]
    rows, grads = [], []
    for f in range(2):
        left = jnp.concatenate([before[f + 2], before[f + 1], before[f]], axis=1)
        mixed = jnp.dot(left, v_ref[...], preferred_element_type=F32)
        s = 0.5 * jnp.tanh(0.5 * mixed) + 0.5
        up_ref[f] = (feat_ref[f].astype(F32) + mixed * s).astype(BF16)
        grad = cot_ref[f].astype(F32) * s * (1.0 + mixed * (1.0 - s))
        rows.append(left)
        grads.append(grad.astype(BF16))
    left = jnp.concatenate(rows, axis=0)
    grad = jnp.concatenate(grads, axis=0)
    g_ref[...] += lax.dot_general(
        left, grad, (((0,), (0,)), ((), ())), preferred_element_type=F32
    )


def mix(half, prev, now, features, cotangent, v, given=()):
    frames, count, width = now.shape
    rows = 512
    taps = v.shape[0] // width
    pair = pl.BlockSpec((frames, rows, width), lambda i: (0, i, 0))
    here = pl.BlockSpec((frames, rows, width), lambda i: (half, i, 0))
    full_v = pl.BlockSpec((taps * width, width), lambda i: (0, 0))
    return pl.pallas_call(
        mix_kernel,
        grid=(count // rows,),
        in_specs=[pair, pair, here, here, full_v]
        + ([full_v, pl.BlockSpec(memory_space=pl.ANY)] if given else []),
        out_specs=[here, full_v],
        out_shape=[
            jax.ShapeDtypeStruct(features.shape, BF16),
            jax.ShapeDtypeStruct((taps * width, width), F32),
        ],
        input_output_aliases={6: 0} if given else {},
        compiler_params=pltpu.CompilerParams(vmem_limit_bytes=40 << 20),
        cost_estimate=pl.CostEstimate(
            flops=4 * frames * count * taps * width * width,
            bytes_accessed=10 << 20,
            transcendentals=frames * count * width,
        ),
        name="mix",
    )(prev, now, features, cotangent, v, *given)


def finish_kernel(scale, g_ref, ws_ref, wt_ref, space_ref, time_ref):
    width = ws_ref.shape[0]
    space = jnp.zeros((width, width), F32)
    for j in range(wt_ref.shape[0]):
        g = g_ref[j * width : (j + 1) * width, :]
        high = g.astype(BF16)
        low = (g - high.astype(F32)).astype(BF16)
        time = 0.0
        for part in (low, high):
            time = time + lax.dot_general(
                ws_ref[...], part, (((0,), (0,)), ((), ())), preferred_element_type=F32
            )
            space = space + lax.dot_general(
                part, wt_ref[j], (((1,), (1,)), ((), ())), preferred_element_type=F32
            )
        time_ref[j] = time * scale
    space_ref[...] = space * scale


def finish(scale, total, w_space, w_time):
    return pl.pallas_call(
        functools.partial(finish_kernel, scale),
        in_specs=[whole_vmem()] * 3,
        out_specs=[whole_vmem()] * 2,
        out_shape=[
            jax.ShapeDtypeStruct(w_space.shape, F32),
            jax.ShapeDtypeStruct(w_time.shape, F32),
        ],
        name="finish",
    )(total, w_space, w_time)


def halo_of(part, nx, ny):
    x_up, x_down = ring(4, 1), ring(4, -1)
    xlo = lax.ppermute(part[:, nx - 1 :], GX, x_up)
    xhi = lax.ppermute(part[:, :1], GX, x_down)
    ylo = lax.ppermute(part[:, :, ny - 1 :], "gy", x_up)
    yhi = lax.ppermute(part[:, :, :1], "gy", x_down)
    clo = lax.ppermute(
        jnp.concatenate([xlo[:, :, ny - 1 :], xhi[:, :, ny - 1 :]], axis=1), "gy", x_up
    )
    chi = lax.ppermute(
        jnp.concatenate([xlo[:, :, :1], xhi[:, :, :1]], axis=1), "gy", x_down
    )
    return xlo, xhi, ylo, yhi, clo, chi


def all_sum(total):
    rows, width = total.shape
    count = lax.axis_size(EVERY)
    block = 8
    padded = jnp.pad(total, ((0, count * block - rows), (0, 0)))
    mine = lax.all_to_all(
        padded.reshape(count, block, width), EVERY, 0, 0, tiled=True
    ).sum(axis=0)
    spread = jnp.broadcast_to(mine[None], (count, block, width))
    back = lax.all_to_all(spread, EVERY, 0, 0, tiled=True)
    return back.reshape(count * block, width)[:rows]


def shards(features, neighbours, adjacency, w_space, w_time, cotangent):
    frames, nx, ny, lipids, width = features.shape
    count = nx * ny * lipids
    codes = neighbours.reshape(-1)
    halo_b = halo_of(features[2:4], nx, ny)
    halo_a = halo_of(features[0:2], nx, ny)
    mask, v = prep(adjacency.reshape(nx * ny, -1, lipids, lipids), w_space, w_time)
    agg_b = aggregate(2, 2, codes, features, halo_b, mask).reshape(2, count, width)
    prev = lax.ppermute(agg_b, "ta", [(i, i + 1) for i in range(7)])
    agg_a = aggregate(0, 2, codes, features, halo_a, mask).reshape(2, count, width)
    feat = features.reshape(frames, count, width)
    cot = cotangent.reshape(frames, count, width)
    updated, total = mix(1, agg_a, agg_b, feat, cot, v)
    updated, total = mix(0, prev, agg_a, feat, cot, v, (total, updated))
    total = all_sum(total)
    scale = 1.0 / math.sqrt(frames * count * lax.axis_size(EVERY))
    grad_space, grad_time = finish(scale, total, w_space, w_time)
    return updated.reshape(features.shape), grad_space, grad_time


def solution(mesh):
    gx, gy, ta = (mesh.shape[a] for a in ("gx", "gy", "ta"))
    fine = Mesh(
        np.asarray(mesh.devices).reshape(2, gx // 2, gy, ta), ("yh", "core", "gy", "ta")
    )
    in_specs = (
        P("ta", GX, "gy", None, None),
        P(GX, "gy", None),
        P(GX, "gy", None, None, None),
        P(),
        P(),
        P("ta", GX, "gy", None, None),
    )
    out_specs = (P("ta", GX, "gy", None, None), P(), P())
    return jax.shard_map(shards, mesh=fine, in_specs=in_specs, out_specs=out_specs, check_vma=False)
```

time: 479 us -> 186 us (0.39)
  waiting for transfers between devices: 327 us -> 64.9 us
  matrix products: 67.5 us -> 0 us
  blocking collectives: 0 us -> 51.8 us
  Pallas kernels: 0 us -> 33 us
  local copies, waits for them, and re-layouts: 40.2 us -> 9.07 us
  other arithmetic: 15.3 us -> 0.95 us
  between operations: 14.3 us -> 0.84 us
  starting transfers between devices: 13.7 us -> 25.3 us
    psum x1 -> x0, waiting for transfers between devices: 152 us -> none  [shards(): lax.psum((lax.dot_general(aggregate, grad_proj, contract, preferred_eleme...]
    ppermute x6 -> x13, waiting for transfers between devices: 175 us -> 64.9 us  [the longest x2 57.8 us: halo_of(): xhi = lax.ppermute(part[:, :1], GX, x_down)]
    dot_general x16 -> x0, matrix products: 67.5 us -> none  [the longest x5 24.4 us: shards(): jnp.dot(window, w_time[offset], preferred_element_type=jnp.float32)]
    all_to_all x0 -> x2, blocking collectives: none -> 51.8 us  [the longest x1 28.4 us: all_sum(): lax.all_to_all(padded.reshape(count, block, width), EVERY, 0, 0, tiled=True)]
    pallas_call x0 -> x6, Pallas kernels: none -> 33 us  [the longest x2 14.6 us: mix(): pl.pallas_call(mix_kernel, grid=(count // rows,), in_specs=[pair, pair, h...]
    gather x4 -> x0, local copies, waits for them, and re-layouts: 25.9 us -> none  [shards(): picked = jnp.take(flat_tiles, source_index, axis=1)]
    ppermute x6 -> x13, starting transfers between devices: 13.7 us -> 25.3 us  [the longest x2 5.49 us: halo_of(): yhi = lax.ppermute(part[:, :, :1], 'gy', x_down)]
    concatenate x2 -> x4, other arithmetic: 6.57 us -> 0.81 us  [the longest x2 0.75 us: halo_of(): jnp.concatenate([xlo[:, :, :1], xhi[:, :, :1]], axis=1)]
  transfers between devices with their start and end apart: 7 -> 13, of which waited for: 6 -> 4; matrix products, arithmetic and copies ran while one was open for 4% -> 1% of each run, Pallas kernels for 0% -> 11%
where the time goes in v1:
time: 186 us
  waiting for transfers between devices  64.9 us (35%)
  blocking collectives  51.8 us (28%)
  Pallas kernels  33 us (18%)
  starting transfers between devices  25.3 us (14%)
  local copies, waits for them, and re-layouts  9.07 us (5%)
    ppermute x2, waiting for transfers between devices, halo_of(): xhi = lax.ppermute(part[:, :1], GX, x_down)  57.8 us
    all_to_all x1, blocking collectives, all_sum(): lax.all_to_all(padded.reshape(count, block, width), EVERY, 0, 0, tiled=True)  28.4 us
    all_to_all x1, blocking collectives, all_sum(): back = lax.all_to_all(spread, EVERY, 0, 0, tiled=True)  23.4 us
    pallas_call x2, Pallas kernels, mix(): pl.pallas_call(mix_kernel, grid=(count // rows,), in_specs=[pair, pair, h...  14.6 us
    pallas_call x1, Pallas kernels, prep(): pl.pallas_call(prep_kernel, grid=(tiles,), in_specs=[pl.BlockSpec((1, slo...  10.4 us
    ppermute x2, waiting for transfers between devices, halo_of(): lax.ppermute(jnp.concatenate([xlo[:, :, ny - 1:], xhi[:, :, ny - 1:]], ax...  5.76 us
    ppermute x2, starting transfers between devices, halo_of(): yhi = lax.ppermute(part[:, :, :1], 'gy', x_down)  5.49 us
    ppermute x2, starting transfers between devices, halo_of(): xlo = lax.ppermute(part[:, nx - 1:], GX, x_up)  5.39 us
  transfers between devices with their start and end apart: 13, of which 4 were waited for; matrix products, arithmetic and copies ran while one was open for 1% of the time, Pallas kernels for 11%

profile of v1, /device:TPU:1, one launch (start us, length us, event | category | flops | bytes accessed | tf_op | source)
XLA Modules:
  0.0 185.8 jit_solution(8447208362488884960)
XLA Ops:
  0.6 0.0 copy-start
  0.6 2.6 %fusion.1 = (bf16[2,1,4,128,256]{4,3,2,1,0:T(8,128)(2,1)}, bf16[2,1,4,128,256]{4,3,2,1,0:T(8,128)(2,1)S(1)}, bf16[2,1,4,128,256]{4,3,2,1,0:T(8,128)(2,1)S(1)}, bf16[2,1,4,128,256]{4,3,2,1,0:T(8,128)(2,1)S(1)}) fusion(bf16[4,4,4,128,256]{4,3,2,1,0:T(8,128)(2,1)} %feat.3), kind=kLoop, calls=%fused_computation.7 | loop fusion | bytes 4194304 | tf_op jit(solution)/shard_map/slice | solution.py:215
  3.3 1.4 collective-permute-start.1
  4.7 2.9 %collective-permute-start = (bf16[2,1,4,128,256]{4,3,2,1,0:T(8,128)(2,1)S(1)}, bf16[2,1,4,128,256]{4,3,2,1,0:T(8,128)(2,1)S(1)}, u32[]{:S(2)}, u32[]{:S(2)}) collective-permute-start(bf16[2,1,4,128,256]{4,3,2,1,0:T(8,128)(2,1)S(1)} %get-tuple-element.26), channel_id=1, source_target_pairs={{0,32},{32,64},{64,96},{96,0},{1,33},{33,65},{65,97},{97,1},{2,34}... | collective-permute-start | bytes 1572872 | tf_op jit(solution)/shard_map/ppermute | solution.py:214
  7.6 1.4 fusion
  9.0 3.8 %collective-permute-start.3 = (bf16[2,4,1,128,256]{4,3,2,1,0:T(8,128)(2,1)}, bf16[2,4,1,128,256]{4,3,2,1,0:T(8,128)(2,1)S(1)}, u32[]{:S(2)}, u32[]{:S(2)}) collective-permute-start(bf16[2,4,1,128,256]{4,3,2,1,0:T(8,128)(2,1)} %get-tuple-element.21), channel_id=1, source_target_pairs={{0,24},{8,0},{16,8},{24,16},{1,25},{9,1},{17,9},{25,17},{2,26},{10... | collective-permute-start | bytes 1572872 | tf_op jit(solution)/shard_map/ppermute | solution.py:217
  12.7 0.0 collective-permute-start.2
  12.7 5.2 %collective-permute-done.1.xhi = bf16[2,1,4,128,256]{4,3,2,1,0:T(8,128)(2,1)S(1)} collective-permute-done((bf16[2,1,4,128,256]{4,3,2,1,0:T(8,128)(2,1)S(1)}, bf16[2,1,4,128,256]{4,3,2,1,0:T(8,128)(2,1)S(1)}, u32[]{:S(2)}, u32[]{:S(2)}) %collective-permute-start.1) | collective-permute-done | bytes 524320 | tf_op jit(solution)/shard_map/ppermute | solution.py:215
  17.9 1.4 collective-permute-done.xlo
  19.4 1.7 collective-permute-start.4
  21.1 0.7 pad_maximum_fusion.1
  21.8 2.1 %collective-permute-start.5 = (bf16[2,2,1,128,256]{4,3,2,1,0:T(8,128)(2,1)}, bf16[2,2,1,128,256]{4,3,2,1,0:T(8,128)(2,1)S(1)}, u32[]{:S(2)}, u32[]{:S(2)}) collective-permute-start(bf16[2,2,1,128,256]{4,3,2,1,0:T(8,128)(2,1)} %pad_maximum_fusion.1), channel_id=1, source_target_pairs={{0,24},{8,0},{16,8},{24,16},{1,25},{9,1},{17,9},{25,17},{2,26},{10... | collective-permute-start | bytes 786440 | tf_op jit(solution)/shard_map/ppermute | solution.py:221
  23.9 0.1 reshape.33.codes
  24.0 10.4 %prep.1 = (bf16[16,128,512]{2,1,0:T(8,128)(2,1)}, bf16[768,256]{1,0:T(8,128)(2,1)}) custom-call(s32[16,4,128,128]{3,2,1,0:T(8,128)} %bitcast.19, bf16[256,256]{1,0:T(8,128)(2,1)} %ws_ref.3, bf16[3,256,256]{2,1,0:T(8,128)(2,1)} %wt_ref.3), custom_call_target="tpu_custom_call" | custom-call | flops 100663296 | bytes 8388608 | tf_op jit(solution)/shard_map/prep/pallas_call | solution.py:46
  34.5 0.0 collective-permute-done.3.yhi
  34.5 0.0 collective-permute-done.2.ylo
  34.5 0.0 collective-permute-done.4.clo
  34.5 0.0 collective-permute-done.5.chi
  34.5 0.0 copy-start.1
  34.5 2.2 %copy-done.1 = bf16[4,4,4,128,256]{4,3,2,1,0:T(8,128)(2,1)S(1)} copy-done((bf16[4,4,4,128,256]{4,3,2,1,0:T(8,128)(2,1)S(1)}, bf16[4,4,4,128,256]{4,3,2,1,0:T(8,128)(2,1)}, u32[]{:S(2)}) %copy-start.1) | copy-done | bytes 4194328
  36.7 1.6 copy-done.4
  38.3 2.5 %aggregate.2 = bf16[2,4,4,128,256]{4,3,2,1,0:T(8,128)(2,1)S(1)} custom-call(s32[64]{0:T(128)S(1)} %reshape.33.codes, bf16[4,4,4,128,256]{4,3,2,1,0:T(8,128)(2,1)S(1)} %copy-done.1, bf16[2,1,4,128,256]{4,3,2,1,0:T(8,128)(2,1)S(1)} %collective-permute-done.xlo, bf16[2,1,4,128,256]{4,3,2,1,0:T(8,128)(2,1)S(1)} %collective-permute-done.1.xhi, ...), custom_call_target="tpu_custom_call" | custom-call | flops 1073741824 | bytes 12582912 | tf_op jit(solution)/shard_map/aggregate/pallas_call | solution.py:111
  40.8 3.7 %collective-permute-start.6 = (bf16[2,2048,256]{2,1,0:T(8,128)(2,1)S(1)}, bf16[2,2048,256]{2,1,0:T(8,128)(2,1)}, u32[]{:S(2)}, u32[]{:S(2)}) collective-permute-start(bf16[2,2048,256]{2,1,0:T(8,128)(2,1)S(1)} %bitcast.16), channel_id=1, source_target_pairs={{0,1},{1,2},{2,3},{3,4},{4,5},{5,6},{6,7},{8,9},{9,10},{10,11},{11... | collective-permute-start | bytes 6291464 | tf_op jit(solution)/shard_map/ppermute | solution.py:248
  44.5 2.6 %collective-permute-start.8 = (bf16[2,1,4,128,256]{4,3,2,1,0:T(8,128)(2,1)S(1)}, bf16[2,1,4,128,256]{4,3,2,1,0:T(8,128)(2,1)S(1)}, u32[]{:S(2)}, u32[]{:S(2)}) collective-permute-start(bf16[2,1,4,128,256]{4,3,2,1,0:T(8,128)(2,1)S(1)} %copy-done.7), channel_id=1, source_target_pairs={{0,96},{32,0},{64,32},{96,64},{1,97},{33,1},{65,33},{97,65},{2,98}... | collective-permute-start | bytes 1572872 | tf_op jit(solution)/shard_map/ppermute | solution.py:215
  47.1 2.5 %collective-permute-start.7 = (bf16[2,1,4,128,256]{4,3,2,1,0:T(8,128)(2,1)S(1)}, bf16[2,1,4,128,256]{4,3,2,1,0:T(8,128)(2,1)S(1)}, u32[]{:S(2)}, u32[]{:S(2)}) collective-permute-start(bf16[2,1,4,128,256]{4,3,2,1,0:T(8,128)(2,1)S(1)} %get-tuple-element.24), channel_id=1, source_target_pairs={{0,32},{32,64},{64,96},{96,0},{1,33},{33,65},{65,97},{97,1},{2,34}... | collective-permute-start | bytes 1572872 | tf_op jit(solution)/shard_map/ppermute | solution.py:214
  49.7 1.7 collective-permute-start.10
  51.4 0.0 collective-permute-start.9
  51.4 52.6 %collective-permute-done.8.xhi = bf16[2,1,4,128,256]{4,3,2,1,0:T(8,128)(2,1)S(1)} collective-permute-done((bf16[2,1,4,128,256]{4,3,2,1,0:T(8,128)(2,1)S(1)}, bf16[2,1,4,128,256]{4,3,2,1,0:T(8,128)(2,1)S(1)}, u32[]{:S(2)}, u32[]{:S(2)}) %collective-permute-start.8) | collective-permute-done | bytes 524320 | tf_op jit(solution)/shard_map/ppermute | solution.py:215
  104.0 0.0 collective-permute-done.7.xlo
  104.1 0.1 collective-permute-start.11
  104.2 0.0 copy-start.2
  104.2 0.0 copy-start.3
  104.2 2.7 %collective-permute-start.12 = (bf16[2,2,1,128,256]{4,3,2,1,0:T(8,128)(2,1)S(1)}, bf16[2,2,1,128,256]{4,3,2,1,0:T(8,128)(2,1)S(1)}, u32[]{:S(2)}, u32[]{:S(2)}) collective-permute-start(bf16[2,2,1,128,256]{4,3,2,1,0:T(8,128)(2,1)S(1)} %pad_maximum_fusion.3), channel_id=1, source_target_pairs={{0,24},{8,0},{16,8},{24,16},{1,25},{9,1},{17,9},{25,17},{2,26},{10... | collective-permute-start | bytes 786440 | tf_op jit(solution)/shard_map/ppermute | solution.py:221
  107.0 0.0 collective-permute-done.10.yhi
  107.0 0.0 collective-permute-done.9.ylo
  107.0 5.8 %collective-permute-done.11.clo = bf16[2,2,1,128,256]{4,3,2,1,0:T(8,128)(2,1)S(1)} collective-permute-done((bf16[2,2,1,128,256]{4,3,2,1,0:T(8,128)(2,1)S(1)}, bf16[2,2,1,128,256]{4,3,2,1,0:T(8,128)(2,1)S(1)}, u32[]{:S(2)}, u32[]{:S(2)}) %collective-permute-start.11) | collective-permute-done | bytes 262176 | tf_op jit(solution)/shard_map/ppermute | solution.py:218
  112.7 0.0 collective-permute-done.12.chi
  112.7 2.5 %aggregate.3 = bf16[2,4,4,128,256]{4,3,2,1,0:T(8,128)(2,1)S(1)} custom-call(s32[64]{0:T(128)S(1)} %reshape.33.codes, bf16[4,4,4,128,256]{4,3,2,1,0:T(8,128)(2,1)S(1)} %copy-done.1, bf16[2,1,4,128,256]{4,3,2,1,0:T(8,128)(2,1)S(1)} %collective-permute-done.7.xlo, bf16[2,1,4,128,256]{4,3,2,1,0:T(8,128)(2,1)S(1)} %collective-permute-done.8.xhi, ...), custom_call_target="tpu_custom_call" | custom-call | flops 1073741824 | bytes 12582912 | tf_op jit(solution)/shard_map/aggregate/pallas_call | solution.py:111
  115.3 7.0 %mix.2 = (bf16[4,2048,256]{2,1,0:T(8,128)(2,1)}, f32[768,256]{1,0:T(8,128)S(1)}) custom-call(bf16[2,2048,256]{2,1,0:T(8,128)(2,1)S(1)} %bitcast.12, bf16[2,2048,256]{2,1,0:T(8,128)(2,1)S(1)} %bitcast.17, bf16[4,2048,256]{2,1,0:T(8,128)(2,1)S(1)} %bitcast.10, bf16[4,2048,256]{2,1,0:T(8,128)(2,1)S(1)} %bitcast.14, bf16[768,256]{1,0:T(8,128)(2,1)S(1)} %copy-done.5), custom_call_target="tpu_custom_call" | custom-call | flops 3221225472 | bytes 10485760 | tf_op jit(solution)/shard_map/mix/pallas_call | solution.py:159
  122.3 0.0 collective-permute-done.6.p_ref
  122.3 7.7 %mix.3 = (bf16[4,2048,256]{2,1,0:T(8,128)(2,1)}, f32[768,256]{1,0:T(8,128)S(1)}) custom-call(bf16[2,2048,256]{2,1,0:T(8,128)(2,1)} %collective-permute-done.6.p_ref, bf16[2,2048,256]{2,1,0:T(8,128)(2,1)S(1)} %bitcast.13, bf16[4,2048,256]{2,1,0:T(8,128)(2,1)S(1)} %bitcast.11, bf16[4,2048,256]{2,1,0:T(8,128)(2,1)S(1)} %bitcast.15, ...), custom_call_target="tpu_custom_call", output_to_operand_aliasing={{0}: (6, {})} | custom-call | flops 3221225472 | bytes 10485760 | tf_op jit(solution)/shard_map/mix/pallas_call | solution.py:159
  129.9 0.1 pad_bitcast_fusion
  130.0 28.4 %all_to_all.10 = f32[128,8,256]{2,1,0:T(8,128)S(1)} all-to-all(f32[128,8,256]{2,1,0:T(8,128)S(1)} %pad_bitcast_fusion), channel_id=1, replica_groups=mesh['yh'=2,'core'=2,'gy'=4,'ta'=8] {'yh','core','gy','ta'}, dimensions={0} | all-to-all | bytes 2097152 | tf_op jit(solution)/shard_map/all_to_all | solution.py:232
  158.4 0.1 reduce_sum.9
  158.6 0.1 broadcast_in_dim.2
  158.7 23.4 %all_to_all.11 = f32[128,8,256]{2,1,0:T(8,128)S(1)} all-to-all(f32[128,8,256]{2,1,0:T(8,128)S(1)} %broadcast_in_dim.2), channel_id=1, replica_groups=mesh['yh'=2,'core'=2,'gy'=4,'ta'=8] {'yh','core','gy','ta'}, dimensions={0} | all-to-all | bytes 2097152 | tf_op jit(solution)/shard_map/all_to_all | solution.py:236
  182.0 0.9 slice_bitcast_fusion.g_ref
  183.0 2.9 %finish.1 = (f32[256,256]{1,0:T(8,128)}, f32[3,256,256]{2,1,0:T(8,128)}) custom-call(f32[768,256]{1,0:T(8,128)} %slice_bitcast_fusion.g_ref, bf16[256,256]{1,0:T(8,128)(2,1)} %ws_ref.3, bf16[3,256,256]{2,1,0:T(8,128)(2,1)} %wt_ref.3), custom_call_target="tpu_custom_call" | custom-call | tf_op jit(solution)/shard_map/finish/pallas_call | solution.py:200
  (19 shorter events, 0.2 us)
Async XLA Ops:
  0.6 7.0 %copy-start = (bf16[4,4,4,128,256]{4,3,2,1,0:T(8,128)(2,1)S(1)}, bf16[4,4,4,128,256]{4,3,2,1,0:T(8,128)(2,1)}, u32[]{:S(2)}) copy-start(bf16[4,4,4,128,256]{4,3,2,1,0:T(8,128)(2,1)} %feat.3) | copy-start | bytes 12582916
  3.3 20.7 %copy-start.8 = (s32[4,4,4]{2,1,0:T(4,128)S(1)}, s32[4,4,4]{2,1,0:T(4,128)}, u32[]{:S(2)}) copy-start(s32[4,4,4]{2,1,0:T(4,128)} %param.7) | copy-start | bytes 772
  3.3 14.6 %collective-permute-start.1 = (bf16[2,1,4,128,256]{4,3,2,1,0:T(8,128)(2,1)S(1)}, bf16[2,1,4,128,256]{4,3,2,1,0:T(8,128)(2,1)S(1)}, u32[]{:S(2)}, u32[]{:S(2)}) collective-permute-start(bf16[2,1,4,128,256]{4,3,2,1,0:T(8,128)(2,1)S(1)} %get-tuple-element.25), channel_id=1, source_target_pairs={{0,96},{32,0},{64,32},{96,64},{1,97},{33,1},{65,33},{97,65},{2,98}... | collective-permute-start | bytes 1572872 | tf_op jit(solution)/shard_map/ppermute | solution.py:215
  4.7 14.6 %collective-permute-start = (bf16[2,1,4,128,256]{4,3,2,1,0:T(8,128)(2,1)S(1)}, bf16[2,1,4,128,256]{4,3,2,1,0:T(8,128)(2,1)S(1)}, u32[]{:S(2)}, u32[]{:S(2)}) collective-permute-start(bf16[2,1,4,128,256]{4,3,2,1,0:T(8,128)(2,1)S(1)} %get-tuple-element.26), channel_id=1, source_target_pairs={{0,32},{32,64},{64,96},{96,0},{1,33},{33,65},{65,97},{97,1},{2,34}... | collective-permute-start | bytes 1572872 | tf_op jit(solution)/shard_map/ppermute | solution.py:214
  9.0 25.5 %collective-permute-start.3 = (bf16[2,4,1,128,256]{4,3,2,1,0:T(8,128)(2,1)}, bf16[2,4,1,128,256]{4,3,2,1,0:T(8,128)(2,1)S(1)}, u32[]{:S(2)}, u32[]{:S(2)}) collective-permute-start(bf16[2,4,1,128,256]{4,3,2,1,0:T(8,128)(2,1)} %get-tuple-element.21), channel_id=1, source_target_pairs={{0,24},{8,0},{16,8},{24,16},{1,25},{9,1},{17,9},{25,17},{2,26},{10... | collective-permute-start | bytes 1572872 | tf_op jit(solution)/shard_map/ppermute | solution.py:217
  12.7 21.7 %collective-permute-start.2 = (bf16[2,4,1,128,256]{4,3,2,1,0:T(8,128)(2,1)}, bf16[2,4,1,128,256]{4,3,2,1,0:T(8,128)(2,1)S(1)}, u32[]{:S(2)}, u32[]{:S(2)}) collective-permute-start(bf16[2,4,1,128,256]{4,3,2,1,0:T(8,128)(2,1)} %get-tuple-element.22), channel_id=1, source_target_pairs={{0,8},{8,16},{16,24},{24,0},{1,9},{9,17},{17,25},{25,1},{2,10},{10... | collective-permute-start | bytes 1572872 | tf_op jit(solution)/shard_map/ppermute | solution.py:216
  19.4 15.1 %collective-permute-start.4 = (bf16[2,2,1,128,256]{4,3,2,1,0:T(8,128)(2,1)S(1)}, bf16[2,2,1,128,256]{4,3,2,1,0:T(8,128)(2,1)S(1)}, u32[]{:S(2)}, u32[]{:S(2)}) collective-permute-start(bf16[2,2,1,128,256]{4,3,2,1,0:T(8,128)(2,1)S(1)} %pad_maximum_fusion), channel_id=1, source_target_pairs={{0,8},{8,16},{16,24},{24,0},{1,9},{9,17},{17,25},{25,1},{2,10},{10... | collective-permute-start | bytes 786440 | tf_op jit(solution)/shard_map/ppermute | solution.py:218
  21.8 12.7 %collective-permute-start.5 = (bf16[2,2,1,128,256]{4,3,2,1,0:T(8,128)(2,1)}, bf16[2,2,1,128,256]{4,3,2,1,0:T(8,128)(2,1)S(1)}, u32[]{:S(2)}, u32[]{:S(2)}) collective-permute-start(bf16[2,2,1,128,256]{4,3,2,1,0:T(8,128)(2,1)} %pad_maximum_fusion.1), channel_id=1, source_target_pairs={{0,24},{8,0},{16,8},{24,16},{1,25},{9,1},{17,9},{25,17},{2,26},{10... | collective-permute-start | bytes 786440 | tf_op jit(solution)/shard_map/ppermute | solution.py:221
  34.5 2.2 %copy-start.1 = (bf16[4,4,4,128,256]{4,3,2,1,0:T(8,128)(2,1)S(1)}, bf16[4,4,4,128,256]{4,3,2,1,0:T(8,128)(2,1)}, u32[]{:S(2)}) copy-start(bf16[4,4,4,128,256]{4,3,2,1,0:T(8,128)(2,1)} %feat.3) | copy-start | bytes 12582916
  36.7 1.6 copy-start.4
  38.3 6.2 %copy-start.7 = (bf16[2,1,4,128,256]{4,3,2,1,0:T(8,128)(2,1)S(1)}, bf16[2,1,4,128,256]{4,3,2,1,0:T(8,128)(2,1)}, u32[]{:S(2)}) copy-start(bf16[2,1,4,128,256]{4,3,2,1,0:T(8,128)(2,1)} %get-tuple-element.23) | copy-start | bytes 1572868
  40.8 81.5 %collective-permute-start.6 = (bf16[2,2048,256]{2,1,0:T(8,128)(2,1)S(1)}, bf16[2,2048,256]{2,1,0:T(8,128)(2,1)}, u32[]{:S(2)}, u32[]{:S(2)}) collective-permute-start(bf16[2,2048,256]{2,1,0:T(8,128)(2,1)S(1)} %bitcast.16), channel_id=1, source_target_pairs={{0,1},{1,2},{2,3},{3,4},{4,5},{5,6},{6,7},{8,9},{9,10},{10,11},{11... | collective-permute-start | bytes 6291464 | tf_op jit(solution)/shard_map/ppermute | solution.py:248
  44.5 59.5 %collective-permute-start.8 = (bf16[2,1,4,128,256]{4,3,2,1,0:T(8,128)(2,1)S(1)}, bf16[2,1,4,128,256]{4,3,2,1,0:T(8,128)(2,1)S(1)}, u32[]{:S(2)}, u32[]{:S(2)}) collective-permute-start(bf16[2,1,4,128,256]{4,3,2,1,0:T(8,128)(2,1)S(1)} %copy-done.7), channel_id=1, source_target_pairs={{0,96},{32,0},{64,32},{96,64},{1,97},{33,1},{65,33},{97,65},{2,98}... | collective-permute-start | bytes 1572872 | tf_op jit(solution)/shard_map/ppermute | solution.py:215
  47.1 56.9 %collective-permute-start.7 = (bf16[2,1,4,128,256]{4,3,2,1,0:T(8,128)(2,1)S(1)}, bf16[2,1,4,128,256]{4,3,2,1,0:T(8,128)(2,1)S(1)}, u32[]{:S(2)}, u32[]{:S(2)}) collective-permute-start(bf16[2,1,4,128,256]{4,3,2,1,0:T(8,128)(2,1)S(1)} %get-tuple-element.24), channel_id=1, source_target_pairs={{0,32},{32,64},{64,96},{96,0},{1,33},{33,65},{65,97},{97,1},{2,34}... | collective-permute-start | bytes 1572872 | tf_op jit(solution)/shard_map/ppermute | solution.py:214
  49.7 57.3 %collective-permute-start.10 = (bf16[2,4,1,128,256]{4,3,2,1,0:T(8,128)(2,1)}, bf16[2,4,1,128,256]{4,3,2,1,0:T(8,128)(2,1)S(1)}, u32[]{:S(2)}, u32[]{:S(2)}) collective-permute-start(bf16[2,4,1,128,256]{4,3,2,1,0:T(8,128)(2,1)} %get-tuple-element.19), channel_id=1, source_target_pairs={{0,24},{8,0},{16,8},{24,16},{1,25},{9,1},{17,9},{25,17},{2,26},{10... | collective-permute-start | bytes 1572872 | tf_op jit(solution)/shard_map/ppermute | solution.py:217
  51.4 55.6 %collective-permute-start.9 = (bf16[2,4,1,128,256]{4,3,2,1,0:T(8,128)(2,1)}, bf16[2,4,1,128,256]{4,3,2,1,0:T(8,128)(2,1)S(1)}, u32[]{:S(2)}, u32[]{:S(2)}) collective-permute-start(bf16[2,4,1,128,256]{4,3,2,1,0:T(8,128)(2,1)} %get-tuple-element.20), channel_id=1, source_target_pairs={{0,8},{8,16},{16,24},{24,0},{1,9},{9,17},{17,25},{25,1},{2,10},{10... | collective-permute-start | bytes 1572872 | tf_op jit(solution)/shard_map/ppermute | solution.py:216
  104.1 8.6 %collective-permute-start.11 = (bf16[2,2,1,128,256]{4,3,2,1,0:T(8,128)(2,1)S(1)}, bf16[2,2,1,128,256]{4,3,2,1,0:T(8,128)(2,1)S(1)}, u32[]{:S(2)}, u32[]{:S(2)}) collective-permute-start(bf16[2,2,1,128,256]{4,3,2,1,0:T(8,128)(2,1)S(1)} %pad_maximum_fusion.2), channel_id=1, source_target_pairs={{0,8},{8,16},{16,24},{24,0},{1,9},{9,17},{17,25},{25,1},{2,10},{10... | collective-permute-start | bytes 786440 | tf_op jit(solution)/shard_map/ppermute | solution.py:218
  104.2 11.1 %copy-start.2 = (bf16[4,4,4,128,256]{4,3,2,1,0:T(8,128)(2,1)S(1)}, bf16[4,4,4,128,256]{4,3,2,1,0:T(8,128)(2,1)}, u32[]{:S(2)}) copy-start(bf16[4,4,4,128,256]{4,3,2,1,0:T(8,128)(2,1)} %feat.3) | copy-start | bytes 12582916
  104.2 11.1 %copy-start.3 = (bf16[4,4,4,128,256]{4,3,2,1,0:T(8,128)(2,1)S(1)}, bf16[4,4,4,128,256]{4,3,2,1,0:T(8,128)(2,1)}, u32[]{:S(2)}) copy-start(bf16[4,4,4,128,256]{4,3,2,1,0:T(8,128)(2,1)} %param.11) | copy-start | bytes 12582916
  104.2 11.1 %copy-start.5 = (bf16[768,256]{1,0:T(8,128)(2,1)S(1)}, bf16[768,256]{1,0:T(8,128)(2,1)}, u32[]{:S(2)}) copy-start(bf16[768,256]{1,0:T(8,128)(2,1)} %get-tuple-element.12.v_ref) | copy-start | bytes 1179652
  104.2 8.5 %collective-permute-start.12 = (bf16[2,2,1,128,256]{4,3,2,1,0:T(8,128)(2,1)S(1)}, bf16[2,2,1,128,256]{4,3,2,1,0:T(8,128)(2,1)S(1)}, u32[]{:S(2)}, u32[]{:S(2)}) collective-permute-start(bf16[2,2,1,128,256]{4,3,2,1,0:T(8,128)(2,1)S(1)} %pad_maximum_fusion.3), channel_id=1, source_target_pairs={{0,24},{8,0},{16,8},{24,16},{1,25},{9,1},{17,9},{25,17},{2,26},{10... | collective-permute-start | bytes 786440 | tf_op jit(solution)/shard_map/ppermute | solution.py:221
  115.3 7.0 %copy-start.6 = (bf16[768,256]{1,0:T(8,128)(2,1)S(1)}, bf16[768,256]{1,0:T(8,128)(2,1)}, u32[]{:S(2)}) copy-start(bf16[768,256]{1,0:T(8,128)(2,1)} %get-tuple-element.12.v_ref) | copy-start | bytes 1179652

commit v2 on v1

v2 whole, which is shorter than its diff:
```python
import functools
import math

import jax
import jax.numpy as jnp
import numpy as np
from jax import lax
from jax.experimental import pallas as pl
from jax.experimental.pallas import tpu as pltpu
from jax.sharding import Mesh
from jax.sharding import PartitionSpec as P

BF16 = jnp.bfloat16
F32 = jnp.float32
GX = ("yh", "core")
MIX_ROWS = 512
VMEM = 20 << 20
EVERY = ("yh", "core", "gy", "ta")
REST = ("yh", "gy", "ta")


def ring(count, step):
    return [(i, (i + step) % count) for i in range(count)]


def whole_vmem():
    return pl.BlockSpec(memory_space=pltpu.VMEM)


def prep_kernel(adj_ref, ws_ref, wt_ref, mask_ref, v_ref):
    slots, lipids = adj_ref.shape[1], adj_ref.shape[2]
    width = ws_ref.shape[1]
    for t in range(adj_ref.shape[0]):
        for k in range(slots):
            mask_ref[t, :, k * lipids : (k + 1) * lipids] = (
                adj_ref[t, k].astype(F32).astype(BF16)
            )

    @pl.when(pl.program_id(0) == 0)
    def _():
        for j in range(wt_ref.shape[0]):
            v_ref[j * width : (j + 1) * width, :] = jnp.dot(
                ws_ref[...], wt_ref[j], preferred_element_type=F32
            ).astype(BF16)


def prep(adjacency, w_space, w_time):
    tiles, slots, lipids, _ = adjacency.shape
    taps, width, _ = w_time.shape
    return pl.pallas_call(
        prep_kernel,
        grid=(tiles // 4,),
        in_specs=[
            pl.BlockSpec((4, slots, lipids, lipids), lambda i: (i, 0, 0, 0)),
            pl.BlockSpec((width, width), lambda i: (0, 0)),
            pl.BlockSpec((taps, width, width), lambda i: (0, 0, 0)),
        ],
        out_specs=[
            pl.BlockSpec((4, lipids, slots * lipids), lambda i: (i, 0, 0)),
            pl.BlockSpec((taps * width, width), lambda i: (0, 0)),
        ],
        out_shape=[
            jax.ShapeDtypeStruct((tiles, lipids, slots * lipids), BF16),
            jax.ShapeDtypeStruct((taps * width, width), BF16),
        ],
        compiler_params=pltpu.CompilerParams(vmem_limit_bytes=VMEM),
        cost_estimate=pl.CostEstimate(
            flops=2 * taps * width**3, bytes_accessed=8 << 20, transcendentals=0
        ),
        name="prep",
    )(adjacency, w_space, w_time)


def pack_kernel(moves, count, *refs):
    *arrays, sems = refs
    copies = [
        pltpu.make_async_copy(arrays[i].at[src], arrays[count + o].at[dst], sems.at[n])
        for n, (i, src, o, dst) in enumerate(moves)
    ]
    for copy in copies:
        copy.start()
    for copy in copies:
        copy.wait()


def pack(arrays, shapes, moves):
    anywhere = pl.BlockSpec(memory_space=pl.ANY)
    return pl.pallas_call(
        functools.partial(pack_kernel, moves, len(arrays)),
        in_specs=[anywhere] * len(arrays),
        out_specs=[anywhere] * len(shapes),
        out_shape=[jax.ShapeDtypeStruct(shape, BF16) for shape in shapes],
        scratch_shapes=[pltpu.SemaphoreType.DMA((len(moves),))],
        compiler_params=pltpu.CompilerParams(vmem_limit_bytes=VMEM),
        cost_estimate=pl.CostEstimate(flops=0, bytes_accessed=6 << 20, transcendentals=0),
        name="pack",
    )(*arrays)


def agg_kernel(first, xs, edge, codes, feat, *rest):
    *halo, mask_hbm, out_ref, ext, mask_ref, sems = rest
    frames, _, ny = out_ref.shape[:3]
    nx = feat.shape[1]
    span = pl.ds(first, frames)
    moves = [
        (feat.at[span], ext.at[:, edge : nx + edge, 1 : ny + 1]),
        (halo[0], ext.at[:, edge : nx + edge, 0:1]),
        (halo[1], ext.at[:, edge : nx + edge, ny + 1 : ny + 2]),
    ] + [
        (mask_hbm.at[x * ny : (x + 1) * ny], mask_ref.at[i * ny : (i + 1) * ny])
        for i, x in enumerate(xs)
    ]
    if edge:
        xlo, xhi, clo, chi = (ref.at[span] for ref in halo[2:])
        moves += [
            (xlo, ext.at[:, 0:1, 1 : ny + 1]),
            (xhi, ext.at[:, nx + 1 : nx + 2, 1 : ny + 1]),
            (clo.at[:, 0:1], ext.at[:, 0:1, 0:1]),
            (clo.at[:, 1:2], ext.at[:, nx + 1 : nx + 2, 0:1]),
            (chi.at[:, 0:1], ext.at[:, 0:1, ny + 1 : ny + 2]),
            (chi.at[:, 1:2], ext.at[:, nx + 1 : nx + 2, ny + 1 : ny + 2]),
        ]
    copies = [
        pltpu.make_async_copy(src, dst, sems.at[i]) for i, (src, dst) in enumerate(moves)
    ]
    for copy in copies:
        copy.start()
    for copy in copies:
        copy.wait()
    slots = mask_ref.shape[2] // mask_ref.shape[1]
    for i, x in enumerate(xs):
        for y in range(ny):
            tile = x * ny + y
            places = []
            for k in range(slots):
                code = codes[tile * slots + k]
                places.append((x - 1 + edge + lax.div(code, 3), y + lax.rem(code, 3)))
            mask = mask_ref[i * ny + y]
            for f in range(frames):
                source = jnp.concatenate([ext[f, sx, sy] for sx, sy in places], axis=0)
                summed = jnp.dot(mask, source, preferred_element_type=F32)
                out_ref[f, i, y] = (0.18 * summed).astype(BF16)


def aggregate(first, xs, codes, features, halo, mask):
    _, nx, ny, lipids, width = features.shape
    frames = 2
    slots = mask.shape[2] // lipids
    edge = 1 if len(halo) > 2 else 0
    anywhere = pl.BlockSpec(memory_space=pl.ANY)
    flops = 2 * frames * len(xs) * ny * lipids * mask.shape[2] * width
    out = pl.pallas_call(
        functools.partial(agg_kernel, first, xs, edge),
        in_specs=[
            pl.BlockSpec(memory_space=pltpu.SMEM),
            pl.BlockSpec(memory_space=pltpu.HBM),
        ]
        + [anywhere] * (len(halo) + 1),
        out_specs=whole_vmem(),
        out_shape=jax.ShapeDtypeStruct((frames, len(xs), ny, lipids, width), BF16),
        scratch_shapes=[
            pltpu.VMEM((frames, nx + 2 * edge, ny + 2, lipids, width), BF16),
            pltpu.VMEM((len(xs) * ny, lipids, slots * lipids), BF16),
            pltpu.SemaphoreType.DMA((9 + len(xs),)),
        ],
        compiler_params=pltpu.CompilerParams(vmem_limit_bytes=VMEM),
        cost_estimate=pl.CostEstimate(
            flops=flops, bytes_accessed=8 << 20, transcendentals=0
        ),
        name="aggregate",
    )(codes, features, *halo, mask)
    return out.reshape(frames, -1, width)


def mix_kernel(p_ref, q_ref, feat_ref, cot_ref, v_ref, *rest):
    *given, up_ref, g_ref = rest

    @pl.when(pl.program_id(0) == 0)
    def _():
        g_ref[...] = given[0][...] if given else jnp.zeros_like(g_ref)

    before = [p_ref[0], p_ref[1], q_ref[0], q_ref[1]]
    rows, grads = [], []
    for f in range(2):
        left = jnp.concatenate([before[f + 2], before[f + 1], before[f]], axis=1)
        mixed = jnp.dot(left, v_ref[...], preferred_element_type=F32)
        s = 0.5 * jnp.tanh(0.5 * mixed) + 0.5
        up_ref[f] = (feat_ref[f].astype(F32) + mixed * s).astype(BF16)
        grad = cot_ref[f].astype(F32) * s * (1.0 + mixed * (1.0 - s))
        rows.append(left)
        grads.append(grad.astype(BF16))
    left = jnp.concatenate(rows, axis=0)
    grad = jnp.concatenate(grads, axis=0)
    g_ref[...] += lax.dot_general(
        left, grad, (((0,), (0,)), ((), ())), preferred_element_type=F32
    )


def mix(half, place, prev, now, features, cotangent, v, given=()):
    frames, count, width = now.shape
    rows = MIX_ROWS
    taps = v.shape[0] // width
    pair = pl.BlockSpec((frames, rows, width), lambda i: (0, i, 0))
    here = pl.BlockSpec((frames, rows, width), lambda i: (half, place(i), 0))
    full_v = pl.BlockSpec((taps * width, width), lambda i: (0, 0))
    return pl.pallas_call(
        mix_kernel,
        grid=(count // rows,),
        in_specs=[pair, pair, here, here, full_v]
        + ([full_v, pl.BlockSpec(memory_space=pl.ANY)] if given else []),
        out_specs=[here, full_v],
        out_shape=[
            jax.ShapeDtypeStruct(features.shape, BF16),
            jax.ShapeDtypeStruct((taps * width, width), F32),
        ],
        input_output_aliases={6: 0} if given else {},
        compiler_params=pltpu.CompilerParams(vmem_limit_bytes=VMEM),
        cost_estimate=pl.CostEstimate(
            flops=4 * frames * count * taps * width * width,
            bytes_accessed=10 << 20,
            transcendentals=frames * count * width,
        ),
        name="mix",
    )(prev, now, features, cotangent, v, *given)


def finish_kernel(scale, g_ref, ws_ref, wt_ref, space_ref, time_ref):
    width = ws_ref.shape[0]
    space = jnp.zeros((width, width), F32)
    for j in range(wt_ref.shape[0]):
        g = g_ref[j * width : (j + 1) * width, :]
        high = g.astype(BF16)
        low = (g - high.astype(F32)).astype(BF16)
        time = 0.0
        for part in (low, high):
            time = time + lax.dot_general(
                ws_ref[...], part, (((0,), (0,)), ((), ())), preferred_element_type=F32
            )
            space = space + lax.dot_general(
                part, wt_ref[j], (((1,), (1,)), ((), ())), preferred_element_type=F32
            )
        time_ref[j] = time * scale
    space_ref[...] = space * scale


def finish(scale, total, w_space, w_time):
    return pl.pallas_call(
        functools.partial(finish_kernel, scale),
        in_specs=[whole_vmem()] * 3,
        out_specs=[whole_vmem()] * 2,
        out_shape=[
            jax.ShapeDtypeStruct(w_space.shape, F32),
            jax.ShapeDtypeStruct(w_time.shape, F32),
        ],
        compiler_params=pltpu.CompilerParams(vmem_limit_bytes=VMEM),
        name="finish",
    )(total, w_space, w_time)


def all_sum(total):
    rows, width = total.shape
    half, block = rows // 2, 8
    count = lax.axis_size(REST)
    me = lax.axis_index("core")
    keep = lax.dynamic_slice_in_dim(total, me * half, half, 0)
    give = lax.dynamic_slice_in_dim(total, (1 - me) * half, half, 0)
    mine = keep + lax.ppermute(give, "core", ring(2, 1))
    mine = jnp.pad(mine, ((0, count * block - half), (0, 0)))
    mine = lax.all_to_all(mine.reshape(count, block, width), REST, 0, 0, tiled=True)
    spread = jnp.broadcast_to(mine.sum(axis=0)[None], (count, block, width))
    back = lax.all_to_all(spread, REST, 0, 0, tiled=True)
    back = back.reshape(count * block, width)[:half]
    other = lax.ppermute(back, "core", ring(2, 1))
    return jnp.where(
        me == 0, jnp.concatenate([back, other]), jnp.concatenate([other, back])
    )


def shards(features, neighbours, adjacency, w_space, w_time, cotangent):
    frames, nx, ny, lipids, width = features.shape
    count = nx * ny * lipids
    codes = neighbours.reshape(-1)
    up, down = ring(4, 1), ring(4, -1)
    onward = [(i, i + 1) for i in range(7)]
    inner, outer = tuple(range(1, nx - 1)), (0, nx - 1)

    y_edge, x_edge = (2, nx, 1, lipids, width), (frames, 1, ny, lipids, width)
    every = slice(None)
    low, high = slice(0, 1), slice(ny - 1, ny)

    def y_halo(high_edge, low_edge):
        return lax.ppermute(high_edge, "gy", up), lax.ppermute(low_edge, "gy", down)

    y_high, y_low, x_high, x_low = pack(
        [features],
        [y_edge, y_edge, x_edge, x_edge],
        [
            (0, (slice(2, 4), every, high), 0, ()),
            (0, (slice(2, 4), every, low), 1, ()),
            (0, (every, slice(nx - 1, nx)), 2, ()),
            (0, (every, low), 3, ()),
        ],
    )
    y_b = y_halo(y_high, y_low)
    xlo, xhi = lax.ppermute(x_high, GX, up), lax.ppermute(x_low, GX, down)
    mask, v = prep(adjacency.reshape(nx * ny, -1, lipids, lipids), w_space, w_time)
    inner_b = aggregate(2, inner, codes, features, y_b, mask)
    prev_inner = lax.ppermute(inner_b, "ta", onward)
    features_a, xlo, xhi, _ = lax.optimization_barrier((features, xlo, xhi, inner_b))
    y_a = y_halo(
        *pack(
            [features_a],
            [y_edge, y_edge],
            [
                (0, (slice(0, 2), every, high), 0, ()),
                (0, (slice(0, 2), every, low), 1, ()),
            ],
        )
    )
    corner = (frames, 2, 1, lipids, width)
    c_high, c_low = pack(
        [xlo, xhi],
        [corner, corner],
        [
            (i, (every, every, side), o, (every, slice(i, i + 1)))
            for i in range(2)
            for o, side in enumerate((high, low))
        ],
    )
    clo, chi = y_halo(c_high, c_low)
    rest = (xlo, xhi, clo, chi)
    outer_b = aggregate(2, outer, codes, features, (*y_b, *rest), mask)
    prev_outer = lax.ppermute(outer_b, "ta", onward)
    mask_a, _ = lax.optimization_barrier((mask, outer_b))
    inner_a = aggregate(0, inner, codes, features, y_a, mask_a)
    outer_a = aggregate(0, outer, codes, features, (*y_a, *rest), mask_a)
    feat = features.reshape(frames, count, width)
    cot = cotangent.reshape(frames, count, width)
    per_row = ny * lipids // MIX_ROWS

    def in_inner(i):
        return i + per_row

    def in_outer(i):
        return i + lax.div(i, per_row) * (nx - 2) * per_row

    updated, total = mix(1, in_inner, inner_a, inner_b, feat, cot, v)
    updated, total = mix(1, in_outer, outer_a, outer_b, feat, cot, v, (total, updated))
    updated, total = mix(0, in_inner, prev_inner, inner_a, feat, cot, v, (total, updated))
    updated, total = mix(0, in_outer, prev_outer, outer_a, feat, cot, v, (total, updated))
    total = all_sum(total)
    scale = 1.0 / math.sqrt(frames * count * lax.axis_size(EVERY))
    grad_space, grad_time = finish(scale, total, w_space, w_time)
    return updated.reshape(features.shape), grad_space, grad_time


def solution(mesh):
    gx, gy, ta = (mesh.shape[a] for a in ("gx", "gy", "ta"))
    fine = Mesh(
        np.asarray(mesh.devices).reshape(2, gx // 2, gy, ta), ("yh", "core", "gy", "ta")
    )
    in_specs = (
        P("ta", GX, "gy", None, None),
        P(GX, "gy", None),
        P(GX, "gy", None, None, None),
        P(),
        P(),
        P("ta", GX, "gy", None, None),
    )
    out_specs = (P("ta", GX, "gy", None, None), P(), P())
    return jax.shard_map(shards, mesh=fine, in_specs=in_specs, out_specs=out_specs, check_vma=False)
```

time: 186 us -> 138 us (0.74)
  waiting for transfers between devices: 64.9 us -> 22.3 us
  blocking collectives: 51.8 us -> 38.1 us
  Pallas kernels: 33 us -> 38.1 us
  local copies, waits for them, and re-layouts: 9.07 us -> 11.1 us
  starting transfers between devices: 25.3 us -> 27.2 us
    ppermute x13 -> x12, waiting for transfers between devices: 64.9 us -> 22.3 us  [the longest x3 14.6 us: y_halo(): lax.ppermute(high_edge, 'gy', up)]
    all_to_all x2, blocking collectives: 51.8 us -> 38.1 us  [the longest x1 22.5 us: all_sum(): lax.all_to_all(mine.reshape(count, block, width), REST, 0, 0, tiled=True)]
    unnamed x18 -> x28, local copies, waits for them, and re-layouts: 3.81 us -> 10.9 us
    slice x7 -> x1, local copies, waits for them, and re-layouts: 5.03 us -> 0.03 us  [all_sum(): back = back.reshape(count * block, width)[:half]]
    pallas_call x2 -> x4, Pallas kernels: 14.6 us -> 18.7 us  [mix(): pl.pallas_call(mix_kernel, grid=(count // rows,), in_specs=[pair, pair, h...]
    pallas_call x3 -> x8, Pallas kernels: 15.5 us -> 17.9 us  [the longest x4 13.5 us: aggregate(): pl.pallas_call(functools.partial(agg_kernel, first, xs, edge), in_specs=[...]
    ppermute x13 -> x12, starting transfers between devices: 25.3 us -> 27.2 us  [the longest x3 6.99 us: y_halo(): lax.ppermute(low_edge, 'gy', down)]
  transfers between devices with their start and end apart: 13 -> 12, of which waited for: 4 -> 8; matrix products, arithmetic and copies ran while one was open for 1% -> 0% of each run, Pallas kernels for 11% -> 21%
where the time goes in v2:
time: 138 us
  Pallas kernels  38.1 us (28%)
  blocking collectives  38.1 us (28%)
  starting transfers between devices  27.2 us (20%)
  waiting for transfers between devices  22.3 us (16%)
  local copies, waits for them, and re-layouts  11.1 us (8%)
    all_to_all x1, blocking collectives, all_sum(): lax.all_to_all(mine.reshape(count, block, width), REST, 0, 0, tiled=True)  22.5 us
    pallas_call x4, Pallas kernels, mix(): pl.pallas_call(mix_kernel, grid=(count // rows,), in_specs=[pair, pair, h...  18.7 us
    all_to_all x1, blocking collectives, all_sum(): back = lax.all_to_all(spread, REST, 0, 0, tiled=True)  15.6 us
    ppermute x3, waiting for transfers between devices, y_halo(): lax.ppermute(high_edge, 'gy', up)  14.6 us
    pallas_call x4, Pallas kernels, aggregate(): pl.pallas_call(functools.partial(agg_kernel, first, xs, edge), in_specs=[...  13.5 us
    unnamed x28, local copies, waits for them, and re-layouts  10.9 us
    ppermute x3, starting transfers between devices, y_halo(): lax.ppermute(low_edge, 'gy', down)  6.99 us
    ppermute x2, starting transfers between devices, shards(): xlo, xhi = (lax.ppermute(x_high, GX, up), lax.ppermute(x_low, GX, down))  4.39 us
  transfers between devices with their start and end apart: 12, of which 8 were waited for; matrix products, arithmetic and copies ran while one was open for 0% of the time, Pallas kernels for 21%

profile of v2, /device:TPU:1, one launch (start us, length us, event | category | flops | bytes accessed | tf_op | source)
XLA Modules:
  0.0 137.8 jit_solution(10292697478051697988)
XLA Ops:
  0.6 0.0 copy-start
  0.6 2.2 %copy-done = bf16[4,4,4,128,256]{4,3,2,1,0:T(8,128)(2,1)S(1)} copy-done((bf16[4,4,4,128,256]{4,3,2,1,0:T(8,128)(2,1)S(1)}, bf16[4,4,4,128,256]{4,3,2,1,0:T(8,128)(2,1)}, u32[]{:S(2)}) %copy-start) | copy-done | bytes 4194328
  2.8 1.7 %pack.3 = (bf16[2,4,1,128,256]{4,3,2,1,0:T(8,128)(2,1)}, bf16[2,4,1,128,256]{4,3,2,1,0:T(8,128)(2,1)}, bf16[4,1,4,128,256]{4,3,2,1,0:T(8,128)(2,1)}, bf16[4,1,4,128,256]{4,3,2,1,0:T(8,128)(2,1)}) custom-call(bf16[4,4,4,128,256]{4,3,2,1,0:T(8,128)(2,1)S(1)} %copy-done), custom_call_target="tpu_custom_call" | custom-call | bytes 6291456 | tf_op jit(solution)/shard_map/pack/pallas_call | solution.py:88
  4.5 4.4 %collective-permute-start.2 = (bf16[4,1,4,128,256]{4,3,2,1,0:T(8,128)(2,1)}, bf16[4,1,4,128,256]{4,3,2,1,0:T(8,128)(2,1)S(1)}, u32[]{:S(2)}, u32[]{:S(2)}) collective-permute-start(bf16[4,1,4,128,256]{4,3,2,1,0:T(8,128)(2,1)} %get-tuple-element.29), channel_id=1, source_target_pairs={{0,32},{32,64},{64,96},{96,0},{1,33},{33,65},{65,97},{97,1},{2,34}... | collective-permute-start | bytes 3145736 | tf_op jit(solution)/shard_map/ppermute | solution.py:305
  8.9 1.6 %collective-permute-start = (bf16[2,4,1,128,256]{4,3,2,1,0:T(8,128)(2,1)}, bf16[2,4,1,128,256]{4,3,2,1,0:T(8,128)(2,1)}, u32[]{:S(2)}, u32[]{:S(2)}) collective-permute-start(bf16[2,4,1,128,256]{4,3,2,1,0:T(8,128)(2,1)} %get-tuple-element.27), channel_id=1, source_target_pairs={{0,8},{8,16},{16,24},{24,0},{1,9},{9,17},{17,25},{25,1},{2,10},{10... | collective-permute-start | bytes 1572872 | tf_op jit(solution)/shard_map/ppermute | solution.py:292
  10.6 2.1 %collective-permute-start.1 = (bf16[2,4,1,128,256]{4,3,2,1,0:T(8,128)(2,1)}, bf16[2,4,1,128,256]{4,3,2,1,0:T(8,128)(2,1)}, u32[]{:S(2)}, u32[]{:S(2)}) collective-permute-start(bf16[2,4,1,128,256]{4,3,2,1,0:T(8,128)(2,1)} %get-tuple-element.28), channel_id=1, source_target_pairs={{0,24},{8,0},{16,8},{24,16},{1,25},{9,1},{17,9},{25,17},{2,26},{10... | collective-permute-start | bytes 1572872 | tf_op jit(solution)/shard_map/ppermute | solution.py:292
  12.7 0.1 reshape.39.codes
  12.8 0.0 copy-start.1
  12.8 0.0 copy-start.4
  12.8 2.3 %copy-done.4 = s32[4,4,4,128,128]{4,3,2,1,0:T(8,128)S(1)} copy-done((s32[4,4,4,128,128]{4,3,2,1,0:T(8,128)S(1)}, s32[4,4,4,128,128]{4,3,2,1,0:T(8,128)}, u32[]{:S(2)}) %copy-start.4) | copy-done | bytes 4194328
  15.1 1.2 copy-done.9
  16.3 0.9 copy-done.11
  17.2 0.6 prep.1
  17.8 7.1 %collective-permute-done.rest_0_ = bf16[2,4,1,128,256]{4,3,2,1,0:T(8,128)(2,1)} collective-permute-done((bf16[2,4,1,128,256]{4,3,2,1,0:T(8,128)(2,1)}, bf16[2,4,1,128,256]{4,3,2,1,0:T(8,128)(2,1)}, u32[]{:S(2)}, u32[]{:S(2)}) %collective-permute-start) | collective-permute-done | bytes 524320 | tf_op jit(solution)/shard_map/ppermute | solution.py:292
  24.9 3.7 %aggregate.4 = bf16[2,2,4,128,256]{4,3,2,1,0:T(8,128)(2,1)} custom-call(s32[64]{0:T(128)S(1)} %reshape.39.codes, bf16[4,4,4,128,256]{4,3,2,1,0:T(8,128)(2,1)S(1)} %copy-done.1, bf16[2,4,1,128,256]{4,3,2,1,0:T(8,128)(2,1)} %collective-permute-done.rest_0_, bf16[2,4,1,128,256]{4,3,2,1,0:T(8,128)(2,1)} %collective-permute-done.1.rest_1_, ...), custom_call_target="tpu_custom_call" | custom-call | flops 536870912 | bytes 8388608 | tf_op jit(solution)/shard_map/aggregate/pallas_call | solution.py:152
  28.6 3.2 %collective-permute-done.2.refs_0_.rest_2_ = bf16[4,1,4,128,256]{4,3,2,1,0:T(8,128)(2,1)S(1)} collective-permute-done((bf16[4,1,4,128,256]{4,3,2,1,0:T(8,128)(2,1)}, bf16[4,1,4,128,256]{4,3,2,1,0:T(8,128)(2,1)S(1)}, u32[]{:S(2)}, u32[]{:S(2)}) %collective-permute-start.2) | collective-permute-done | bytes 1048608 | tf_op jit(solution)/shard_map/ppermute | solution.py:305
  31.8 0.9 collective-permute-done.3.refs_1_.rest_3_
  32.6 1.1 pack.4
  33.7 1.8 %collective-permute-start.4 = (bf16[4,2,1,128,256]{4,3,2,1,0:T(8,128)(2,1)S(1)}, bf16[4,2,1,128,256]{4,3,2,1,0:T(8,128)(2,1)S(1)}, u32[]{:S(2)}, u32[]{:S(2)}) collective-permute-start(bf16[4,2,1,128,256]{4,3,2,1,0:T(8,128)(2,1)S(1)} %get-tuple-element.34), channel_id=1, source_target_pairs={{0,8},{8,16},{16,24},{24,0},{1,9},{9,17},{17,25},{25,1},{2,10},{10... | collective-permute-start | bytes 1572872 | tf_op jit(solution)/shard_map/ppermute | solution.py:292
  35.5 2.2 %collective-permute-start.5 = (bf16[4,2,1,128,256]{4,3,2,1,0:T(8,128)(2,1)S(1)}, bf16[4,2,1,128,256]{4,3,2,1,0:T(8,128)(2,1)S(1)}, u32[]{:S(2)}, u32[]{:S(2)}) collective-permute-start(bf16[4,2,1,128,256]{4,3,2,1,0:T(8,128)(2,1)S(1)} %get-tuple-element.35), channel_id=1, source_target_pairs={{0,24},{8,0},{16,8},{24,16},{1,25},{9,1},{17,9},{25,17},{2,26},{10... | collective-permute-start | bytes 1572872 | tf_op jit(solution)/shard_map/ppermute | solution.py:292
  37.7 4.2 %collective-permute-start.9 = (bf16[2,1024,256]{2,1,0:T(8,128)(2,1)}, bf16[2,1024,256]{2,1,0:T(8,128)(2,1)}, u32[]{:S(2)}, u32[]{:S(2)}) collective-permute-start(bf16[2,1024,256]{2,1,0:T(8,128)(2,1)} %bitcast.1.q_ref), channel_id=1, source_target_pairs={{0,1},{1,2},{2,3},{3,4},{4,5},{5,6},{6,7},{8,9},{9,10},{10,11},{11... | collective-permute-start | bytes 3145736 | tf_op jit(solution)/shard_map/ppermute | solution.py:308
  41.9 1.0 pack.5
  42.9 0.1 collective-permute-start.7
  43.0 2.7 %collective-permute-start.8 = (bf16[2,4,1,128,256]{4,3,2,1,0:T(8,128)(2,1)}, bf16[2,4,1,128,256]{4,3,2,1,0:T(8,128)(2,1)}, u32[]{:S(2)}, u32[]{:S(2)}) collective-permute-start(bf16[2,4,1,128,256]{4,3,2,1,0:T(8,128)(2,1)} %get-tuple-element.38), channel_id=1, source_target_pairs={{0,24},{8,0},{16,8},{24,16},{1,25},{9,1},{17,9},{25,17},{2,26},{10... | collective-permute-start | bytes 1572872 | tf_op jit(solution)/shard_map/ppermute | solution.py:292
  45.6 4.4 %collective-permute-done.4.rest_4_ = bf16[4,2,1,128,256]{4,3,2,1,0:T(8,128)(2,1)S(1)} collective-permute-done((bf16[4,2,1,128,256]{4,3,2,1,0:T(8,128)(2,1)S(1)}, bf16[4,2,1,128,256]{4,3,2,1,0:T(8,128)(2,1)S(1)}, u32[]{:S(2)}, u32[]{:S(2)}) %collective-permute-start.4) | collective-permute-done | bytes 524320 | tf_op jit(solution)/shard_map/ppermute | solution.py:292
  50.0 3.9 %aggregate.5 = bf16[2,2,4,128,256]{4,3,2,1,0:T(8,128)(2,1)} custom-call(s32[64]{0:T(128)S(1)} %reshape.39.codes, bf16[4,4,4,128,256]{4,3,2,1,0:T(8,128)(2,1)S(1)} %copy-done.1, bf16[2,4,1,128,256]{4,3,2,1,0:T(8,128)(2,1)} %collective-permute-done.rest_0_, bf16[2,4,1,128,256]{4,3,2,1,0:T(8,128)(2,1)} %collective-permute-done.1.rest_1_, ...), custom_call_target="tpu_custom_call" | custom-call | flops 536870912 | bytes 8388608 | tf_op jit(solution)/shard_map/aggregate/pallas_call | solution.py:152
  53.9 4.4 %collective-permute-start.6 = (bf16[2,1024,256]{2,1,0:T(8,128)(2,1)}, bf16[2,1024,256]{2,1,0:T(8,128)(2,1)}, u32[]{:S(2)}, u32[]{:S(2)}) collective-permute-start(bf16[2,1024,256]{2,1,0:T(8,128)(2,1)} %bitcast.2.q_ref), channel_id=1, source_target_pairs={{0,1},{1,2},{2,3},{3,4},{4,5},{5,6},{6,7},{8,9},{9,10},{10,11},{11... | collective-permute-start | bytes 3145736 | tf_op jit(solution)/shard_map/ppermute | solution.py:333
  58.3 3.1 %collective-permute-done.7.rest_0_ = bf16[2,4,1,128,256]{4,3,2,1,0:T(8,128)(2,1)} collective-permute-done((bf16[2,4,1,128,256]{4,3,2,1,0:T(8,128)(2,1)}, bf16[2,4,1,128,256]{4,3,2,1,0:T(8,128)(2,1)}, u32[]{:S(2)}, u32[]{:S(2)}) %collective-permute-start.7) | collective-permute-done | bytes 524320 | tf_op jit(solution)/shard_map/ppermute | solution.py:292
  61.4 2.2 %copy-done.2 = bf16[4,4,4,128,256]{4,3,2,1,0:T(8,128)(2,1)S(1)} copy-done((bf16[4,4,4,128,256]{4,3,2,1,0:T(8,128)(2,1)S(1)}, bf16[4,4,4,128,256]{4,3,2,1,0:T(8,128)(2,1)}, u32[]{:S(2)}) %copy-start.2) | copy-done | bytes 4194328
  63.6 1.0 copy-done.6
  64.6 1.0 copy-done.8
  65.7 2.9 %aggregate.6 = bf16[2,2,4,128,256]{4,3,2,1,0:T(8,128)(2,1)S(1)} custom-call(s32[64]{0:T(128)S(1)} %reshape.39.codes, bf16[4,4,4,128,256]{4,3,2,1,0:T(8,128)(2,1)S(1)} %copy-done.2, bf16[2,4,1,128,256]{4,3,2,1,0:T(8,128)(2,1)} %collective-permute-done.7.rest_0_, bf16[2,4,1,128,256]{4,3,2,1,0:T(8,128)(2,1)} %collective-permute-done.8.rest_1_, ...), custom_call_target="tpu_custom_call" | custom-call | flops 536870912 | bytes 8388608 | tf_op jit(solution)/shard_map/aggregate/pallas_call | solution.py:152
  68.6 3.0 %aggregate.7 = bf16[2,2,4,128,256]{4,3,2,1,0:T(8,128)(2,1)S(1)} custom-call(s32[64]{0:T(128)S(1)} %reshape.39.codes, bf16[4,4,4,128,256]{4,3,2,1,0:T(8,128)(2,1)S(1)} %copy-done.2, bf16[2,4,1,128,256]{4,3,2,1,0:T(8,128)(2,1)} %collective-permute-done.7.rest_0_, bf16[2,4,1,128,256]{4,3,2,1,0:T(8,128)(2,1)} %collective-permute-done.8.rest_1_, ...), custom_call_target="tpu_custom_call" | custom-call | flops 536870912 | bytes 8388608 | tf_op jit(solution)/shard_map/aggregate/pallas_call | solution.py:152
  71.6 4.7 %mix.4 = (bf16[4,2048,256]{2,1,0:T(8,128)(2,1)}, f32[768,256]{1,0:T(8,128)S(1)}) custom-call(bf16[2,1024,256]{2,1,0:T(8,128)(2,1)S(1)} %bitcast.20, bf16[2,1024,256]{2,1,0:T(8,128)(2,1)} %bitcast.1.q_ref, bf16[4,2048,256]{2,1,0:T(8,128)(2,1)S(1)} %bitcast.12, bf16[4,2048,256]{2,1,0:T(8,128)(2,1)S(1)} %bitcast.16, bf16[768,256]{1,0:T(8,128)(2,1)S(1)} %get-tuple-element.40.v_ref), custom_call_target="tpu_custom_call" | custom-call | flops 1610612736 | bytes 10485760 | tf_op jit(solution)/shard_map/mix/pallas_call | solution.py:206
  76.3 4.7 %mix.5 = (bf16[4,2048,256]{2,1,0:T(8,128)(2,1)}, f32[768,256]{1,0:T(8,128)S(1)}) custom-call(bf16[2,1024,256]{2,1,0:T(8,128)(2,1)S(1)} %bitcast.22, bf16[2,1024,256]{2,1,0:T(8,128)(2,1)} %bitcast.2.q_ref, bf16[4,2048,256]{2,1,0:T(8,128)(2,1)S(1)} %bitcast.13, bf16[4,2048,256]{2,1,0:T(8,128)(2,1)S(1)} %bitcast.17, ...), custom_call_target="tpu_custom_call", output_to_operand_aliasing={{0}: (6, {})} | custom-call | flops 1610612736 | bytes 10485760 | tf_op jit(solution)/shard_map/mix/pallas_call | solution.py:206
  81.0 4.7 %mix.6 = (bf16[4,2048,256]{2,1,0:T(8,128)(2,1)}, f32[768,256]{1,0:T(8,128)S(1)}) custom-call(bf16[2,1024,256]{2,1,0:T(8,128)(2,1)} %collective-permute-done.9.p_ref, bf16[2,1024,256]{2,1,0:T(8,128)(2,1)S(1)} %bitcast.21, bf16[4,2048,256]{2,1,0:T(8,128)(2,1)S(1)} %bitcast.14, bf16[4,2048,256]{2,1,0:T(8,128)(2,1)S(1)} %bitcast.18, ...), custom_call_target="tpu_custom_call", output_to_operand_aliasing={{0}: (6, {})} | custom-call | flops 1610612736 | bytes 10485760 | tf_op jit(solution)/shard_map/mix/pallas_call | solution.py:206
  85.7 0.7 collective-permute-done.6.p_ref
  86.4 4.6 %mix.7 = (bf16[4,2048,256]{2,1,0:T(8,128)(2,1)}, f32[768,256]{1,0:T(8,128)S(1)}) custom-call(bf16[2,1024,256]{2,1,0:T(8,128)(2,1)} %collective-permute-done.6.p_ref, bf16[2,1024,256]{2,1,0:T(8,128)(2,1)S(1)} %bitcast.23, bf16[4,2048,256]{2,1,0:T(8,128)(2,1)S(1)} %bitcast.15, bf16[4,2048,256]{2,1,0:T(8,128)(2,1)S(1)} %bitcast.19, ...), custom_call_target="tpu_custom_call", output_to_operand_aliasing={{0}: (6, {})} | custom-call | flops 1610612736 | bytes 10485760 | tf_op jit(solution)/shard_map/mix/pallas_call | solution.py:206
  91.1 0.2 collective-permute-start.10
  91.3 1.6 %collective-permute-done.10 = f32[384,256]{1,0:T(8,128)S(1)} collective-permute-done((f32[384,256]{1,0:T(8,128)S(1)}, f32[384,256]{1,0:T(8,128)S(1)}, u32[]{:S(2)}, u32[]{:S(2)}) %collective-permute-start.10) | collective-permute-done | bytes 393248 | tf_op jit(solution)/shard_map/ppermute | solution.py:267
  92.9 0.1 dynamic-slice_add_fusion
  93.0 22.5 %all_to_all.10 = f32[64,8,256]{2,1,0:T(8,128)S(1)} all-to-all(f32[64,8,256]{2,1,0:T(8,128)S(1)} %pad_bitcast_fusion), channel_id=1, replica_groups=mesh['yh'=2,'core'=2,'gy'=4,'ta'=8] {'yh','gy','ta'}, dimensions={0} | all-to-all | bytes 1048576 | tf_op jit(solution)/shard_map/all_to_all | solution.py:269
  115.5 0.1 reduce_sum.9
  115.6 15.6 %all_to_all.11 = f32[64,8,256]{2,1,0:T(8,128)S(1)} all-to-all(f32[64,8,256]{2,1,0:T(8,128)S(1)} %broadcast_in_dim.2), channel_id=1, replica_groups=mesh['yh'=2,'core'=2,'gy'=4,'ta'=8] {'yh','gy','ta'}, dimensions={0} | all-to-all | bytes 1048576 | tf_op jit(solution)/shard_map/all_to_all | solution.py:271
  131.3 3.5 %collective-permute-start.11 = (f32[384,256]{1,0:T(8,128)S(1)}, f32[384,256]{1,0:T(8,128)S(1)}, u32[]{:S(2)}, u32[]{:S(2)}) collective-permute-start(f32[384,256]{1,0:T(8,128)S(1)} %slice_bitcast_fusion), channel_id=1, source_target_pairs={{0,32},{32,0},{1,33},{33,1},{2,34},{34,2},{3,35},{35,3},{4,36},{36... | collective-permute-start | bytes 1179656 | tf_op jit(solution)/shard_map/ppermute | solution.py:273
  134.8 1.3 collective-permute-done.11
  136.1 0.1 maximum_select_fusion.g_ref
  136.2 1.6 %finish.1 = (f32[256,256]{1,0:T(8,128)}, f32[3,256,256]{2,1,0:T(8,128)}) custom-call(f32[768,256]{1,0:T(8,128)S(1)} %maximum_select_fusion.g_ref, bf16[256,256]{1,0:T(8,128)(2,1)S(1)} %copy-done.12, bf16[3,256,256]{2,1,0:T(8,128)(2,1)S(1)} %copy-done.10), custom_call_target="tpu_custom_call" | custom-call | tf_op jit(solution)/shard_map/finish/pallas_call | solution.py:247
  (27 shorter events, 0.2 us)
Async XLA Ops:
  0.6 2.2 %copy-start = (bf16[4,4,4,128,256]{4,3,2,1,0:T(8,128)(2,1)S(1)}, bf16[4,4,4,128,256]{4,3,2,1,0:T(8,128)(2,1)}, u32[]{:S(2)}) copy-start(bf16[4,4,4,128,256]{4,3,2,1,0:T(8,128)(2,1)} %feat.7) | copy-start | bytes 12582916
  2.8 9.9 %copy-start.13 = (s32[4,4,4]{2,1,0:T(4,128)S(1)}, s32[4,4,4]{2,1,0:T(4,128)}, u32[]{:S(2)}) copy-start(s32[4,4,4]{2,1,0:T(4,128)} %param.7) | copy-start | bytes 772
  4.5 27.2 %collective-permute-start.2 = (bf16[4,1,4,128,256]{4,3,2,1,0:T(8,128)(2,1)}, bf16[4,1,4,128,256]{4,3,2,1,0:T(8,128)(2,1)S(1)}, u32[]{:S(2)}, u32[]{:S(2)}) collective-permute-start(bf16[4,1,4,128,256]{4,3,2,1,0:T(8,128)(2,1)} %get-tuple-element.29), channel_id=1, source_target_pairs={{0,32},{32,64},{64,96},{96,0},{1,33},{33,65},{65,97},{97,1},{2,34}... | collective-permute-start | bytes 3145736 | tf_op jit(solution)/shard_map/ppermute | solution.py:305
  8.9 23.7 %collective-permute-start.3 = (bf16[4,1,4,128,256]{4,3,2,1,0:T(8,128)(2,1)}, bf16[4,1,4,128,256]{4,3,2,1,0:T(8,128)(2,1)}, u32[]{:S(2)}, u32[]{:S(2)}) collective-permute-start(bf16[4,1,4,128,256]{4,3,2,1,0:T(8,128)(2,1)} %get-tuple-element.30), channel_id=1, source_target_pairs={{0,96},{32,0},{64,32},{96,64},{1,97},{33,1},{65,33},{97,65},{2,98}... | collective-permute-start | bytes 3145736 | tf_op jit(solution)/shard_map/ppermute | solution.py:305
  8.9 16.0 %collective-permute-start = (bf16[2,4,1,128,256]{4,3,2,1,0:T(8,128)(2,1)}, bf16[2,4,1,128,256]{4,3,2,1,0:T(8,128)(2,1)}, u32[]{:S(2)}, u32[]{:S(2)}) collective-permute-start(bf16[2,4,1,128,256]{4,3,2,1,0:T(8,128)(2,1)} %get-tuple-element.27), channel_id=1, source_target_pairs={{0,8},{8,16},{16,24},{24,0},{1,9},{9,17},{17,25},{25,1},{2,10},{10... | collective-permute-start | bytes 1572872 | tf_op jit(solution)/shard_map/ppermute | solution.py:292
  10.6 14.3 %collective-permute-start.1 = (bf16[2,4,1,128,256]{4,3,2,1,0:T(8,128)(2,1)}, bf16[2,4,1,128,256]{4,3,2,1,0:T(8,128)(2,1)}, u32[]{:S(2)}, u32[]{:S(2)}) collective-permute-start(bf16[2,4,1,128,256]{4,3,2,1,0:T(8,128)(2,1)} %get-tuple-element.28), channel_id=1, source_target_pairs={{0,24},{8,0},{16,8},{24,16},{1,25},{9,1},{17,9},{25,17},{2,26},{10... | collective-permute-start | bytes 1572872 | tf_op jit(solution)/shard_map/ppermute | solution.py:292
  12.8 12.1 %copy-start.1 = (bf16[4,4,4,128,256]{4,3,2,1,0:T(8,128)(2,1)S(1)}, bf16[4,4,4,128,256]{4,3,2,1,0:T(8,128)(2,1)}, u32[]{:S(2)}) copy-start(bf16[4,4,4,128,256]{4,3,2,1,0:T(8,128)(2,1)} %feat.7) | copy-start | bytes 12582916
  12.8 2.3 %copy-start.4 = (s32[4,4,4,128,128]{4,3,2,1,0:T(8,128)S(1)}, s32[4,4,4,128,128]{4,3,2,1,0:T(8,128)}, u32[]{:S(2)}) copy-start(s32[4,4,4,128,128]{4,3,2,1,0:T(8,128)} %param.8) | copy-start | bytes 12582916
  15.1 1.2 copy-start.9
  16.3 0.9 copy-start.11
  33.7 16.3 %collective-permute-start.4 = (bf16[4,2,1,128,256]{4,3,2,1,0:T(8,128)(2,1)S(1)}, bf16[4,2,1,128,256]{4,3,2,1,0:T(8,128)(2,1)S(1)}, u32[]{:S(2)}, u32[]{:S(2)}) collective-permute-start(bf16[4,2,1,128,256]{4,3,2,1,0:T(8,128)(2,1)S(1)} %get-tuple-element.34), channel_id=1, source_target_pairs={{0,8},{8,16},{16,24},{24,0},{1,9},{9,17},{17,25},{25,1},{2,10},{10... | collective-permute-start | bytes 1572872 | tf_op jit(solution)/shard_map/ppermute | solution.py:292
  35.5 14.5 %collective-permute-start.5 = (bf16[4,2,1,128,256]{4,3,2,1,0:T(8,128)(2,1)S(1)}, bf16[4,2,1,128,256]{4,3,2,1,0:T(8,128)(2,1)S(1)}, u32[]{:S(2)}, u32[]{:S(2)}) collective-permute-start(bf16[4,2,1,128,256]{4,3,2,1,0:T(8,128)(2,1)S(1)} %get-tuple-element.35), channel_id=1, source_target_pairs={{0,24},{8,0},{16,8},{24,16},{1,25},{9,1},{17,9},{25,17},{2,26},{10... | collective-permute-start | bytes 1572872 | tf_op jit(solution)/shard_map/ppermute | solution.py:292
  37.7 43.3 %collective-permute-start.9 = (bf16[2,1024,256]{2,1,0:T(8,128)(2,1)}, bf16[2,1024,256]{2,1,0:T(8,128)(2,1)}, u32[]{:S(2)}, u32[]{:S(2)}) collective-permute-start(bf16[2,1024,256]{2,1,0:T(8,128)(2,1)} %bitcast.1.q_ref), channel_id=1, source_target_pairs={{0,1},{1,2},{2,3},{3,4},{4,5},{5,6},{6,7},{8,9},{9,10},{10,11},{11... | collective-permute-start | bytes 3145736 | tf_op jit(solution)/shard_map/ppermute | solution.py:308
  42.9 18.5 %collective-permute-start.7 = (bf16[2,4,1,128,256]{4,3,2,1,0:T(8,128)(2,1)}, bf16[2,4,1,128,256]{4,3,2,1,0:T(8,128)(2,1)}, u32[]{:S(2)}, u32[]{:S(2)}) collective-permute-start(bf16[2,4,1,128,256]{4,3,2,1,0:T(8,128)(2,1)} %get-tuple-element.37), channel_id=1, source_target_pairs={{0,8},{8,16},{16,24},{24,0},{1,9},{9,17},{17,25},{25,1},{2,10},{10... | collective-permute-start | bytes 1572872 | tf_op jit(solution)/shard_map/ppermute | solution.py:292
  43.0 18.4 %collective-permute-start.8 = (bf16[2,4,1,128,256]{4,3,2,1,0:T(8,128)(2,1)}, bf16[2,4,1,128,256]{4,3,2,1,0:T(8,128)(2,1)}, u32[]{:S(2)}, u32[]{:S(2)}) collective-permute-start(bf16[2,4,1,128,256]{4,3,2,1,0:T(8,128)(2,1)} %get-tuple-element.38), channel_id=1, source_target_pairs={{0,24},{8,0},{16,8},{24,16},{1,25},{9,1},{17,9},{25,17},{2,26},{10... | collective-permute-start | bytes 1572872 | tf_op jit(solution)/shard_map/ppermute | solution.py:292
  50.0 3.9 %copy-start.5 = (bf16[4,2,1,128,256]{4,3,2,1,0:T(8,128)(2,1)}, bf16[4,2,1,128,256]{4,3,2,1,0:T(8,128)(2,1)S(1)}, u32[]{:S(2)}) copy-start(bf16[4,2,1,128,256]{4,3,2,1,0:T(8,128)(2,1)S(1)} %collective-permute-done.4.rest_4_) | copy-start | bytes 1572868
  50.0 3.9 %copy-start.7 = (bf16[4,2,1,128,256]{4,3,2,1,0:T(8,128)(2,1)}, bf16[4,2,1,128,256]{4,3,2,1,0:T(8,128)(2,1)S(1)}, u32[]{:S(2)}) copy-start(bf16[4,2,1,128,256]{4,3,2,1,0:T(8,128)(2,1)S(1)} %collective-permute-done.5.rest_5_) | copy-start | bytes 1572868
  53.9 32.5 %collective-permute-start.6 = (bf16[2,1024,256]{2,1,0:T(8,128)(2,1)}, bf16[2,1024,256]{2,1,0:T(8,128)(2,1)}, u32[]{:S(2)}, u32[]{:S(2)}) collective-permute-start(bf16[2,1024,256]{2,1,0:T(8,128)(2,1)} %bitcast.2.q_ref), channel_id=1, source_target_pairs={{0,1},{1,2},{2,3},{3,4},{4,5},{5,6},{6,7},{8,9},{9,10},{10,11},{11... | collective-permute-start | bytes 3145736 | tf_op jit(solution)/shard_map/ppermute | solution.py:333
  61.4 2.2 %copy-start.2 = (bf16[4,4,4,128,256]{4,3,2,1,0:T(8,128)(2,1)S(1)}, bf16[4,4,4,128,256]{4,3,2,1,0:T(8,128)(2,1)}, u32[]{:S(2)}) copy-start(bf16[4,4,4,128,256]{4,3,2,1,0:T(8,128)(2,1)} %feat.7) | copy-start | bytes 12582916
  63.6 1.0 copy-start.6
  64.6 1.0 copy-start.8
  68.6 3.1 %copy-start.3 = (bf16[4,4,4,128,256]{4,3,2,1,0:T(8,128)(2,1)S(1)}, bf16[4,4,4,128,256]{4,3,2,1,0:T(8,128)(2,1)}, u32[]{:S(2)}) copy-start(bf16[4,4,4,128,256]{4,3,2,1,0:T(8,128)(2,1)} %param.11) | copy-start | bytes 12582916
  91.1 45.1 %copy-start.10 = (bf16[3,256,256]{2,1,0:T(8,128)(2,1)S(1)}, bf16[3,256,256]{2,1,0:T(8,128)(2,1)}, u32[]{:S(2)}) copy-start(bf16[3,256,256]{2,1,0:T(8,128)(2,1)} %wt_ref.3) | copy-start | bytes 1179652
  91.1 45.2 %copy-start.12 = (bf16[256,256]{1,0:T(8,128)(2,1)S(1)}, bf16[256,256]{1,0:T(8,128)(2,1)}, u32[]{:S(2)}) copy-start(bf16[256,256]{1,0:T(8,128)(2,1)} %ws_ref.3) | copy-start | bytes 393220
  91.1 1.8 %collective-permute-start.10 = (f32[384,256]{1,0:T(8,128)S(1)}, f32[384,256]{1,0:T(8,128)S(1)}, u32[]{:S(2)}, u32[]{:S(2)}) collective-permute-start(f32[384,256]{1,0:T(8,128)S(1)} %constant_dynamic-slice_fusion), channel_id=1, source_target_pairs={{0,32},{32,0},{1,33},{33,1},{2,34},{34,2},{3,35},{35,3},{4,36},{36... | collective-permute-start | bytes 1179656 | tf_op jit(solution)/shard_map/ppermute | solution.py:267
  131.3 4.9 %collective-permute-start.11 = (f32[384,256]{1,0:T(8,128)S(1)}, f32[384,256]{1,0:T(8,128)S(1)}, u32[]{:S(2)}, u32[]{:S(2)}) collective-permute-start(f32[384,256]{1,0:T(8,128)S(1)} %slice_bitcast_fusion), channel_id=1, source_target_pairs={{0,32},{32,0},{1,33},{33,1},{2,34},{34,2},{3,35},{35,3},{4,36},{36... | collective-permute-start | bytes 1179656 | tf_op jit(solution)/shard_map/ppermute | solution.py:273

commit v3 on v2

--- a/solution.py
+++ b/solution.py
@@ -14,7 +14,7 @@
 F32 = jnp.float32
 GX = ("yh", "core")
 MIX_ROWS = 512
-VMEM = 20 << 20
+VMEM = 65300 << 10
 EVERY = ("yh", "core", "gy", "ta")
 REST = ("yh", "gy", "ta")
 
@@ -111,7 +111,7 @@
         for i, x in enumerate(xs)
     ]
     if edge:
-        xlo, xhi, clo, chi = (ref.at[span] for ref in halo[2:])
+        xlo, xhi, clo, chi = halo[2:]
         moves += [
             (xlo, ext.at[:, 0:1, 1 : ny + 1]),
             (xhi, ext.at[:, nx + 1 : nx + 2, 1 : ny + 1]),
@@ -252,7 +252,7 @@
             jax.ShapeDtypeStruct(w_space.shape, F32),
             jax.ShapeDtypeStruct(w_time.shape, F32),
         ],
-        compiler_params=pltpu.CompilerParams(vmem_limit_bytes=VMEM),
+        compiler_params=pltpu.CompilerParams(vmem_limit_bytes=20 << 20),
         name="finish",
     )(total, w_space, w_time)
 
@@ -284,56 +284,57 @@
     onward = [(i, i + 1) for i in range(7)]
     inner, outer = tuple(range(1, nx - 1)), (0, nx - 1)
 
-    y_edge, x_edge = (2, nx, 1, lipids, width), (frames, 1, ny, lipids, width)
     every = slice(None)
     low, high = slice(0, 1), slice(ny - 1, ny)
 
-    def y_halo(high_edge, low_edge):
-        return lax.ppermute(high_edge, "gy", up), lax.ppermute(low_edge, "gy", down)
-
-    y_high, y_low, x_high, x_low = pack(
-        [features],
-        [y_edge, y_edge, x_edge, x_edge],
-        [
-            (0, (slice(2, 4), every, high), 0, ()),
-            (0, (slice(2, 4), every, low), 1, ()),
-            (0, (every, slice(nx - 1, nx)), 2, ()),
-            (0, (every, low), 3, ()),
-        ],
-    )
-    y_b = y_halo(y_high, y_low)
-    xlo, xhi = lax.ppermute(x_high, GX, up), lax.ppermute(x_low, GX, down)
+    def exchange(axis, high_edge, low_edge):
+        return lax.ppermute(high_edge, axis, up), lax.ppermute(low_edge, axis, down)
+
+    def edges(first, source):
+        pair = slice(first, first + 2)
+        x_edge, y_edge = (2, 1, ny, lipids, width), (2, nx, 1, lipids, width)
+        return pack(
+            [source],
+            [x_edge, x_edge, y_edge, y_edge],
+            [
+                (0, (pair, slice(nx - 1, nx)), 0, ()),
+                (0, (pair, low), 1, ()),
+                (0, (pair, every, high), 2, ()),
+                (0, (pair, every, low), 3, ()),
+            ],
+        )
+
+    def corners(x_halo):
+        corner = (2, 2, 1, lipids, width)
+        ends = pack(
+            x_halo,
+            [corner, corner],
+            [
+                (i, (every, every, side), o, (every, slice(i, i + 1)))
+                for i in range(2)
+                for o, side in enumerate((high, low))
+            ],
+        )
+        return exchange("gy", *ends)
+
+    edges_b = edges(2, features)
+    x_b = exchange(GX, *edges_b[:2])
+    y_b = exchange("gy", *edges_b[2:])
     mask, v = prep(adjacency.reshape(nx * ny, -1, lipids, lipids), w_space, w_time)
+    later, _, _ = lax.optimization_barrier((features, edges_b, mask))
+    edges_a = edges(0, later)
+    x_a = exchange(GX, *edges_a[:2])
+    y_a = exchange("gy", *edges_a[2:])
+    c_b = corners(x_b)
     inner_b = aggregate(2, inner, codes, features, y_b, mask)
     prev_inner = lax.ppermute(inner_b, "ta", onward)
-    features_a, xlo, xhi, _ = lax.optimization_barrier((features, xlo, xhi, inner_b))
-    y_a = y_halo(
-        *pack(
-            [features_a],
-            [y_edge, y_edge],
-            [
-                (0, (slice(0, 2), every, high), 0, ()),
-                (0, (slice(0, 2), every, low), 1, ()),
-            ],
-        )
-    )
-    corner = (frames, 2, 1, lipids, width)
-    c_high, c_low = pack(
-        [xlo, xhi],
-        [corner, corner],
-        [
-            (i, (every, every, side), o, (every, slice(i, i + 1)))
-            for i in range(2)
-            for o, side in enumerate((high, low))
-        ],
-    )
-    clo, chi = y_halo(c_high, c_low)
-    rest = (xlo, xhi, clo, chi)
-    outer_b = aggregate(2, outer, codes, features, (*y_b, *rest), mask)
+    c_b, _, _ = lax.optimization_barrier((c_b, inner_b, x_a))
+    outer_b = aggregate(2, outer, codes, features, (*y_b, *x_b, *c_b), mask)
     prev_outer = lax.ppermute(outer_b, "ta", onward)
-    mask_a, _ = lax.optimization_barrier((mask, outer_b))
+    x_a, y_a, mask_a, _ = lax.optimization_barrier((x_a, y_a, mask, outer_b))
+    c_a = corners(x_a)
     inner_a = aggregate(0, inner, codes, features, y_a, mask_a)
-    outer_a = aggregate(0, outer, codes, features, (*y_a, *rest), mask_a)
+    outer_a = aggregate(0, outer, codes, features, (*y_a, *x_a, *c_a), mask_a)
     feat = features.reshape(frames, count, width)
     cot = cotangent.reshape(frames, count, width)
     per_row = ny * lipids // MIX_ROWS

time: 138 us -> 288 us (2.09)
  Pallas kernels: 38.1 us -> 212 us
  waiting for transfers between devices: 22.3 us -> 5.16 us
  local copies, waits for them, and re-layouts: 11.1 us -> 1.8 us
  starting transfers between devices: 27.2 us -> 33.5 us
  blocking collectives: 38.1 us -> 32.8 us
    pallas_call x3 -> x4, Pallas kernels: 3.79 us -> 163 us  [pack(): pl.pallas_call(functools.partial(pack_kernel, moves, len(arrays)), in_spe...]
    ppermute x8 -> x12, waiting for transfers between devices: 18.6 us -> 2.45 us  [the longest x6 1.48 us: exchange(): lax.ppermute(high_edge, axis, up)]
    unnamed x28 -> x6, local copies, waits for them, and re-layouts: 10.9 us -> 0.01 us
    pallas_call x4, Pallas kernels: 13.5 us -> 19.4 us  [aggregate(): pl.pallas_call(functools.partial(agg_kernel, first, xs, edge), in_specs=[...]
    all_to_all x1, blocking collectives: 22.5 us -> 17.2 us  [all_sum(): lax.all_to_all(mine.reshape(count, block, width), REST, 0, 0, tiled=True)]
    pallas_call x4, Pallas kernels: 18.7 us -> 23.1 us  [mix(): pl.pallas_call(mix_kernel, grid=(count // rows,), in_specs=[pair, pair, h...]
    pallas_call x1, Pallas kernels: 0.59 us -> 4.83 us  [prep(): pl.pallas_call(prep_kernel, grid=(tiles // 4,), in_specs=[pl.BlockSpec((4...]
    ppermute x1, starting transfers between devices: 0.21 us -> 4.03 us  [all_sum(): mine = keep + lax.ppermute(give, 'core', ring(2, 1))]
  transfers between devices with their start and end apart: 12 -> 16, of which waited for: 8 -> 4; matrix products, arithmetic and copies ran while one was open for 0% -> 0% of each run, Pallas kernels for 21% -> 49%
where the time goes in v3:
time: 288 us
  Pallas kernels  212 us (74%)
  starting transfers between devices  33.5 us (12%)
  blocking collectives  32.8 us (11%)
  waiting for transfers between devices  5.16 us (2%)
    pallas_call x4, Pallas kernels, pack(): pl.pallas_call(functools.partial(pack_kernel, moves, len(arrays)), in_spe...  163 us
    pallas_call x4, Pallas kernels, mix(): pl.pallas_call(mix_kernel, grid=(count // rows,), in_specs=[pair, pair, h...  23.1 us
    pallas_call x4, Pallas kernels, aggregate(): pl.pallas_call(functools.partial(agg_kernel, first, xs, edge), in_specs=[...  19.4 us
    all_to_all x1, blocking collectives, all_sum(): lax.all_to_all(mine.reshape(count, block, width), REST, 0, 0, tiled=True)  17.2 us
    all_to_all x1, blocking collectives, all_sum(): back = lax.all_to_all(spread, REST, 0, 0, tiled=True)  15.6 us
    ppermute x6, starting transfers between devices, exchange(): lax.ppermute(high_edge, axis, up)  10.7 us
    ppermute x6, starting transfers between devices, exchange(): lax.ppermute(low_edge, axis, down)  7.98 us
  transfers between devices with their start and end apart: 16, of which 4 were waited for; matrix products, arithmetic and copies ran while one was open for 0% of the time, Pallas kernels for 49%

profile of v3, /device:TPU:1, one launch (start us, length us, event | category | flops | bytes accessed | tf_op | source)
XLA Modules:
  0.0 287.6 jit_solution(4977593753162878426)
XLA Ops:
  0.6 64.7 %pack.4 = (bf16[2,1,4,128,256]{4,3,2,1,0:T(8,128)(2,1)}, bf16[2,1,4,128,256]{4,3,2,1,0:T(8,128)(2,1)}, bf16[2,4,1,128,256]{4,3,2,1,0:T(8,128)(2,1)}, bf16[2,4,1,128,256]{4,3,2,1,0:T(8,128)(2,1)}) custom-call(bf16[4,4,4,128,256]{4,3,2,1,0:T(8,128)(2,1)} %feat.7), custom_call_target="tpu_custom_call" | custom-call | bytes 6291456 | tf_op jit(solution)/shard_map/pack/pallas_call | solution.py:88
  65.3 4.4 %collective-permute-start.2 = (bf16[2,1,4,128,256]{4,3,2,1,0:T(8,128)(2,1)}, bf16[2,1,4,128,256]{4,3,2,1,0:T(8,128)(2,1)}, u32[]{:S(2)}, u32[]{:S(2)}) collective-permute-start(bf16[2,1,4,128,256]{4,3,2,1,0:T(8,128)(2,1)} %get-tuple-element.37), channel_id=1, source_target_pairs={{0,32},{32,64},{64,96},{96,0},{1,33},{33,65},{65,97},{97,1},{2,34}... | collective-permute-start | bytes 1572872 | tf_op jit(solution)/shard_map/ppermute | solution.py:291
  69.7 0.0 collective-permute-start.3
  69.7 1.6 collective-permute-start
  71.3 2.1 collective-permute-start.1
  73.4 4.8 %prep.1 = (bf16[16,128,512]{2,1,0:T(8,128)(2,1)}, bf16[768,256]{1,0:T(8,128)(2,1)}) custom-call(s32[16,4,128,128]{3,2,1,0:T(8,128)} %bitcast.25, bf16[256,256]{1,0:T(8,128)(2,1)} %ws_ref.3, bf16[3,256,256]{2,1,0:T(8,128)(2,1)} %wt_ref.3), custom_call_target="tpu_custom_call" | custom-call | flops 100663296 | bytes 8388608 | tf_op jit(solution)/shard_map/prep/pallas_call | solution.py:50
  78.3 64.7 %pack.6 = (bf16[2,1,4,128,256]{4,3,2,1,0:T(8,128)(2,1)}, bf16[2,1,4,128,256]{4,3,2,1,0:T(8,128)(2,1)}, bf16[2,4,1,128,256]{4,3,2,1,0:T(8,128)(2,1)}, bf16[2,4,1,128,256]{4,3,2,1,0:T(8,128)(2,1)}) custom-call(bf16[4,4,4,128,256]{4,3,2,1,0:T(8,128)(2,1)} %feat.7), custom_call_target="tpu_custom_call" | custom-call | bytes 6291456 | tf_op jit(solution)/shard_map/pack/pallas_call | solution.py:88
  142.9 3.6 %collective-permute-start.6 = (bf16[2,1,4,128,256]{4,3,2,1,0:T(8,128)(2,1)}, bf16[2,1,4,128,256]{4,3,2,1,0:T(8,128)(2,1)}, u32[]{:S(2)}, u32[]{:S(2)}) collective-permute-start(bf16[2,1,4,128,256]{4,3,2,1,0:T(8,128)(2,1)} %get-tuple-element.43), channel_id=1, source_target_pairs={{0,32},{32,64},{64,96},{96,0},{1,33},{33,65},{65,97},{97,1},{2,34}... | collective-permute-start | bytes 1572872 | tf_op jit(solution)/shard_map/ppermute | solution.py:291
  146.5 0.0 collective-permute-done.2.refs_0_.rest_2_
  146.6 17.0 %pack.5 = (bf16[2,2,1,128,256]{4,3,2,1,0:T(8,128)(2,1)}, bf16[2,2,1,128,256]{4,3,2,1,0:T(8,128)(2,1)}) custom-call(bf16[2,1,4,128,256]{4,3,2,1,0:T(8,128)(2,1)} %collective-permute-done.2.refs_0_.rest_2_, bf16[2,1,4,128,256]{4,3,2,1,0:T(8,128)(2,1)} %collective-permute-done.3.refs_1_.rest_3_), custom_call_target="tpu_custom_call" | custom-call | bytes 6291456 | tf_op jit(solution)/shard_map/pack/pallas_call | solution.py:88
  163.6 0.1 collective-permute-start.4
  163.7 0.0 collective-permute-done.rest_0_
  163.7 2.7 collective-permute-start.5
  166.3 0.6 reshape.39.codes
  166.9 4.6 %aggregate.4 = bf16[2,2,4,128,256]{4,3,2,1,0:T(8,128)(2,1)} custom-call(s32[64]{0:T(128)} %reshape.39.codes, bf16[4,4,4,128,256]{4,3,2,1,0:T(8,128)(2,1)} %feat.7, bf16[2,4,1,128,256]{4,3,2,1,0:T(8,128)(2,1)} %collective-permute-done.rest_0_, bf16[2,4,1,128,256]{4,3,2,1,0:T(8,128)(2,1)} %collective-permute-done.1.rest_1_, ...), custom_call_target="tpu_custom_call" | custom-call | flops 536870912 | bytes 8388608 | tf_op jit(solution)/shard_map/aggregate/pallas_call | solution.py:152
  171.6 3.3 %collective-permute-start.13 = (bf16[2,1024,256]{2,1,0:T(8,128)(2,1)}, bf16[2,1024,256]{2,1,0:T(8,128)(2,1)}, u32[]{:S(2)}, u32[]{:S(2)}) collective-permute-start(bf16[2,1024,256]{2,1,0:T(8,128)(2,1)} %bitcast.26), channel_id=1, source_target_pairs={{0,1},{1,2},{2,3},{3,4},{4,5},{5,6},{6,7},{8,9},{9,10},{10,11},{11... | collective-permute-start | bytes 3145736 | tf_op jit(solution)/shard_map/ppermute | solution.py:330
  174.8 0.0 collective-permute-done.6.refs_0_.rest_2_
  174.8 0.5 collective-permute-start.10
  175.4 0.9 collective-permute-start.9
  176.3 0.0 collective-permute-done.4.rest_4_
  176.3 0.0 collective-permute-done.5.rest_5_
  176.3 5.1 %aggregate.5 = bf16[2,2,4,128,256]{4,3,2,1,0:T(8,128)(2,1)} custom-call(s32[64]{0:T(128)} %reshape.39.codes, bf16[4,4,4,128,256]{4,3,2,1,0:T(8,128)(2,1)} %feat.7, bf16[2,4,1,128,256]{4,3,2,1,0:T(8,128)(2,1)} %collective-permute-done.rest_0_, bf16[2,4,1,128,256]{4,3,2,1,0:T(8,128)(2,1)} %collective-permute-done.1.rest_1_, ...), custom_call_target="tpu_custom_call" | custom-call | flops 536870912 | bytes 8388608 | tf_op jit(solution)/shard_map/aggregate/pallas_call | solution.py:152
  181.4 4.0 %collective-permute-start.8 = (bf16[2,1024,256]{2,1,0:T(8,128)(2,1)}, bf16[2,1024,256]{2,1,0:T(8,128)(2,1)}, u32[]{:S(2)}, u32[]{:S(2)}) collective-permute-start(bf16[2,1024,256]{2,1,0:T(8,128)(2,1)} %bitcast.28), channel_id=1, source_target_pairs={{0,1},{1,2},{2,3},{3,4},{4,5},{5,6},{6,7},{8,9},{9,10},{10,11},{11... | collective-permute-start | bytes 3145736 | tf_op jit(solution)/shard_map/ppermute | solution.py:333
  185.4 1.0 collective-permute-done.10.rest_1_
  186.4 1.5 collective-permute-done.9.rest_0_
  187.8 17.0 %pack.7 = (bf16[2,2,1,128,256]{4,3,2,1,0:T(8,128)(2,1)}, bf16[2,2,1,128,256]{4,3,2,1,0:T(8,128)(2,1)}) custom-call(bf16[2,1,4,128,256]{4,3,2,1,0:T(8,128)(2,1)} %collective-permute-done.6.refs_0_.rest_2_, bf16[2,1,4,128,256]{4,3,2,1,0:T(8,128)(2,1)} %collective-permute-done.7.refs_1_.rest_3_), custom_call_target="tpu_custom_call" | custom-call | bytes 6291456 | tf_op jit(solution)/shard_map/pack/pallas_call | solution.py:88
  204.9 0.1 collective-permute-start.11
  205.0 2.7 collective-permute-start.12
  207.6 4.7 %aggregate.7 = bf16[2,2,4,128,256]{4,3,2,1,0:T(8,128)(2,1)} custom-call(s32[64]{0:T(128)} %reshape.39.codes, bf16[4,4,4,128,256]{4,3,2,1,0:T(8,128)(2,1)} %feat.7, bf16[2,4,1,128,256]{4,3,2,1,0:T(8,128)(2,1)} %collective-permute-done.9.rest_0_, bf16[2,4,1,128,256]{4,3,2,1,0:T(8,128)(2,1)} %collective-permute-done.10.rest_1_, ...), custom_call_target="tpu_custom_call" | custom-call | flops 536870912 | bytes 8388608 | tf_op jit(solution)/shard_map/aggregate/pallas_call | solution.py:152
  212.3 5.6 %mix.4 = (bf16[4,2048,256]{2,1,0:T(8,128)(2,1)}, f32[768,256]{1,0:T(8,128)}) custom-call(bf16[2,1024,256]{2,1,0:T(8,128)(2,1)} %bitcast.21, bf16[2,1024,256]{2,1,0:T(8,128)(2,1)} %bitcast.27, bf16[4,2048,256]{2,1,0:T(8,128)(2,1)} %bitcast.12, bf16[4,2048,256]{2,1,0:T(8,128)(2,1)} %bitcast.16, bf16[768,256]{1,0:T(8,128)(2,1)} %get-tuple-element.56.v_ref), custom_call_target="tpu_custom_call" | custom-call | flops 1610612736 | bytes 10485760 | tf_op jit(solution)/shard_map/mix/pallas_call | solution.py:206
  217.9 0.0 collective-permute-done.12.rest_5_
  217.9 5.0 %aggregate.6 = bf16[2,2,4,128,256]{4,3,2,1,0:T(8,128)(2,1)} custom-call(s32[64]{0:T(128)} %reshape.39.codes, bf16[4,4,4,128,256]{4,3,2,1,0:T(8,128)(2,1)} %feat.7, bf16[2,4,1,128,256]{4,3,2,1,0:T(8,128)(2,1)} %collective-permute-done.9.rest_0_, bf16[2,4,1,128,256]{4,3,2,1,0:T(8,128)(2,1)} %collective-permute-done.10.rest_1_, ...), custom_call_target="tpu_custom_call" | custom-call | flops 536870912 | bytes 8388608 | tf_op jit(solution)/shard_map/aggregate/pallas_call | solution.py:152
  223.0 5.9 %mix.5 = (bf16[4,2048,256]{2,1,0:T(8,128)(2,1)}, f32[768,256]{1,0:T(8,128)}) custom-call(bf16[2,1024,256]{2,1,0:T(8,128)(2,1)} %bitcast.23, bf16[2,1024,256]{2,1,0:T(8,128)(2,1)} %bitcast.29, bf16[4,2048,256]{2,1,0:T(8,128)(2,1)} %bitcast.13, bf16[4,2048,256]{2,1,0:T(8,128)(2,1)} %bitcast.17, ...), custom_call_target="tpu_custom_call", output_to_operand_aliasing={{0}: (6, {})} | custom-call | flops 1610612736 | bytes 10485760 | tf_op jit(solution)/shard_map/mix/pallas_call | solution.py:206
  228.8 0.0 collective-permute-done.13.p_ref
  228.8 5.8 %mix.6 = (bf16[4,2048,256]{2,1,0:T(8,128)(2,1)}, f32[768,256]{1,0:T(8,128)}) custom-call(bf16[2,1024,256]{2,1,0:T(8,128)(2,1)} %collective-permute-done.13.p_ref, bf16[2,1024,256]{2,1,0:T(8,128)(2,1)} %bitcast.22, bf16[4,2048,256]{2,1,0:T(8,128)(2,1)} %bitcast.14, bf16[4,2048,256]{2,1,0:T(8,128)(2,1)} %bitcast.18, ...), custom_call_target="tpu_custom_call", output_to_operand_aliasing={{0}: (6, {})} | custom-call | flops 1610612736 | bytes 10485760 | tf_op jit(solution)/shard_map/mix/pallas_call | solution.py:206
  234.7 5.9 %mix.7 = (bf16[4,2048,256]{2,1,0:T(8,128)(2,1)}, f32[768,256]{1,0:T(8,128)}) custom-call(bf16[2,1024,256]{2,1,0:T(8,128)(2,1)} %collective-permute-done.8.p_ref, bf16[2,1024,256]{2,1,0:T(8,128)(2,1)} %bitcast.24, bf16[4,2048,256]{2,1,0:T(8,128)(2,1)} %bitcast.15, bf16[4,2048,256]{2,1,0:T(8,128)(2,1)} %bitcast.19, ...), custom_call_target="tpu_custom_call", output_to_operand_aliasing={{0}: (6, {})} | custom-call | flops 1610612736 | bytes 10485760 | tf_op jit(solution)/shard_map/mix/pallas_call | solution.py:206
  240.6 0.0 copy-start.1
  240.6 1.1 constant_dynamic-slice_fusion
  241.7 4.0 %collective-permute-start.14 = (f32[384,256]{1,0:T(8,128)S(1)}, f32[384,256]{1,0:T(8,128)S(1)}, u32[]{:S(2)}, u32[]{:S(2)}) collective-permute-start(f32[384,256]{1,0:T(8,128)S(1)} %constant_dynamic-slice_fusion), channel_id=1, source_target_pairs={{0,32},{32,0},{1,33},{33,1},{2,34},{34,2},{3,35},{35,3},{4,36},{36... | collective-permute-start | bytes 1179656 | tf_op jit(solution)/shard_map/ppermute | solution.py:267
  245.7 1.3 collective-permute-done.14
  247.0 1.0 dynamic-slice_add_fusion
  248.1 17.2 %all_to_all.10 = f32[64,8,256]{2,1,0:T(8,128)S(1)} all-to-all(f32[64,8,256]{2,1,0:T(8,128)S(1)} %pad_bitcast_fusion), channel_id=1, replica_groups=mesh['yh'=2,'core'=2,'gy'=4,'ta'=8] {'yh','gy','ta'}, dimensions={0} | all-to-all | bytes 1048576 | tf_op jit(solution)/shard_map/all_to_all | solution.py:269
  265.3 0.1 reduce_sum.9
  265.4 15.6 %all_to_all.11 = f32[64,8,256]{2,1,0:T(8,128)S(1)} all-to-all(f32[64,8,256]{2,1,0:T(8,128)S(1)} %broadcast_in_dim.2), channel_id=1, replica_groups=mesh['yh'=2,'core'=2,'gy'=4,'ta'=8] {'yh','gy','ta'}, dimensions={0} | all-to-all | bytes 1048576 | tf_op jit(solution)/shard_map/all_to_all | solution.py:271
  281.1 3.5 %collective-permute-start.15 = (f32[384,256]{1,0:T(8,128)S(1)}, f32[384,256]{1,0:T(8,128)S(1)}, u32[]{:S(2)}, u32[]{:S(2)}) collective-permute-start(f32[384,256]{1,0:T(8,128)S(1)} %slice_bitcast_fusion), channel_id=1, source_target_pairs={{0,32},{32,0},{1,33},{33,1},{2,34},{34,2},{3,35},{35,3},{4,36},{36... | collective-permute-start | bytes 1179656 | tf_op jit(solution)/shard_map/ppermute | solution.py:273
  284.6 1.3 collective-permute-done.15
  286.0 0.1 maximum_select_fusion.g_ref
  286.1 1.6 finish.1
  (14 shorter events, 0.1 us)
Async XLA Ops:
  65.3 81.2 %collective-permute-start.2 = (bf16[2,1,4,128,256]{4,3,2,1,0:T(8,128)(2,1)}, bf16[2,1,4,128,256]{4,3,2,1,0:T(8,128)(2,1)}, u32[]{:S(2)}, u32[]{:S(2)}) collective-permute-start(bf16[2,1,4,128,256]{4,3,2,1,0:T(8,128)(2,1)} %get-tuple-element.37), channel_id=1, source_target_pairs={{0,32},{32,64},{64,96},{96,0},{1,33},{33,65},{65,97},{97,1},{2,34}... | collective-permute-start | bytes 1572872 | tf_op jit(solution)/shard_map/ppermute | solution.py:291
  69.7 76.9 %collective-permute-start.3 = (bf16[2,1,4,128,256]{4,3,2,1,0:T(8,128)(2,1)}, bf16[2,1,4,128,256]{4,3,2,1,0:T(8,128)(2,1)}, u32[]{:S(2)}, u32[]{:S(2)}) collective-permute-start(bf16[2,1,4,128,256]{4,3,2,1,0:T(8,128)(2,1)} %get-tuple-element.38), channel_id=1, source_target_pairs={{0,96},{32,0},{64,32},{96,64},{1,97},{33,1},{65,33},{97,65},{2,98}... | collective-permute-start | bytes 1572872 | tf_op jit(solution)/shard_map/ppermute | solution.py:291
  69.7 94.0 %collective-permute-start = (bf16[2,4,1,128,256]{4,3,2,1,0:T(8,128)(2,1)}, bf16[2,4,1,128,256]{4,3,2,1,0:T(8,128)(2,1)}, u32[]{:S(2)}, u32[]{:S(2)}) collective-permute-start(bf16[2,4,1,128,256]{4,3,2,1,0:T(8,128)(2,1)} %get-tuple-element.35), channel_id=1, source_target_pairs={{0,8},{8,16},{16,24},{24,0},{1,9},{9,17},{17,25},{25,1},{2,10},{10... | collective-permute-start | bytes 1572872 | tf_op jit(solution)/shard_map/ppermute | solution.py:291
  71.3 95.6 %collective-permute-start.1 = (bf16[2,4,1,128,256]{4,3,2,1,0:T(8,128)(2,1)}, bf16[2,4,1,128,256]{4,3,2,1,0:T(8,128)(2,1)}, u32[]{:S(2)}, u32[]{:S(2)}) collective-permute-start(bf16[2,4,1,128,256]{4,3,2,1,0:T(8,128)(2,1)} %get-tuple-element.36), channel_id=1, source_target_pairs={{0,24},{8,0},{16,8},{24,16},{1,25},{9,1},{17,9},{25,17},{2,26},{10... | collective-permute-start | bytes 1572872 | tf_op jit(solution)/shard_map/ppermute | solution.py:291
  73.4 92.9 %copy-start.2 = (s32[4,4,4]{2,1,0:T(4,128)S(1)}, s32[4,4,4]{2,1,0:T(4,128)}, u32[]{:S(2)}) copy-start(s32[4,4,4]{2,1,0:T(4,128)} %param.7) | copy-start | bytes 772
  142.9 31.9 %collective-permute-start.6 = (bf16[2,1,4,128,256]{4,3,2,1,0:T(8,128)(2,1)}, bf16[2,1,4,128,256]{4,3,2,1,0:T(8,128)(2,1)}, u32[]{:S(2)}, u32[]{:S(2)}) collective-permute-start(bf16[2,1,4,128,256]{4,3,2,1,0:T(8,128)(2,1)} %get-tuple-element.43), channel_id=1, source_target_pairs={{0,32},{32,64},{64,96},{96,0},{1,33},{33,65},{65,97},{97,1},{2,34}... | collective-permute-start | bytes 1572872 | tf_op jit(solution)/shard_map/ppermute | solution.py:291
  146.5 28.8 %collective-permute-start.7 = (bf16[2,1,4,128,256]{4,3,2,1,0:T(8,128)(2,1)}, bf16[2,1,4,128,256]{4,3,2,1,0:T(8,128)(2,1)}, u32[]{:S(2)}, u32[]{:S(2)}) collective-permute-start(bf16[2,1,4,128,256]{4,3,2,1,0:T(8,128)(2,1)} %get-tuple-element.44), channel_id=1, source_target_pairs={{0,96},{32,0},{64,32},{96,64},{1,97},{33,1},{65,33},{97,65},{2,98}... | collective-permute-start | bytes 1572872 | tf_op jit(solution)/shard_map/ppermute | solution.py:291
  163.6 12.7 %collective-permute-start.4 = (bf16[2,2,1,128,256]{4,3,2,1,0:T(8,128)(2,1)}, bf16[2,2,1,128,256]{4,3,2,1,0:T(8,128)(2,1)}, u32[]{:S(2)}, u32[]{:S(2)}) collective-permute-start(bf16[2,2,1,128,256]{4,3,2,1,0:T(8,128)(2,1)} %get-tuple-element.39), channel_id=1, source_target_pairs={{0,8},{8,16},{16,24},{24,0},{1,9},{9,17},{17,25},{25,1},{2,10},{10... | collective-permute-start | bytes 786440 | tf_op jit(solution)/shard_map/ppermute | solution.py:291
  163.7 12.6 %collective-permute-start.5 = (bf16[2,2,1,128,256]{4,3,2,1,0:T(8,128)(2,1)}, bf16[2,2,1,128,256]{4,3,2,1,0:T(8,128)(2,1)}, u32[]{:S(2)}, u32[]{:S(2)}) collective-permute-start(bf16[2,2,1,128,256]{4,3,2,1,0:T(8,128)(2,1)} %get-tuple-element.40), channel_id=1, source_target_pairs={{0,24},{8,0},{16,8},{24,16},{1,25},{9,1},{17,9},{25,17},{2,26},{10... | collective-permute-start | bytes 786440 | tf_op jit(solution)/shard_map/ppermute | solution.py:291
  171.6 57.3 %collective-permute-start.13 = (bf16[2,1024,256]{2,1,0:T(8,128)(2,1)}, bf16[2,1024,256]{2,1,0:T(8,128)(2,1)}, u32[]{:S(2)}, u32[]{:S(2)}) collective-permute-start(bf16[2,1024,256]{2,1,0:T(8,128)(2,1)} %bitcast.26), channel_id=1, source_target_pairs={{0,1},{1,2},{2,3},{3,4},{4,5},{5,6},{6,7},{8,9},{9,10},{10,11},{11... | collective-permute-start | bytes 3145736 | tf_op jit(solution)/shard_map/ppermute | solution.py:330
  174.8 11.5 %collective-permute-start.10 = (bf16[2,4,1,128,256]{4,3,2,1,0:T(8,128)(2,1)}, bf16[2,4,1,128,256]{4,3,2,1,0:T(8,128)(2,1)}, u32[]{:S(2)}, u32[]{:S(2)}) collective-permute-start(bf16[2,4,1,128,256]{4,3,2,1,0:T(8,128)(2,1)} %get-tuple-element.48), channel_id=1, source_target_pairs={{0,24},{8,0},{16,8},{24,16},{1,25},{9,1},{17,9},{25,17},{2,26},{10... | collective-permute-start | bytes 1572872 | tf_op jit(solution)/shard_map/ppermute | solution.py:291
  175.4 12.5 %collective-permute-start.9 = (bf16[2,4,1,128,256]{4,3,2,1,0:T(8,128)(2,1)}, bf16[2,4,1,128,256]{4,3,2,1,0:T(8,128)(2,1)}, u32[]{:S(2)}, u32[]{:S(2)}) collective-permute-start(bf16[2,4,1,128,256]{4,3,2,1,0:T(8,128)(2,1)} %get-tuple-element.47), channel_id=1, source_target_pairs={{0,8},{8,16},{16,24},{24,0},{1,9},{9,17},{17,25},{25,1},{2,10},{10... | collective-permute-start | bytes 1572872 | tf_op jit(solution)/shard_map/ppermute | solution.py:291
  181.4 53.3 %collective-permute-start.8 = (bf16[2,1024,256]{2,1,0:T(8,128)(2,1)}, bf16[2,1024,256]{2,1,0:T(8,128)(2,1)}, u32[]{:S(2)}, u32[]{:S(2)}) collective-permute-start(bf16[2,1024,256]{2,1,0:T(8,128)(2,1)} %bitcast.28), channel_id=1, source_target_pairs={{0,1},{1,2},{2,3},{3,4},{4,5},{5,6},{6,7},{8,9},{9,10},{10,11},{11... | collective-permute-start | bytes 3145736 | tf_op jit(solution)/shard_map/ppermute | solution.py:333
  204.9 13.0 %collective-permute-start.11 = (bf16[2,2,1,128,256]{4,3,2,1,0:T(8,128)(2,1)}, bf16[2,2,1,128,256]{4,3,2,1,0:T(8,128)(2,1)}, u32[]{:S(2)}, u32[]{:S(2)}) collective-permute-start(bf16[2,2,1,128,256]{4,3,2,1,0:T(8,128)(2,1)} %get-tuple-element.53), channel_id=1, source_target_pairs={{0,8},{8,16},{16,24},{24,0},{1,9},{9,17},{17,25},{25,1},{2,10},{10... | collective-permute-start | bytes 786440 | tf_op jit(solution)/shard_map/ppermute | solution.py:291
  205.0 13.0 %collective-permute-start.12 = (bf16[2,2,1,128,256]{4,3,2,1,0:T(8,128)(2,1)}, bf16[2,2,1,128,256]{4,3,2,1,0:T(8,128)(2,1)}, u32[]{:S(2)}, u32[]{:S(2)}) collective-permute-start(bf16[2,2,1,128,256]{4,3,2,1,0:T(8,128)(2,1)} %get-tuple-element.54), channel_id=1, source_target_pairs={{0,24},{8,0},{16,8},{24,16},{1,25},{9,1},{17,9},{25,17},{2,26},{10... | collective-permute-start | bytes 786440 | tf_op jit(solution)/shard_map/ppermute | solution.py:291
  240.5 45.5 %copy-start = (bf16[3,256,256]{2,1,0:T(8,128)(2,1)S(1)}, bf16[3,256,256]{2,1,0:T(8,128)(2,1)}, u32[]{:S(2)}) copy-start(bf16[3,256,256]{2,1,0:T(8,128)(2,1)} %wt_ref.3) | copy-start | bytes 1179652
  240.6 45.5 %copy-start.1 = (bf16[256,256]{1,0:T(8,128)(2,1)S(1)}, bf16[256,256]{1,0:T(8,128)(2,1)}, u32[]{:S(2)}) copy-start(bf16[256,256]{1,0:T(8,128)(2,1)} %ws_ref.3) | copy-start | bytes 393220
  241.7 5.4 %collective-permute-start.14 = (f32[384,256]{1,0:T(8,128)S(1)}, f32[384,256]{1,0:T(8,128)S(1)}, u32[]{:S(2)}, u32[]{:S(2)}) collective-permute-start(f32[384,256]{1,0:T(8,128)S(1)} %constant_dynamic-slice_fusion), channel_id=1, source_target_pairs={{0,32},{32,0},{1,33},{33,1},{2,34},{34,2},{3,35},{35,3},{4,36},{36... | collective-permute-start | bytes 1179656 | tf_op jit(solution)/shard_map/ppermute | solution.py:267
  281.1 4.9 %collective-permute-start.15 = (f32[384,256]{1,0:T(8,128)S(1)}, f32[384,256]{1,0:T(8,128)S(1)}, u32[]{:S(2)}, u32[]{:S(2)}) collective-permute-start(f32[384,256]{1,0:T(8,128)S(1)} %slice_bitcast_fusion), channel_id=1, source_target_pairs={{0,32},{32,0},{1,33},{33,1},{2,34},{34,2},{3,35},{35,3},{4,36},{36... | collective-permute-start | bytes 1179656 | tf_op jit(solution)/shard_map/ppermute | solution.py:273

commit v4 on v3

--- a/solution.py
+++ b/solution.py
@@ -13,7 +13,7 @@
 BF16 = jnp.bfloat16
 F32 = jnp.float32
 GX = ("yh", "core")
-MIX_ROWS = 512
+MIX_ROWS = 256
 VMEM = 65300 << 10
 EVERY = ("yh", "core", "gy", "ta")
 REST = ("yh", "gy", "ta")
@@ -88,7 +88,7 @@
     return pl.pallas_call(
         functools.partial(pack_kernel, moves, len(arrays)),
         in_specs=[anywhere] * len(arrays),
-        out_specs=[anywhere] * len(shapes),
+        out_specs=[whole_vmem()] * len(shapes),
         out_shape=[jax.ShapeDtypeStruct(shape, BF16) for shape in shapes],
         scratch_shapes=[pltpu.SemaphoreType.DMA((len(moves),))],
         compiler_params=pltpu.CompilerParams(vmem_limit_bytes=VMEM),
@@ -97,71 +97,99 @@
     )(*arrays)
 
 
-def agg_kernel(first, xs, edge, codes, feat, *rest):
-    *halo, mask_hbm, out_ref, ext, mask_ref, sems = rest
+def agg_kernel(first, xs, edge, pieces, codes, feat, *rest):
+    *ins, ext, mask_ref, out_ref, sems = rest
+    halo, mask_hbm, outs = ins[: -pieces - 1], ins[-pieces - 1], ins[-pieces:]
     frames, _, ny = out_ref.shape[:3]
     nx = feat.shape[1]
-    span = pl.ds(first, frames)
-    moves = [
-        (feat.at[span], ext.at[:, edge : nx + edge, 1 : ny + 1]),
-        (halo[0], ext.at[:, edge : nx + edge, 0:1]),
-        (halo[1], ext.at[:, edge : nx + edge, ny + 1 : ny + 2]),
-    ] + [
-        (mask_hbm.at[x * ny : (x + 1) * ny], mask_ref.at[i * ny : (i + 1) * ny])
-        for i, x in enumerate(xs)
-    ]
-    if edge:
-        xlo, xhi, clo, chi = halo[2:]
-        moves += [
-            (xlo, ext.at[:, 0:1, 1 : ny + 1]),
-            (xhi, ext.at[:, nx + 1 : nx + 2, 1 : ny + 1]),
-            (clo.at[:, 0:1], ext.at[:, 0:1, 0:1]),
-            (clo.at[:, 1:2], ext.at[:, nx + 1 : nx + 2, 0:1]),
-            (chi.at[:, 0:1], ext.at[:, 0:1, ny + 1 : ny + 2]),
-            (chi.at[:, 1:2], ext.at[:, nx + 1 : nx + 2, ny + 1 : ny + 2]),
+    inside = slice(edge, nx + edge)
+    groups = []
+    for f in range(frames):
+        moves = [
+            (feat.at[first + f], ext.at[f, inside, 1 : ny + 1]),
+            (halo[0].at[f], ext.at[f, inside, 0:1]),
+            (halo[1].at[f], ext.at[f, inside, ny + 1 : ny + 2]),
         ]
-    copies = [
-        pltpu.make_async_copy(src, dst, sems.at[i]) for i, (src, dst) in enumerate(moves)
-    ]
-    for copy in copies:
-        copy.start()
-    for copy in copies:
+        if f == 0:
+            moves += [
+                (mask_hbm.at[x * ny : (x + 1) * ny], mask_ref.at[i * ny : (i + 1) * ny])
+                for i, x in enumerate(xs)
+            ]
+        if edge:
+            xlo, xhi, clo, chi = (ref.at[f] for ref in halo[2:])
+            moves += [
+                (xlo, ext.at[f, 0:1, 1 : ny + 1]),
+                (xhi, ext.at[f, nx + 1 : nx + 2, 1 : ny + 1]),
+                (clo.at[0:1], ext.at[f, 0:1, 0:1]),
+                (clo.at[1:2], ext.at[f, nx + 1 : nx + 2, 0:1]),
+                (chi.at[0:1], ext.at[f, 0:1, ny + 1 : ny + 2]),
+                (chi.at[1:2], ext.at[f, nx + 1 : nx + 2, ny + 1 : ny + 2]),
+            ]
+        groups.append(moves)
+    copies, used = [], 0
+    for moves in groups:
+        copies.append(
+            [
+                pltpu.make_async_copy(src, dst, sems.at[used + i])
+                for i, (src, dst) in enumerate(moves)
+            ]
+        )
+        used += len(moves)
+        for copy in copies[-1]:
+            copy.start()
+    slots = mask_ref.shape[2] // mask_ref.shape[1]
+    sent = []
+    for f in range(frames):
+        for copy in copies[f]:
+            copy.wait()
+        for i, x in enumerate(xs):
+            for y in range(ny):
+                places = []
+                for k in range(slots):
+                    code = codes[(x * ny + y) * slots + k]
+                    places.append(
+                        (x - 1 + edge + lax.div(code, 3), y + lax.rem(code, 3))
+                    )
+                source = jnp.concatenate([ext[f, sx, sy] for sx, sy in places], axis=0)
+                summed = jnp.dot(
+                    mask_ref[i * ny + y], source, preferred_element_type=F32
+                )
+                out_ref[f, i, y] = (0.18 * summed).astype(BF16)
+        piece = len(xs) // pieces
+        for n, out in enumerate(outs):
+            rows = slice(n * piece, (n + 1) * piece)
+            copy = pltpu.make_async_copy(
+                out_ref.at[f, rows], out.at[f], sems.at[used + f * pieces + n]
+            )
+            copy.start()
+            sent.append(copy)
+    for copy in sent:
         copy.wait()
-    slots = mask_ref.shape[2] // mask_ref.shape[1]
-    for i, x in enumerate(xs):
-        for y in range(ny):
-            tile = x * ny + y
-            places = []
-            for k in range(slots):
-                code = codes[tile * slots + k]
-                places.append((x - 1 + edge + lax.div(code, 3), y + lax.rem(code, 3)))
-            mask = mask_ref[i * ny + y]
-            for f in range(frames):
-                source = jnp.concatenate([ext[f, sx, sy] for sx, sy in places], axis=0)
-                summed = jnp.dot(mask, source, preferred_element_type=F32)
-                out_ref[f, i, y] = (0.18 * summed).astype(BF16)
-
-
-def aggregate(first, xs, codes, features, halo, mask):
+
+
+def aggregate(first, xs, codes, features, halo, mask, pieces=1):
     _, nx, ny, lipids, width = features.shape
     frames = 2
     slots = mask.shape[2] // lipids
     edge = 1 if len(halo) > 2 else 0
     anywhere = pl.BlockSpec(memory_space=pl.ANY)
     flops = 2 * frames * len(xs) * ny * lipids * mask.shape[2] * width
+    out_shape = (frames, len(xs), ny, lipids, width)
     out = pl.pallas_call(
-        functools.partial(agg_kernel, first, xs, edge),
-        in_specs=[
-            pl.BlockSpec(memory_space=pltpu.SMEM),
-            pl.BlockSpec(memory_space=pltpu.HBM),
+        functools.partial(agg_kernel, first, xs, edge, pieces),
+        in_specs=[pl.BlockSpec(memory_space=pltpu.SMEM)] + [anywhere] * (len(halo) + 2),
+        out_specs=[anywhere] * pieces,
+        out_shape=[
+            jax.ShapeDtypeStruct(
+                (frames, len(xs) // pieces, ny, lipids, width), BF16
+            )
         ]
-        + [anywhere] * (len(halo) + 1),
-        out_specs=whole_vmem(),
-        out_shape=jax.ShapeDtypeStruct((frames, len(xs), ny, lipids, width), BF16),
+        * pieces,
         scratch_shapes=[
             pltpu.VMEM((frames, nx + 2 * edge, ny + 2, lipids, width), BF16),
             pltpu.VMEM((len(xs) * ny, lipids, slots * lipids), BF16),
-            pltpu.SemaphoreType.DMA((9 + len(xs),)),
+            pltpu.VMEM(out_shape, BF16),
+            pltpu.SemaphoreType.DMA((frames * (12 + len(xs)),)),
         ],
         compiler_params=pltpu.CompilerParams(vmem_limit_bytes=VMEM),
         cost_estimate=pl.CostEstimate(
@@ -169,57 +197,89 @@
         ),
         name="aggregate",
     )(codes, features, *halo, mask)
-    return out.reshape(frames, -1, width)
-
-
-def mix_kernel(p_ref, q_ref, feat_ref, cot_ref, v_ref, *rest):
-    *given, up_ref, g_ref = rest
-
-    @pl.when(pl.program_id(0) == 0)
-    def _():
-        g_ref[...] = given[0][...] if given else jnp.zeros_like(g_ref)
-
-    before = [p_ref[0], p_ref[1], q_ref[0], q_ref[1]]
-    rows, grads = [], []
-    for f in range(2):
-        left = jnp.concatenate([before[f + 2], before[f + 1], before[f]], axis=1)
-        mixed = jnp.dot(left, v_ref[...], preferred_element_type=F32)
-        s = 0.5 * jnp.tanh(0.5 * mixed) + 0.5
-        up_ref[f] = (feat_ref[f].astype(F32) + mixed * s).astype(BF16)
-        grad = cot_ref[f].astype(F32) * s * (1.0 + mixed * (1.0 - s))
-        rows.append(left)
-        grads.append(grad.astype(BF16))
-    left = jnp.concatenate(rows, axis=0)
-    grad = jnp.concatenate(grads, axis=0)
-    g_ref[...] += lax.dot_general(
-        left, grad, (((0,), (0,)), ((), ())), preferred_element_type=F32
-    )
-
-
-def mix(half, place, prev, now, features, cotangent, v, given=()):
+    return [piece.reshape(frames, -1, width) for piece in out]
+
+
+def mix_kernel(half, places, *refs):
+    p_hbm, q_hbm, feat_hbm, cot_hbm, v_hbm, *given = refs[:-9]
+    up_hbm, g_ref, p_ref, q_ref, feat_ref, cot_ref, v_ref, up_ref, sems = refs[-9:]
+    rows, count = MIX_ROWS, len(places)
+    pair = slice(2 * half, 2 * half + 2)
+    loads = [[pltpu.make_async_copy(v_hbm, v_ref, sems.at[0])]]
+    for c, place in enumerate(places):
+        here, there = slice(c * rows, (c + 1) * rows), slice(place, place + rows)
+        loads += [
+            [
+                pltpu.make_async_copy(src, dst.at[:, here], sems.at[1 + 4 * c + i])
+                for i, (src, dst) in enumerate(
+                    (
+                        (q_hbm.at[:, here], q_ref),
+                        (p_hbm.at[:, here], p_ref),
+                        (feat_hbm.at[pair, there], feat_ref),
+                        (cot_hbm.at[pair, there], cot_ref),
+                    )
+                )
+            ]
+        ]
+    stores = [
+        pltpu.make_async_copy(
+            up_ref.at[:, c * rows : (c + 1) * rows],
+            up_hbm.at[pair, place : place + rows],
+            sems.at[1 + 4 * count + c],
+        )
+        for c, place in enumerate(places)
+    ]
+    for copy in sum(loads, []):
+        copy.start()
+    loads[0][0].wait()
+    g_ref[...] = given[0][...] if given else jnp.zeros_like(g_ref)
+    for c in range(count):
+        for copy in loads[c + 1]:
+            copy.wait()
+        here = slice(c * rows, (c + 1) * rows)
+        before = [p_ref[0, here], p_ref[1, here], q_ref[0, here], q_ref[1, here]]
+        lefts, grads = [], []
+        for f in range(2):
+            left = jnp.concatenate([before[f + 2], before[f + 1], before[f]], axis=1)
+            mixed = jnp.dot(left, v_ref[...], preferred_element_type=F32)
+            s = 0.5 * jnp.tanh(0.5 * mixed) + 0.5
+            silu = mixed * s
+            up_ref[f, here] = (feat_ref[f, here].astype(F32) + silu).astype(BF16)
+            grad = cot_ref[f, here].astype(F32) * (s + silu * (1.0 - s))
+            lefts.append(left)
+            grads.append(grad.astype(BF16))
+        stores[c].start()
+        g_ref[...] += lax.dot_general(
+            jnp.concatenate(lefts, axis=0),
+            jnp.concatenate(grads, axis=0),
+            (((0,), (0,)), ((), ())),
+            preferred_element_type=F32,
+        )
+    for copy in stores:
+        copy.wait()
+
+
+def mix(half, places, prev, now, features, cotangent, v, given=(), vmem=None):
     frames, count, width = now.shape
-    rows = MIX_ROWS
-    taps = v.shape[0] // width
-    pair = pl.BlockSpec((frames, rows, width), lambda i: (0, i, 0))
-    here = pl.BlockSpec((frames, rows, width), lambda i: (half, place(i), 0))
-    full_v = pl.BlockSpec((taps * width, width), lambda i: (0, 0))
+    anywhere = pl.BlockSpec(memory_space=pl.ANY)
+    block = pltpu.VMEM(now.shape, BF16)
     return pl.pallas_call(
-        mix_kernel,
-        grid=(count // rows,),
-        in_specs=[pair, pair, here, here, full_v]
-        + ([full_v, pl.BlockSpec(memory_space=pl.ANY)] if given else []),
-        out_specs=[here, full_v],
+        functools.partial(mix_kernel, half, places),
+        in_specs=[anywhere] * 5 + ([whole_vmem(), anywhere] if given else []),
+        out_specs=[anywhere, whole_vmem()],
         out_shape=[
             jax.ShapeDtypeStruct(features.shape, BF16),
-            jax.ShapeDtypeStruct((taps * width, width), F32),
+            jax.ShapeDtypeStruct(v.shape, F32),
+        ],
+        scratch_shapes=[block] * 4
+        + [
+            pltpu.VMEM(v.shape, BF16),
+            block,
+            pltpu.SemaphoreType.DMA((1 + 5 * len(places),)),
         ],
         input_output_aliases={6: 0} if given else {},
-        compiler_params=pltpu.CompilerParams(vmem_limit_bytes=VMEM),
-        cost_estimate=pl.CostEstimate(
-            flops=4 * frames * count * taps * width * width,
-            bytes_accessed=10 << 20,
-            transcendentals=frames * count * width,
-        ),
+        compiler_params=pltpu.CompilerParams(vmem_limit_bytes=vmem or VMEM),
+        cost_estimate=pl.CostEstimate(flops=1, bytes_accessed=1, transcendentals=0),
         name="mix",
     )(prev, now, features, cotangent, v, *given)
 
@@ -326,29 +386,31 @@
     x_a = exchange(GX, *edges_a[:2])
     y_a = exchange("gy", *edges_a[2:])
     c_b = corners(x_b)
-    inner_b = aggregate(2, inner, codes, features, y_b, mask)
+    (inner_b,) = aggregate(2, inner, codes, features, y_b, mask)
     prev_inner = lax.ppermute(inner_b, "ta", onward)
-    c_b, _, _ = lax.optimization_barrier((c_b, inner_b, x_a))
-    outer_b = aggregate(2, outer, codes, features, (*y_b, *x_b, *c_b), mask)
-    prev_outer = lax.ppermute(outer_b, "ta", onward)
+    c_b, _, _, _ = lax.optimization_barrier((c_b, inner_b, x_a, y_a))
+    outer_b = aggregate(2, outer, codes, features, (*y_b, *x_b, *c_b), mask, 2)
+    prev_first = lax.ppermute(outer_b[0], "ta", onward)
+    prev_last = lax.ppermute(outer_b[1], "ta", onward)
     x_a, y_a, mask_a, _ = lax.optimization_barrier((x_a, y_a, mask, outer_b))
     c_a = corners(x_a)
-    inner_a = aggregate(0, inner, codes, features, y_a, mask_a)
-    outer_a = aggregate(0, outer, codes, features, (*y_a, *x_a, *c_a), mask_a)
+    (inner_a,) = aggregate(0, inner, codes, features, y_a, mask_a)
+    outer_a = aggregate(0, outer, codes, features, (*y_a, *x_a, *c_a), mask_a, 2)
     feat = features.reshape(frames, count, width)
     cot = cotangent.reshape(frames, count, width)
-    per_row = ny * lipids // MIX_ROWS
-
-    def in_inner(i):
-        return i + per_row
-
-    def in_outer(i):
-        return i + lax.div(i, per_row) * (nx - 2) * per_row
-
-    updated, total = mix(1, in_inner, inner_a, inner_b, feat, cot, v)
-    updated, total = mix(1, in_outer, outer_a, outer_b, feat, cot, v, (total, updated))
-    updated, total = mix(0, in_inner, prev_inner, inner_a, feat, cot, v, (total, updated))
-    updated, total = mix(0, in_outer, prev_outer, outer_a, feat, cot, v, (total, updated))
+    a_row = ny * lipids
+    groups = [inner, outer[:1], outer[1:]]
+    chunks = [
+        [x * a_row + r for x in xs for r in range(0, a_row, MIX_ROWS)] for xs in groups
+    ]
+    now_b, now_a = (inner_b, *outer_b), (inner_a, *outer_a)
+    state = ()
+    for chunk, prev, now in zip(chunks, now_a, now_b):
+        updated, total = mix(1, chunk, prev, now, feat, cot, v, state)
+        state = (total, updated)
+    for chunk, prev, now in zip(chunks, (prev_inner, prev_first, prev_last), now_a):
+        updated, total = mix(0, chunk, prev, now, feat, cot, v, state)
+        state = (total, updated)
     total = all_sum(total)
     scale = 1.0 / math.sqrt(frames * count * lax.axis_size(EVERY))
     grad_space, grad_time = finish(scale, total, w_space, w_time)

time: 288 us -> 183 us (0.64)
  Pallas kernels: 212 us -> 70.2 us
  blocking collectives: 32.8 us -> 63 us
  starting transfers between devices: 33.5 us -> 37.4 us
    pallas_call x4, Pallas kernels: 163 us -> 9.72 us  [pack(): pl.pallas_call(functools.partial(pack_kernel, moves, len(arrays)), in_spe...]
    all_to_all x1, blocking collectives: 17.2 us -> 47.4 us  [all_sum(): lax.all_to_all(mine.reshape(count, block, width), REST, 0, 0, tiled=True)]
    pallas_call x8 -> x10, Pallas kernels: 42.6 us -> 54.1 us  [the longest x6 36.1 us: mix(): pl.pallas_call(functools.partial(mix_kernel, half, places), in_specs=[any...]
    ppermute x6, waiting for transfers between devices: 1.48 us -> 4.74 us  [exchange(): lax.ppermute(high_edge, axis, up)]
    ppermute x1 -> x2, starting transfers between devices: 4.01 us -> 6.77 us  [the longest x1 4.62 us: shards(): prev_first = lax.ppermute(outer_b[0], 'ta', onward)]
  transfers between devices with their start and end apart: 16 -> 17, of which waited for: 4 -> 4; matrix products, arithmetic and copies ran while one was open for 0% -> 0% of each run, Pallas kernels for 49% -> 33%
where the time goes in v4:
time: 183 us; the launch traced here: 182 us
  Pallas kernels  70.2 us (38%)
  blocking collectives  63 us (34%)
  starting transfers between devices  37.4 us (20%)
  waiting for transfers between devices  7.47 us (4%)
  local copies, waits for them, and re-layouts  1.86 us (1%)
    all_to_all x1, blocking collectives, all_sum(): lax.all_to_all(mine.reshape(count, block, width), REST, 0, 0, tiled=True)  47.4 us
    pallas_call x6, Pallas kernels, mix(): pl.pallas_call(functools.partial(mix_kernel, half, places), in_specs=[any...  36.1 us
    pallas_call x4, Pallas kernels, aggregate(): pl.pallas_call(functools.partial(agg_kernel, first, xs, edge, pieces), in...  18 us
    all_to_all x1, blocking collectives, all_sum(): back = lax.all_to_all(spread, REST, 0, 0, tiled=True)  15.6 us
    ppermute x6, starting transfers between devices, exchange(): lax.ppermute(high_edge, axis, up)  9.99 us
    ppermute x6, starting transfers between devices, exchange(): lax.ppermute(low_edge, axis, down)  9.97 us
    pallas_call x4, Pallas kernels, pack(): pl.pallas_call(functools.partial(pack_kernel, moves, len(arrays)), in_spe...  9.72 us
    pallas_call x1, Pallas kernels, prep(): pl.pallas_call(prep_kernel, grid=(tiles // 4,), in_specs=[pl.BlockSpec((4...  4.85 us
  transfers between devices with their start and end apart: 17, of which 4 were waited for; matrix products, arithmetic and copies ran while one was open for 0% of the time, Pallas kernels for 33%

profile of v4, /device:TPU:1, one launch (start us, length us, event | category | flops | bytes accessed | tf_op | source)
XLA Modules:
  0.0 182.0 jit_solution(16458179082738987993)
XLA Ops:
  0.6 2.9 %pack.4 = (bf16[2,1,4,128,256]{4,3,2,1,0:T(8,128)(2,1)}, bf16[2,1,4,128,256]{4,3,2,1,0:T(8,128)(2,1)}, bf16[2,4,1,128,256]{4,3,2,1,0:T(8,128)(2,1)}, bf16[2,4,1,128,256]{4,3,2,1,0:T(8,128)(2,1)}) custom-call(bf16[4,4,4,128,256]{4,3,2,1,0:T(8,128)(2,1)} %feat.7), custom_call_target="tpu_custom_call" | custom-call | bytes 6291456 | tf_op jit(solution)/shard_map/pack/pallas_call | solution.py:88
  3.5 2.5 %collective-permute-start = (bf16[2,4,1,128,256]{4,3,2,1,0:T(8,128)(2,1)}, bf16[2,4,1,128,256]{4,3,2,1,0:T(8,128)(2,1)}, u32[]{:S(2)}, u32[]{:S(2)}) collective-permute-start(bf16[2,4,1,128,256]{4,3,2,1,0:T(8,128)(2,1)} %get-tuple-element.43), channel_id=1, source_target_pairs={{0,8},{8,16},{16,24},{24,0},{1,9},{9,17},{17,25},{25,1},{2,10},{10... | collective-permute-start | bytes 1572872 | tf_op jit(solution)/shard_map/ppermute | solution.py:351
  6.1 2.2 %collective-permute-start.1 = (bf16[2,4,1,128,256]{4,3,2,1,0:T(8,128)(2,1)}, bf16[2,4,1,128,256]{4,3,2,1,0:T(8,128)(2,1)}, u32[]{:S(2)}, u32[]{:S(2)}) collective-permute-start(bf16[2,4,1,128,256]{4,3,2,1,0:T(8,128)(2,1)} %get-tuple-element.44), channel_id=1, source_target_pairs={{0,24},{8,0},{16,8},{24,16},{1,25},{9,1},{17,9},{25,17},{2,26},{10... | collective-permute-start | bytes 1572872 | tf_op jit(solution)/shard_map/ppermute | solution.py:351
  8.3 3.8 %collective-permute-start.2 = (bf16[2,1,4,128,256]{4,3,2,1,0:T(8,128)(2,1)}, bf16[2,1,4,128,256]{4,3,2,1,0:T(8,128)(2,1)}, u32[]{:S(2)}, u32[]{:S(2)}) collective-permute-start(bf16[2,1,4,128,256]{4,3,2,1,0:T(8,128)(2,1)} %get-tuple-element.45), channel_id=1, source_target_pairs={{0,32},{32,64},{64,96},{96,0},{1,33},{33,65},{65,97},{97,1},{2,34}... | collective-permute-start | bytes 1572872 | tf_op jit(solution)/shard_map/ppermute | solution.py:351
  12.0 4.8 %prep.1 = (bf16[16,128,512]{2,1,0:T(8,128)(2,1)}, bf16[768,256]{1,0:T(8,128)(2,1)}) custom-call(s32[16,4,128,128]{3,2,1,0:T(8,128)} %bitcast.29, bf16[256,256]{1,0:T(8,128)(2,1)} %ws_ref.3, bf16[3,256,256]{2,1,0:T(8,128)(2,1)} %wt_ref.3), custom_call_target="tpu_custom_call" | custom-call | flops 100663296 | bytes 8388608 | tf_op jit(solution)/shard_map/prep/pallas_call | solution.py:50
  16.9 3.0 %pack.6 = (bf16[2,1,4,128,256]{4,3,2,1,0:T(8,128)(2,1)}, bf16[2,1,4,128,256]{4,3,2,1,0:T(8,128)(2,1)}, bf16[2,4,1,128,256]{4,3,2,1,0:T(8,128)(2,1)}, bf16[2,4,1,128,256]{4,3,2,1,0:T(8,128)(2,1)}) custom-call(bf16[4,4,4,128,256]{4,3,2,1,0:T(8,128)(2,1)} %feat.7), custom_call_target="tpu_custom_call" | custom-call | bytes 6291456 | tf_op jit(solution)/shard_map/pack/pallas_call | solution.py:88
  19.9 3.3 %collective-permute-start.6 = (bf16[2,1,4,128,256]{4,3,2,1,0:T(8,128)(2,1)}, bf16[2,1,4,128,256]{4,3,2,1,0:T(8,128)(2,1)}, u32[]{:S(2)}, u32[]{:S(2)}) collective-permute-start(bf16[2,1,4,128,256]{4,3,2,1,0:T(8,128)(2,1)} %get-tuple-element.51), channel_id=1, source_target_pairs={{0,32},{32,64},{64,96},{96,0},{1,33},{33,65},{65,97},{97,1},{2,34}... | collective-permute-start | bytes 1572872 | tf_op jit(solution)/shard_map/ppermute | solution.py:351
  23.2 0.1 collective-permute-start.8
  23.3 0.2 collective-permute-done.2.refs_0_.rest_2_
  23.5 2.5 %collective-permute-start.9 = (bf16[2,4,1,128,256]{4,3,2,1,0:T(8,128)(2,1)}, bf16[2,4,1,128,256]{4,3,2,1,0:T(8,128)(2,1)}, u32[]{:S(2)}, u32[]{:S(2)}) collective-permute-start(bf16[2,4,1,128,256]{4,3,2,1,0:T(8,128)(2,1)} %get-tuple-element.54), channel_id=1, source_target_pairs={{0,24},{8,0},{16,8},{24,16},{1,25},{9,1},{17,9},{25,17},{2,26},{10... | collective-permute-start | bytes 1572872 | tf_op jit(solution)/shard_map/ppermute | solution.py:351
  25.9 0.7 reshape.45.codes
  26.6 4.3 %aggregate.4 = bf16[2,2,4,128,256]{4,3,2,1,0:T(8,128)(2,1)} custom-call(s32[64]{0:T(128)} %reshape.45.codes, bf16[4,4,4,128,256]{4,3,2,1,0:T(8,128)(2,1)} %feat.7, bf16[2,4,1,128,256]{4,3,2,1,0:T(8,128)(2,1)} %collective-permute-done.rest_0_, bf16[2,4,1,128,256]{4,3,2,1,0:T(8,128)(2,1)} %collective-permute-done.1.rest_1_, ...), custom_call_target="tpu_custom_call" | custom-call | flops 536870912 | bytes 8388608 | tf_op jit(solution)/shard_map/aggregate/pallas_call | solution.py:178
  30.9 0.0 collective-permute-done.3.refs_1_.rest_3_
  30.9 3.3 %collective-permute-start.14 = (bf16[2,1024,256]{2,1,0:T(8,128)(2,1)}, bf16[2,1024,256]{2,1,0:T(8,128)(2,1)}, u32[]{:S(2)}, u32[]{:S(2)}) collective-permute-start(bf16[2,1024,256]{2,1,0:T(8,128)(2,1)} %bitcast.30), channel_id=1, source_target_pairs={{0,1},{1,2},{2,3},{3,4},{4,5},{5,6},{6,7},{8,9},{9,10},{10,11},{11... | collective-permute-start | bytes 3145736 | tf_op jit(solution)/shard_map/ppermute | solution.py:390
  34.2 1.9 %pack.5 = (bf16[2,2,1,128,256]{4,3,2,1,0:T(8,128)(2,1)}, bf16[2,2,1,128,256]{4,3,2,1,0:T(8,128)(2,1)}) custom-call(bf16[2,1,4,128,256]{4,3,2,1,0:T(8,128)(2,1)} %collective-permute-done.2.refs_0_.rest_2_, bf16[2,1,4,128,256]{4,3,2,1,0:T(8,128)(2,1)} %collective-permute-done.3.refs_1_.rest_3_), custom_call_target="tpu_custom_call" | custom-call | bytes 6291456 | tf_op jit(solution)/shard_map/pack/pallas_call | solution.py:88
  36.2 0.0 collective-permute-done.6.refs_0_.rest_2_
  36.2 0.1 collective-permute-start.4
  36.3 0.0 collective-permute-done.7.refs_1_.rest_3_
  36.3 2.7 %collective-permute-start.5 = (bf16[2,2,1,128,256]{4,3,2,1,0:T(8,128)(2,1)}, bf16[2,2,1,128,256]{4,3,2,1,0:T(8,128)(2,1)}, u32[]{:S(2)}, u32[]{:S(2)}) collective-permute-start(bf16[2,2,1,128,256]{4,3,2,1,0:T(8,128)(2,1)} %get-tuple-element.48), channel_id=1, source_target_pairs={{0,24},{8,0},{16,8},{24,16},{1,25},{9,1},{17,9},{25,17},{2,26},{10... | collective-permute-start | bytes 786440 | tf_op jit(solution)/shard_map/ppermute | solution.py:351
  38.9 0.0 collective-permute-done.9.rest_1_
  38.9 4.5 %collective-permute-done.4.rest_4_ = bf16[2,2,1,128,256]{4,3,2,1,0:T(8,128)(2,1)} collective-permute-done((bf16[2,2,1,128,256]{4,3,2,1,0:T(8,128)(2,1)}, bf16[2,2,1,128,256]{4,3,2,1,0:T(8,128)(2,1)}, u32[]{:S(2)}, u32[]{:S(2)}) %collective-permute-start.4) | collective-permute-done | bytes 262176 | tf_op jit(solution)/shard_map/ppermute | solution.py:351
  43.5 4.7 %aggregate.5 = (bf16[2,1,4,128,256]{4,3,2,1,0:T(8,128)(2,1)}, bf16[2,1,4,128,256]{4,3,2,1,0:T(8,128)(2,1)}) custom-call(s32[64]{0:T(128)} %reshape.45.codes, bf16[4,4,4,128,256]{4,3,2,1,0:T(8,128)(2,1)} %feat.7, bf16[2,4,1,128,256]{4,3,2,1,0:T(8,128)(2,1)} %collective-permute-done.rest_0_, bf16[2,4,1,128,256]{4,3,2,1,0:T(8,128)(2,1)} %collective-permute-done.1.rest_1_, ...), custom_call_target="tpu_custom_call" | custom-call | flops 536870912 | bytes 8388608 | tf_op jit(solution)/shard_map/aggregate/pallas_call | solution.py:178
  48.2 4.6 %collective-permute-start.13 = (bf16[2,512,256]{2,1,0:T(8,128)(2,1)}, bf16[2,512,256]{2,1,0:T(8,128)(2,1)}, u32[]{:S(2)}, u32[]{:S(2)}) collective-permute-start(bf16[2,512,256]{2,1,0:T(8,128)(2,1)} %bitcast.38), channel_id=1, source_target_pairs={{0,1},{1,2},{2,3},{3,4},{4,5},{5,6},{6,7},{8,9},{9,10},{10,11},{11... | collective-permute-start | bytes 1572872 | tf_op jit(solution)/shard_map/ppermute | solution.py:393
  52.8 2.2 %collective-permute-start.10 = (bf16[2,512,256]{2,1,0:T(8,128)(2,1)}, bf16[2,512,256]{2,1,0:T(8,128)(2,1)}, u32[]{:S(2)}, u32[]{:S(2)}) collective-permute-start(bf16[2,512,256]{2,1,0:T(8,128)(2,1)} %bitcast.36), channel_id=1, source_target_pairs={{0,1},{1,2},{2,3},{3,4},{4,5},{5,6},{6,7},{8,9},{9,10},{10,11},{11... | collective-permute-start | bytes 1572872 | tf_op jit(solution)/shard_map/ppermute | solution.py:394
  54.9 1.9 %pack.7 = (bf16[2,2,1,128,256]{4,3,2,1,0:T(8,128)(2,1)}, bf16[2,2,1,128,256]{4,3,2,1,0:T(8,128)(2,1)}) custom-call(bf16[2,1,4,128,256]{4,3,2,1,0:T(8,128)(2,1)} %collective-permute-done.6.refs_0_.rest_2_, bf16[2,1,4,128,256]{4,3,2,1,0:T(8,128)(2,1)} %collective-permute-done.7.refs_1_.rest_3_), custom_call_target="tpu_custom_call" | custom-call | bytes 6291456 | tf_op jit(solution)/shard_map/pack/pallas_call | solution.py:88
  56.9 0.2 collective-permute-start.11
  57.1 2.7 %collective-permute-start.12 = (bf16[2,2,1,128,256]{4,3,2,1,0:T(8,128)(2,1)}, bf16[2,2,1,128,256]{4,3,2,1,0:T(8,128)(2,1)}, u32[]{:S(2)}, u32[]{:S(2)}) collective-permute-start(bf16[2,2,1,128,256]{4,3,2,1,0:T(8,128)(2,1)} %get-tuple-element.64), channel_id=1, source_target_pairs={{0,24},{8,0},{16,8},{24,16},{1,25},{9,1},{17,9},{25,17},{2,26},{10... | collective-permute-start | bytes 786440 | tf_op jit(solution)/shard_map/ppermute | solution.py:351
  59.8 4.3 %aggregate.7 = bf16[2,2,4,128,256]{4,3,2,1,0:T(8,128)(2,1)} custom-call(s32[64]{0:T(128)} %reshape.45.codes, bf16[4,4,4,128,256]{4,3,2,1,0:T(8,128)(2,1)} %feat.7, bf16[2,4,1,128,256]{4,3,2,1,0:T(8,128)(2,1)} %collective-permute-done.8.rest_0_, bf16[2,4,1,128,256]{4,3,2,1,0:T(8,128)(2,1)} %collective-permute-done.9.rest_1_, ...), custom_call_target="tpu_custom_call" | custom-call | flops 536870912 | bytes 8388608 | tf_op jit(solution)/shard_map/aggregate/pallas_call | solution.py:178
  64.1 6.2 %mix.6 = (bf16[4,2048,256]{2,1,0:T(8,128)(2,1)}, f32[768,256]{1,0:T(8,128)}) custom-call(bf16[2,1024,256]{2,1,0:T(8,128)(2,1)} %bitcast.27, bf16[2,1024,256]{2,1,0:T(8,128)(2,1)} %bitcast.31, bf16[4,2048,256]{2,1,0:T(8,128)(2,1)} %bitcast.14, bf16[4,2048,256]{2,1,0:T(8,128)(2,1)} %bitcast.20, bf16[768,256]{1,0:T(8,128)(2,1)} %get-tuple-element.67.refs_4_), custom_call_target="tpu_custom_call" | custom-call | flops 1 | bytes 1 | tf_op jit(solution)/shard_map/mix/pallas_call | solution.py:266
  70.3 4.7 %aggregate.6 = (bf16[2,1,4,128,256]{4,3,2,1,0:T(8,128)(2,1)}, bf16[2,1,4,128,256]{4,3,2,1,0:T(8,128)(2,1)}) custom-call(s32[64]{0:T(128)} %reshape.45.codes, bf16[4,4,4,128,256]{4,3,2,1,0:T(8,128)(2,1)} %feat.7, bf16[2,4,1,128,256]{4,3,2,1,0:T(8,128)(2,1)} %collective-permute-done.8.rest_0_, bf16[2,4,1,128,256]{4,3,2,1,0:T(8,128)(2,1)} %collective-permute-done.9.rest_1_, ...), custom_call_target="tpu_custom_call" | custom-call | flops 536870912 | bytes 8388608 | tf_op jit(solution)/shard_map/aggregate/pallas_call | solution.py:178
  75.0 5.6 %mix.7 = (bf16[4,2048,256]{2,1,0:T(8,128)(2,1)}, f32[768,256]{1,0:T(8,128)}) custom-call(bf16[2,512,256]{2,1,0:T(8,128)(2,1)} %bitcast.34, bf16[2,512,256]{2,1,0:T(8,128)(2,1)} %bitcast.39, bf16[4,2048,256]{2,1,0:T(8,128)(2,1)} %bitcast.15, bf16[4,2048,256]{2,1,0:T(8,128)(2,1)} %bitcast.21, ...), custom_call_target="tpu_custom_call", output_to_operand_aliasing={{0}: (6, {})} | custom-call | flops 1 | bytes 1 | tf_op jit(solution)/shard_map/mix/pallas_call | solution.py:266
  80.6 5.6 %mix.8 = (bf16[4,2048,256]{2,1,0:T(8,128)(2,1)}, f32[768,256]{1,0:T(8,128)}) custom-call(bf16[2,512,256]{2,1,0:T(8,128)(2,1)} %bitcast.32, bf16[2,512,256]{2,1,0:T(8,128)(2,1)} %bitcast.37, bf16[4,2048,256]{2,1,0:T(8,128)(2,1)} %bitcast.16, bf16[4,2048,256]{2,1,0:T(8,128)(2,1)} %bitcast.22, ...), custom_call_target="tpu_custom_call", output_to_operand_aliasing={{0}: (6, {})} | custom-call | flops 1 | bytes 1 | tf_op jit(solution)/shard_map/mix/pallas_call | solution.py:266
  86.2 7.3 %mix.9 = (bf16[4,2048,256]{2,1,0:T(8,128)(2,1)}, f32[768,256]{1,0:T(8,128)}) custom-call(bf16[2,1024,256]{2,1,0:T(8,128)(2,1)} %collective-permute-done.14.refs_0_, bf16[2,1024,256]{2,1,0:T(8,128)(2,1)} %bitcast.28, bf16[4,2048,256]{2,1,0:T(8,128)(2,1)} %bitcast.17, bf16[4,2048,256]{2,1,0:T(8,128)(2,1)} %bitcast.23, ...), custom_call_target="tpu_custom_call", output_to_operand_aliasing={{0}: (6, {})} | custom-call | flops 1 | bytes 1 | tf_op jit(solution)/shard_map/mix/pallas_call | solution.py:266
  93.6 5.6 %mix.10 = (bf16[4,2048,256]{2,1,0:T(8,128)(2,1)}, f32[768,256]{1,0:T(8,128)}) custom-call(bf16[2,512,256]{2,1,0:T(8,128)(2,1)} %collective-permute-done.13.refs_0_, bf16[2,512,256]{2,1,0:T(8,128)(2,1)} %bitcast.35, bf16[4,2048,256]{2,1,0:T(8,128)(2,1)} %bitcast.18, bf16[4,2048,256]{2,1,0:T(8,128)(2,1)} %bitcast.24, ...), custom_call_target="tpu_custom_call", output_to_operand_aliasing={{0}: (6, {})} | custom-call | flops 1 | bytes 1 | tf_op jit(solution)/shard_map/mix/pallas_call | solution.py:266
  99.2 5.8 %mix.11 = (bf16[4,2048,256]{2,1,0:T(8,128)(2,1)}, f32[768,256]{1,0:T(8,128)}) custom-call(bf16[2,512,256]{2,1,0:T(8,128)(2,1)} %collective-permute-done.10.refs_0_, bf16[2,512,256]{2,1,0:T(8,128)(2,1)} %bitcast.33, bf16[4,2048,256]{2,1,0:T(8,128)(2,1)} %bitcast.19, bf16[4,2048,256]{2,1,0:T(8,128)(2,1)} %bitcast.25, ...), custom_call_target="tpu_custom_call", output_to_operand_aliasing={{0}: (6, {})} | custom-call | flops 1 | bytes 1 | tf_op jit(solution)/shard_map/mix/pallas_call | solution.py:266
  105.0 0.0 copy-start
  105.0 0.0 copy-start.1
  105.0 1.1 constant_dynamic-slice_fusion
  106.1 3.8 %collective-permute-start.15 = (f32[384,256]{1,0:T(8,128)S(1)}, f32[384,256]{1,0:T(8,128)S(1)}, u32[]{:S(2)}, u32[]{:S(2)}) collective-permute-start(f32[384,256]{1,0:T(8,128)S(1)} %constant_dynamic-slice_fusion), channel_id=1, source_target_pairs={{0,32},{32,0},{1,33},{33,1},{2,34},{34,2},{3,35},{35,3},{4,36},{36... | collective-permute-start | bytes 1179656 | tf_op jit(solution)/shard_map/ppermute | solution.py:327
  109.9 1.3 collective-permute-done.15
  111.3 1.0 dynamic-slice_add_fusion
  112.4 47.4 %all_to_all.10 = f32[64,8,256]{2,1,0:T(8,128)S(1)} all-to-all(f32[64,8,256]{2,1,0:T(8,128)S(1)} %pad_bitcast_fusion), channel_id=1, replica_groups=mesh['yh'=2,'core'=2,'gy'=4,'ta'=8] {'yh','gy','ta'}, dimensions={0} | all-to-all | bytes 1048576 | tf_op jit(solution)/shard_map/all_to_all | solution.py:329
  159.7 0.1 reduce_sum.9
  159.9 15.6 %all_to_all.11 = f32[64,8,256]{2,1,0:T(8,128)S(1)} all-to-all(f32[64,8,256]{2,1,0:T(8,128)S(1)} %broadcast_in_dim.2), channel_id=1, replica_groups=mesh['yh'=2,'core'=2,'gy'=4,'ta'=8] {'yh','gy','ta'}, dimensions={0} | all-to-all | bytes 1048576 | tf_op jit(solution)/shard_map/all_to_all | solution.py:331
  175.5 3.5 %collective-permute-start.16 = (f32[384,256]{1,0:T(8,128)S(1)}, f32[384,256]{1,0:T(8,128)S(1)}, u32[]{:S(2)}, u32[]{:S(2)}) collective-permute-start(f32[384,256]{1,0:T(8,128)S(1)} %slice_bitcast_fusion), channel_id=1, source_target_pairs={{0,32},{32,0},{1,33},{33,1},{2,34},{34,2},{3,35},{35,3},{4,36},{36... | collective-permute-start | bytes 1179656 | tf_op jit(solution)/shard_map/ppermute | solution.py:333
  179.0 1.3 collective-permute-done.16
  180.4 0.1 maximum_select_fusion.g_ref
  180.5 1.6 finish.1
  (18 shorter events, 0.1 us)
Async XLA Ops:
  3.5 19.7 %collective-permute-start = (bf16[2,4,1,128,256]{4,3,2,1,0:T(8,128)(2,1)}, bf16[2,4,1,128,256]{4,3,2,1,0:T(8,128)(2,1)}, u32[]{:S(2)}, u32[]{:S(2)}) collective-permute-start(bf16[2,4,1,128,256]{4,3,2,1,0:T(8,128)(2,1)} %get-tuple-element.43), channel_id=1, source_target_pairs={{0,8},{8,16},{16,24},{24,0},{1,9},{9,17},{17,25},{25,1},{2,10},{10... | collective-permute-start | bytes 1572872 | tf_op jit(solution)/shard_map/ppermute | solution.py:351
  6.1 17.1 %collective-permute-start.1 = (bf16[2,4,1,128,256]{4,3,2,1,0:T(8,128)(2,1)}, bf16[2,4,1,128,256]{4,3,2,1,0:T(8,128)(2,1)}, u32[]{:S(2)}, u32[]{:S(2)}) collective-permute-start(bf16[2,4,1,128,256]{4,3,2,1,0:T(8,128)(2,1)} %get-tuple-element.44), channel_id=1, source_target_pairs={{0,24},{8,0},{16,8},{24,16},{1,25},{9,1},{17,9},{25,17},{2,26},{10... | collective-permute-start | bytes 1572872 | tf_op jit(solution)/shard_map/ppermute | solution.py:351
  8.3 15.2 %collective-permute-start.2 = (bf16[2,1,4,128,256]{4,3,2,1,0:T(8,128)(2,1)}, bf16[2,1,4,128,256]{4,3,2,1,0:T(8,128)(2,1)}, u32[]{:S(2)}, u32[]{:S(2)}) collective-permute-start(bf16[2,1,4,128,256]{4,3,2,1,0:T(8,128)(2,1)} %get-tuple-element.45), channel_id=1, source_target_pairs={{0,32},{32,64},{64,96},{96,0},{1,33},{33,65},{65,97},{97,1},{2,34}... | collective-permute-start | bytes 1572872 | tf_op jit(solution)/shard_map/ppermute | solution.py:351
  12.0 18.9 %collective-permute-start.3 = (bf16[2,1,4,128,256]{4,3,2,1,0:T(8,128)(2,1)}, bf16[2,1,4,128,256]{4,3,2,1,0:T(8,128)(2,1)}, u32[]{:S(2)}, u32[]{:S(2)}) collective-permute-start(bf16[2,1,4,128,256]{4,3,2,1,0:T(8,128)(2,1)} %get-tuple-element.46), channel_id=1, source_target_pairs={{0,96},{32,0},{64,32},{96,64},{1,97},{33,1},{65,33},{97,65},{2,98}... | collective-permute-start | bytes 1572872 | tf_op jit(solution)/shard_map/ppermute | solution.py:351
  12.0 13.9 %copy-start.2 = (s32[4,4,4]{2,1,0:T(4,128)S(1)}, s32[4,4,4]{2,1,0:T(4,128)}, u32[]{:S(2)}) copy-start(s32[4,4,4]{2,1,0:T(4,128)} %param.7) | copy-start | bytes 772
  19.9 16.3 %collective-permute-start.6 = (bf16[2,1,4,128,256]{4,3,2,1,0:T(8,128)(2,1)}, bf16[2,1,4,128,256]{4,3,2,1,0:T(8,128)(2,1)}, u32[]{:S(2)}, u32[]{:S(2)}) collective-permute-start(bf16[2,1,4,128,256]{4,3,2,1,0:T(8,128)(2,1)} %get-tuple-element.51), channel_id=1, source_target_pairs={{0,32},{32,64},{64,96},{96,0},{1,33},{33,65},{65,97},{97,1},{2,34}... | collective-permute-start | bytes 1572872 | tf_op jit(solution)/shard_map/ppermute | solution.py:351
  23.2 13.1 %collective-permute-start.7 = (bf16[2,1,4,128,256]{4,3,2,1,0:T(8,128)(2,1)}, bf16[2,1,4,128,256]{4,3,2,1,0:T(8,128)(2,1)}, u32[]{:S(2)}, u32[]{:S(2)}) collective-permute-start(bf16[2,1,4,128,256]{4,3,2,1,0:T(8,128)(2,1)} %get-tuple-element.52), channel_id=1, source_target_pairs={{0,96},{32,0},{64,32},{96,64},{1,97},{33,1},{65,33},{97,65},{2,98}... | collective-permute-start | bytes 1572872 | tf_op jit(solution)/shard_map/ppermute | solution.py:351
  23.2 15.7 %collective-permute-start.8 = (bf16[2,4,1,128,256]{4,3,2,1,0:T(8,128)(2,1)}, bf16[2,4,1,128,256]{4,3,2,1,0:T(8,128)(2,1)}, u32[]{:S(2)}, u32[]{:S(2)}) collective-permute-start(bf16[2,4,1,128,256]{4,3,2,1,0:T(8,128)(2,1)} %get-tuple-element.53), channel_id=1, source_target_pairs={{0,8},{8,16},{16,24},{24,0},{1,9},{9,17},{17,25},{25,1},{2,10},{10... | collective-permute-start | bytes 1572872 | tf_op jit(solution)/shard_map/ppermute | solution.py:351
  23.5 15.4 %collective-permute-start.9 = (bf16[2,4,1,128,256]{4,3,2,1,0:T(8,128)(2,1)}, bf16[2,4,1,128,256]{4,3,2,1,0:T(8,128)(2,1)}, u32[]{:S(2)}, u32[]{:S(2)}) collective-permute-start(bf16[2,4,1,128,256]{4,3,2,1,0:T(8,128)(2,1)} %get-tuple-element.54), channel_id=1, source_target_pairs={{0,24},{8,0},{16,8},{24,16},{1,25},{9,1},{17,9},{25,17},{2,26},{10... | collective-permute-start | bytes 1572872 | tf_op jit(solution)/shard_map/ppermute | solution.py:351
  30.9 55.3 %collective-permute-start.14 = (bf16[2,1024,256]{2,1,0:T(8,128)(2,1)}, bf16[2,1024,256]{2,1,0:T(8,128)(2,1)}, u32[]{:S(2)}, u32[]{:S(2)}) collective-permute-start(bf16[2,1024,256]{2,1,0:T(8,128)(2,1)} %bitcast.30), channel_id=1, source_target_pairs={{0,1},{1,2},{2,3},{3,4},{4,5},{5,6},{6,7},{8,9},{9,10},{10,11},{11... | collective-permute-start | bytes 3145736 | tf_op jit(solution)/shard_map/ppermute | solution.py:390
  36.2 7.3 %collective-permute-start.4 = (bf16[2,2,1,128,256]{4,3,2,1,0:T(8,128)(2,1)}, bf16[2,2,1,128,256]{4,3,2,1,0:T(8,128)(2,1)}, u32[]{:S(2)}, u32[]{:S(2)}) collective-permute-start(bf16[2,2,1,128,256]{4,3,2,1,0:T(8,128)(2,1)} %get-tuple-element.47), channel_id=1, source_target_pairs={{0,8},{8,16},{16,24},{24,0},{1,9},{9,17},{17,25},{25,1},{2,10},{10... | collective-permute-start | bytes 786440 | tf_op jit(solution)/shard_map/ppermute | solution.py:351
  36.3 7.2 %collective-permute-start.5 = (bf16[2,2,1,128,256]{4,3,2,1,0:T(8,128)(2,1)}, bf16[2,2,1,128,256]{4,3,2,1,0:T(8,128)(2,1)}, u32[]{:S(2)}, u32[]{:S(2)}) collective-permute-start(bf16[2,2,1,128,256]{4,3,2,1,0:T(8,128)(2,1)} %get-tuple-element.48), channel_id=1, source_target_pairs={{0,24},{8,0},{16,8},{24,16},{1,25},{9,1},{17,9},{25,17},{2,26},{10... | collective-permute-start | bytes 786440 | tf_op jit(solution)/shard_map/ppermute | solution.py:351
  48.2 45.4 %collective-permute-start.13 = (bf16[2,512,256]{2,1,0:T(8,128)(2,1)}, bf16[2,512,256]{2,1,0:T(8,128)(2,1)}, u32[]{:S(2)}, u32[]{:S(2)}) collective-permute-start(bf16[2,512,256]{2,1,0:T(8,128)(2,1)} %bitcast.38), channel_id=1, source_target_pairs={{0,1},{1,2},{2,3},{3,4},{4,5},{5,6},{6,7},{8,9},{9,10},{10,11},{11... | collective-permute-start | bytes 1572872 | tf_op jit(solution)/shard_map/ppermute | solution.py:393
  52.8 46.4 %collective-permute-start.10 = (bf16[2,512,256]{2,1,0:T(8,128)(2,1)}, bf16[2,512,256]{2,1,0:T(8,128)(2,1)}, u32[]{:S(2)}, u32[]{:S(2)}) collective-permute-start(bf16[2,512,256]{2,1,0:T(8,128)(2,1)} %bitcast.36), channel_id=1, source_target_pairs={{0,1},{1,2},{2,3},{3,4},{4,5},{5,6},{6,7},{8,9},{9,10},{10,11},{11... | collective-permute-start | bytes 1572872 | tf_op jit(solution)/shard_map/ppermute | solution.py:394
  56.9 13.4 %collective-permute-start.11 = (bf16[2,2,1,128,256]{4,3,2,1,0:T(8,128)(2,1)}, bf16[2,2,1,128,256]{4,3,2,1,0:T(8,128)(2,1)}, u32[]{:S(2)}, u32[]{:S(2)}) collective-permute-start(bf16[2,2,1,128,256]{4,3,2,1,0:T(8,128)(2,1)} %get-tuple-element.63), channel_id=1, source_target_pairs={{0,8},{8,16},{16,24},{24,0},{1,9},{9,17},{17,25},{25,1},{2,10},{10... | collective-permute-start | bytes 786440 | tf_op jit(solution)/shard_map/ppermute | solution.py:351
  57.1 13.1 %collective-permute-start.12 = (bf16[2,2,1,128,256]{4,3,2,1,0:T(8,128)(2,1)}, bf16[2,2,1,128,256]{4,3,2,1,0:T(8,128)(2,1)}, u32[]{:S(2)}, u32[]{:S(2)}) collective-permute-start(bf16[2,2,1,128,256]{4,3,2,1,0:T(8,128)(2,1)} %get-tuple-element.64), channel_id=1, source_target_pairs={{0,24},{8,0},{16,8},{24,16},{1,25},{9,1},{17,9},{25,17},{2,26},{10... | collective-permute-start | bytes 786440 | tf_op jit(solution)/shard_map/ppermute | solution.py:351
  105.0 75.5 %copy-start = (bf16[3,256,256]{2,1,0:T(8,128)(2,1)S(1)}, bf16[3,256,256]{2,1,0:T(8,128)(2,1)}, u32[]{:S(2)}) copy-start(bf16[3,256,256]{2,1,0:T(8,128)(2,1)} %wt_ref.3) | copy-start | bytes 1179652
  105.0 75.5 %copy-start.1 = (bf16[256,256]{1,0:T(8,128)(2,1)S(1)}, bf16[256,256]{1,0:T(8,128)(2,1)}, u32[]{:S(2)}) copy-start(bf16[256,256]{1,0:T(8,128)(2,1)} %ws_ref.3) | copy-start | bytes 393220
  106.1 5.2 %collective-permute-start.15 = (f32[384,256]{1,0:T(8,128)S(1)}, f32[384,256]{1,0:T(8,128)S(1)}, u32[]{:S(2)}, u32[]{:S(2)}) collective-permute-start(f32[384,256]{1,0:T(8,128)S(1)} %constant_dynamic-slice_fusion), channel_id=1, source_target_pairs={{0,32},{32,0},{1,33},{33,1},{2,34},{34,2},{3,35},{35,3},{4,36},{36... | collective-permute-start | bytes 1179656 | tf_op jit(solution)/shard_map/ppermute | solution.py:327
  175.5 4.9 %collective-permute-start.16 = (f32[384,256]{1,0:T(8,128)S(1)}, f32[384,256]{1,0:T(8,128)S(1)}, u32[]{:S(2)}, u32[]{:S(2)}) collective-permute-start(f32[384,256]{1,0:T(8,128)S(1)} %slice_bitcast_fusion), channel_id=1, source_target_pairs={{0,32},{32,0},{1,33},{33,1},{2,34},{34,2},{3,35},{35,3},{4,36},{36... | collective-permute-start | bytes 1179656 | tf_op jit(solution)/shard_map/ppermute | solution.py:333

commit v5 on v4

--- a/solution.py
+++ b/solution.py
@@ -116,7 +116,8 @@
                 for i, x in enumerate(xs)
             ]
         if edge:
-            xlo, xhi, clo, chi = (ref.at[f] for ref in halo[2:])
+            xlo, xhi = (ref.at[first + f] for ref in halo[2:4])
+            clo, chi = (ref.at[f] for ref in halo[4:])
             moves += [
                 (xlo, ext.at[f, 0:1, 1 : ny + 1]),
                 (xhi, ext.at[f, nx + 1 : nx + 2, 1 : ny + 1]),
@@ -200,41 +201,45 @@
     return [piece.reshape(frames, -1, width) for piece in out]
 
 
-def mix_kernel(half, places, *refs):
-    p_hbm, q_hbm, feat_hbm, cot_hbm, v_hbm, *given = refs[:-9]
-    up_hbm, g_ref, p_ref, q_ref, feat_ref, cot_ref, v_ref, up_ref, sems = refs[-9:]
-    rows, count = MIX_ROWS, len(places)
+def mix_kernel(half, chunks, sizes, final, *refs):
+    n_prev, n_now = sizes
+    prevs, nows = refs[:n_prev], refs[n_prev : n_prev + n_now]
+    feat_hbm, cot_hbm, v_hbm, *refs = refs[n_prev + n_now :]
+    *refs, p_ref, q_ref, feat_ref, cot_ref, v_ref, up_ref, g_ref, given_ref, sems = refs
+    given = refs[0] if half == 0 else None
+    up_hbm, outs = refs[-2 - final], refs[-1 - final :]
+    rows, count = MIX_ROWS, len(chunks)
     pair = slice(2 * half, 2 * half + 2)
-    loads = [[pltpu.make_async_copy(v_hbm, v_ref, sems.at[0])]]
-    for c, place in enumerate(places):
+    first = pltpu.make_async_copy(v_hbm, v_ref, sems.at[0])
+    last = pltpu.make_async_copy(given, given_ref, sems.at[1]) if given is not None else None
+    loads, stores = [], []
+    for c, (p, p_row, q, q_row, place) in enumerate(chunks):
         here, there = slice(c * rows, (c + 1) * rows), slice(place, place + rows)
-        loads += [
+        moves = (
+            (nows[q].at[:, q_row : q_row + rows], q_ref),
+            (prevs[p].at[:, p_row : p_row + rows], p_ref),
+            (feat_hbm.at[pair, there], feat_ref),
+            (cot_hbm.at[pair, there], cot_ref),
+        )
+        loads.append(
             [
-                pltpu.make_async_copy(src, dst.at[:, here], sems.at[1 + 4 * c + i])
-                for i, (src, dst) in enumerate(
-                    (
-                        (q_hbm.at[:, here], q_ref),
-                        (p_hbm.at[:, here], p_ref),
-                        (feat_hbm.at[pair, there], feat_ref),
-                        (cot_hbm.at[pair, there], cot_ref),
-                    )
-                )
+                pltpu.make_async_copy(src, dst.at[:, here], sems.at[2 + 5 * c + i])
+                for i, (src, dst) in enumerate(moves)
             ]
-        ]
-    stores = [
-        pltpu.make_async_copy(
-            up_ref.at[:, c * rows : (c + 1) * rows],
-            up_hbm.at[pair, place : place + rows],
-            sems.at[1 + 4 * count + c],
-        )
-        for c, place in enumerate(places)
-    ]
+        )
+        stores.append(
+            pltpu.make_async_copy(
+                up_ref.at[:, here], up_hbm.at[pair, there], sems.at[2 + 5 * c + 4]
+            )
+        )
+    first.start()
     for copy in sum(loads, []):
         copy.start()
-    loads[0][0].wait()
-    g_ref[...] = given[0][...] if given else jnp.zeros_like(g_ref)
+    if last is not None:
+        last.start()
+    first.wait()
     for c in range(count):
-        for copy in loads[c + 1]:
+        for copy in loads[c]:
             copy.wait()
         here = slice(c * rows, (c + 1) * rows)
         before = [p_ref[0, here], p_ref[1, here], q_ref[0, here], q_ref[1, here]]
@@ -249,39 +254,69 @@
             lefts.append(left)
             grads.append(grad.astype(BF16))
         stores[c].start()
-        g_ref[...] += lax.dot_general(
+        terms = lax.dot_general(
             jnp.concatenate(lefts, axis=0),
             jnp.concatenate(grads, axis=0),
             (((0,), (0,)), ((), ())),
             preferred_element_type=F32,
         )
+        g_ref[...] = terms if c == 0 else g_ref[...] + terms
+    if last is not None:
+        last.wait()
+    if final:
+        me = refs[1][0]
+        share = g_ref.shape[0] // 2
+        low, high = slice(0, share), slice(share, 2 * share)
+        for core, (mine, theirs) in enumerate(((low, high), (high, low))):
+
+            @pl.when(me == core)
+            def _(mine=mine, theirs=theirs):
+                outs[0][...] = g_ref[mine] + given_ref[mine]
+                outs[1][...] = g_ref[theirs] + given_ref[theirs]
+
+    else:
+        outs[0][...] = g_ref[...] + given_ref[...] if last is not None else g_ref[...]
     for copy in stores:
         copy.wait()
 
 
-def mix(half, places, prev, now, features, cotangent, v, given=(), vmem=None):
-    frames, count, width = now.shape
+def mix(half, chunks, prevs, nows, features, cotangent, v, given=None, me=None):
+    frames, width = 2, v.shape[1]
     anywhere = pl.BlockSpec(memory_space=pl.ANY)
-    block = pltpu.VMEM(now.shape, BF16)
+    block = pltpu.VMEM((frames, len(chunks) * MIX_ROWS, width), BF16)
+    sums = jax.ShapeDtypeStruct(v.shape, F32)
+    share = jax.ShapeDtypeStruct((v.shape[0] // 2, width), F32)
+    arrays = [*prevs, *nows, features, cotangent, v]
+    specs = [anywhere] * len(arrays)
+    aliases = {}
+    if given is not None:
+        final = 1 if me is not None else 0
+        total, updated = given
+        core = me if final else jnp.zeros((1,), jnp.int32)
+        arrays += [total, core, updated]
+        aliases = {len(arrays) - 1: 0}
+        specs += [anywhere, pl.BlockSpec(memory_space=pltpu.SMEM), anywhere]
+    else:
+        final = 0
     return pl.pallas_call(
-        functools.partial(mix_kernel, half, places),
-        in_specs=[anywhere] * 5 + ([whole_vmem(), anywhere] if given else []),
-        out_specs=[anywhere, whole_vmem()],
-        out_shape=[
-            jax.ShapeDtypeStruct(features.shape, BF16),
-            jax.ShapeDtypeStruct(v.shape, F32),
-        ],
+        functools.partial(mix_kernel, half, chunks, (len(prevs), len(nows)), final),
+        in_specs=specs,
+        out_specs=[anywhere] + [whole_vmem()] * (1 + final),
+        out_shape=[jax.ShapeDtypeStruct(features.shape, BF16)]
+        + ([share, share] if final else [sums]),
         scratch_shapes=[block] * 4
         + [
             pltpu.VMEM(v.shape, BF16),
             block,
-            pltpu.SemaphoreType.DMA((1 + 5 * len(places),)),
-        ],
-        input_output_aliases={6: 0} if given else {},
-        compiler_params=pltpu.CompilerParams(vmem_limit_bytes=vmem or VMEM),
+            pltpu.VMEM(v.shape, F32),
+            pltpu.VMEM(v.shape, F32),
+            pltpu.SemaphoreType.DMA((2 + 5 * len(chunks),)),
+        ],
+        input_output_aliases=aliases,
+        compiler_params=pltpu.CompilerParams(vmem_limit_bytes=VMEM),
         cost_estimate=pl.CostEstimate(flops=1, bytes_accessed=1, transcendentals=0),
         name="mix",
-    )(prev, now, features, cotangent, v, *given)
+    )(*arrays)
 
 
 def finish_kernel(scale, g_ref, ws_ref, wt_ref, space_ref, time_ref):
@@ -317,13 +352,9 @@
     )(total, w_space, w_time)
 
 
-def all_sum(total):
-    rows, width = total.shape
-    half, block = rows // 2, 8
-    count = lax.axis_size(REST)
-    me = lax.axis_index("core")
-    keep = lax.dynamic_slice_in_dim(total, me * half, half, 0)
-    give = lax.dynamic_slice_in_dim(total, (1 - me) * half, half, 0)
+def all_sum(keep, give):
+    half, width = keep.shape
+    block, count = 8, lax.axis_size(REST)
     mine = keep + lax.ppermute(give, "core", ring(2, 1))
     mine = jnp.pad(mine, ((0, count * block - half), (0, 0)))
     mine = lax.all_to_all(mine.reshape(count, block, width), REST, 0, 0, tiled=True)
@@ -331,8 +362,9 @@
     back = lax.all_to_all(spread, REST, 0, 0, tiled=True)
     back = back.reshape(count * block, width)[:half]
     other = lax.ppermute(back, "core", ring(2, 1))
+    first = lax.axis_index("core") == 0
     return jnp.where(
-        me == 0, jnp.concatenate([back, other]), jnp.concatenate([other, back])
+        first, jnp.concatenate([back, other]), jnp.concatenate([other, back])
     )
 
 
@@ -350,68 +382,92 @@
     def exchange(axis, high_edge, low_edge):
         return lax.ppermute(high_edge, axis, up), lax.ppermute(low_edge, axis, down)
 
-    def edges(first, source):
+    def x_edges(source):
+        edge = (frames, 1, ny, lipids, width)
+        moves = [(0, (every, slice(nx - 1, nx)), 0, ()), (0, (every, low), 1, ())]
+        return pack([source], [edge, edge], moves)
+
+    def y_edges(first, source):
+        edge = (2, nx, 1, lipids, width)
         pair = slice(first, first + 2)
-        x_edge, y_edge = (2, 1, ny, lipids, width), (2, nx, 1, lipids, width)
-        return pack(
-            [source],
-            [x_edge, x_edge, y_edge, y_edge],
-            [
-                (0, (pair, slice(nx - 1, nx)), 0, ()),
-                (0, (pair, low), 1, ()),
-                (0, (pair, every, high), 2, ()),
-                (0, (pair, every, low), 3, ()),
-            ],
-        )
-
-    def corners(x_halo):
+        moves = [(0, (pair, every, side), o, ()) for o, side in enumerate((high, low))]
+        return pack([source], [edge, edge], moves)
+
+    def corners(first, x_halo):
         corner = (2, 2, 1, lipids, width)
+        pair = slice(first, first + 2)
         ends = pack(
             x_halo,
             [corner, corner],
             [
-                (i, (every, every, side), o, (every, slice(i, i + 1)))
+                (i, (pair, every, side), o, (every, slice(i, i + 1)))
                 for i in range(2)
                 for o, side in enumerate((high, low))
             ],
         )
         return exchange("gy", *ends)
 
-    edges_b = edges(2, features)
-    x_b = exchange(GX, *edges_b[:2])
-    y_b = exchange("gy", *edges_b[2:])
-    mask, v = prep(adjacency.reshape(nx * ny, -1, lipids, lipids), w_space, w_time)
-    later, _, _ = lax.optimization_barrier((features, edges_b, mask))
-    edges_a = edges(0, later)
-    x_a = exchange(GX, *edges_a[:2])
-    y_a = exchange("gy", *edges_a[2:])
-    c_b = corners(x_b)
+    edges_b = y_edges(2, features)
+    y_b = exchange("gy", *edges_b)
+    later, _ = lax.optimization_barrier((features, edges_b))
+    edges_x = x_edges(later)
+    x_halo = exchange(GX, *edges_x)
+    later, _ = lax.optimization_barrier((features, edges_x))
+    edges_a = y_edges(0, later)
+    y_a = exchange("gy", *edges_a)
+    contacts = adjacency.reshape(nx * ny, -1, lipids, lipids)
+    contacts, _ = lax.optimization_barrier((contacts, edges_x))
+    mask, v = prep(contacts, w_space, w_time)
     (inner_b,) = aggregate(2, inner, codes, features, y_b, mask)
-    prev_inner = lax.ppermute(inner_b, "ta", onward)
-    c_b, _, _, _ = lax.optimization_barrier((c_b, inner_b, x_a, y_a))
-    outer_b = aggregate(2, outer, codes, features, (*y_b, *x_b, *c_b), mask, 2)
-    prev_first = lax.ppermute(outer_b[0], "ta", onward)
-    prev_last = lax.ppermute(outer_b[1], "ta", onward)
-    x_a, y_a, mask_a, _ = lax.optimization_barrier((x_a, y_a, mask, outer_b))
-    c_a = corners(x_a)
-    (inner_a,) = aggregate(0, inner, codes, features, y_a, mask_a)
-    outer_a = aggregate(0, outer, codes, features, (*y_a, *x_a, *c_a), mask_a, 2)
+    x_halo, y_a, sent = lax.optimization_barrier((x_halo, y_a, inner_b))
+    prev_inner = lax.ppermute(sent, "ta", onward)
+    c_b = corners(2, x_halo)
+    c_a = corners(0, x_halo)
+    outer_b = aggregate(2, outer, codes, features, (*y_b, *x_halo, *c_b), mask, 2)
+    c_a, sent = lax.optimization_barrier((c_a, outer_b))
+    prev_first = lax.ppermute(sent[0], "ta", onward)
+    prev_last = lax.ppermute(sent[1], "ta", onward)
+    every_x = tuple(range(nx))
+    (agg_a,) = aggregate(0, every_x, codes, features, (*y_a, *x_halo, *c_a), mask)
     feat = features.reshape(frames, count, width)
     cot = cotangent.reshape(frames, count, width)
     a_row = ny * lipids
-    groups = [inner, outer[:1], outer[1:]]
-    chunks = [
-        [x * a_row + r for x in xs for r in range(0, a_row, MIX_ROWS)] for xs in groups
-    ]
-    now_b, now_a = (inner_b, *outer_b), (inner_a, *outer_a)
-    state = ()
-    for chunk, prev, now in zip(chunks, now_a, now_b):
-        updated, total = mix(1, chunk, prev, now, feat, cot, v, state)
-        state = (total, updated)
-    for chunk, prev, now in zip(chunks, (prev_inner, prev_first, prev_last), now_a):
-        updated, total = mix(0, chunk, prev, now, feat, cot, v, state)
-        state = (total, updated)
-    total = all_sum(total)
+    end = count - a_row
+    updated, total = mix(
+        1,
+        [(0, r, 0, r - a_row, r) for r in range(a_row, end, MIX_ROWS)]
+        + [(0, r, 1, r, r) for r in range(0, a_row, MIX_ROWS)]
+        + [(0, r, 2, r - end, r) for r in range(end, count, MIX_ROWS)],
+        [agg_a],
+        [inner_b, *outer_b],
+        feat,
+        cot,
+        v,
+    )
+    updated, total = mix(
+        0,
+        [(0, r - a_row, 0, r, r) for r in range(a_row, end, MIX_ROWS)]
+        + [(1, r, 0, r, r) for r in range(0, a_row, MIX_ROWS)],
+        [prev_inner, prev_first],
+        [agg_a],
+        feat,
+        cot,
+        v,
+        (total, updated),
+    )
+    me = lax.axis_index("core").reshape(1)
+    updated, keep, give = mix(
+        0,
+        [(0, r - end, 0, r, r) for r in range(end, count, MIX_ROWS)],
+        [prev_last],
+        [agg_a],
+        feat,
+        cot,
+        v,
+        (total, updated),
+        me,
+    )
+    total = all_sum(keep, give)
     scale = 1.0 / math.sqrt(frames * count * lax.axis_size(EVERY))
     grad_space, grad_time = finish(scale, total, w_space, w_time)
     return updated.reshape(features.shape), grad_space, grad_time

time: 183 us -> 140 us (0.77)
  blocking collectives: 63 us -> 35.9 us
  Pallas kernels: 70.2 us -> 54.1 us
  waiting for transfers between devices: 7.47 us -> 14.5 us
  starting transfers between devices: 37.4 us -> 31.9 us
    all_to_all x1, blocking collectives: 47.4 us -> 20.3 us  [all_sum(): lax.all_to_all(mine.reshape(count, block, width), REST, 0, 0, tiled=True)]
    pallas_call x6 -> x3, Pallas kernels: 36.1 us -> 22 us  [mix(): pl.pallas_call(functools.partial(mix_kernel, half, chunks, (len(prevs), l...]
    ppermute x6 -> x5, waiting for transfers between devices: 0.02 us -> 7.07 us  [exchange(): lax.ppermute(low_edge, axis, down)]
    ppermute x6 -> x5, starting transfers between devices: 9.97 us -> 6.29 us  [exchange(): lax.ppermute(low_edge, axis, down)]
    pallas_call x4 -> x3, Pallas kernels: 18 us -> 14.6 us  [aggregate(): pl.pallas_call(functools.partial(agg_kernel, first, xs, edge, pieces), in...]
    pallas_call x4 -> x5, Pallas kernels: 9.72 us -> 11.1 us  [pack(): pl.pallas_call(functools.partial(pack_kernel, moves, len(arrays)), in_spe...]
    ppermute x6 -> x5, starting transfers between devices: 9.99 us -> 8.64 us  [exchange(): lax.ppermute(high_edge, axis, up)]
    ppermute x6 -> x5, waiting for transfers between devices: 4.74 us -> 4.54 us  [exchange(): lax.ppermute(high_edge, axis, up)]
  transfers between devices with their start and end apart: 17 -> 15, of which waited for: 4 -> 9; matrix products, arithmetic and copies ran while one was open for 0% -> 0% of each run, Pallas kernels for 33% -> 33%
where the time goes in v5:
time: 140 us; the launch traced here: 139 us
  Pallas kernels  54.1 us (39%)
  blocking collectives  35.9 us (26%)
  starting transfers between devices  31.9 us (23%)
  waiting for transfers between devices  14.5 us (10%)
    pallas_call x3, Pallas kernels, mix(): pl.pallas_call(functools.partial(mix_kernel, half, chunks, (len(prevs), l...  22 us
    all_to_all x1, blocking collectives, all_sum(): lax.all_to_all(mine.reshape(count, block, width), REST, 0, 0, tiled=True)  20.3 us
    all_to_all x1, blocking collectives, all_sum(): back = lax.all_to_all(spread, REST, 0, 0, tiled=True)  15.6 us
    pallas_call x3, Pallas kernels, aggregate(): pl.pallas_call(functools.partial(agg_kernel, first, xs, edge, pieces), in...  14.6 us
    pallas_call x5, Pallas kernels, pack(): pl.pallas_call(functools.partial(pack_kernel, moves, len(arrays)), in_spe...  11.1 us
    ppermute x5, starting transfers between devices, exchange(): lax.ppermute(high_edge, axis, up)  8.64 us
    ppermute x5, waiting for transfers between devices, exchange(): lax.ppermute(low_edge, axis, down)  7.07 us
    ppermute x5, starting transfers between devices, exchange(): lax.ppermute(low_edge, axis, down)  6.29 us
  transfers between devices with their start and end apart: 15, of which 9 were waited for; matrix products, arithmetic and copies ran while one was open for 0% of the time, Pallas kernels for 33%

profile of v5, /device:TPU:1, one launch (start us, length us, event | category | flops | bytes accessed | tf_op | source)
XLA Modules:
  0.0 139.2 jit_solution(2418967435776702577)
XLA Ops:
  0.6 2.2 %pack.5 = (bf16[2,4,1,128,256]{4,3,2,1,0:T(8,128)(2,1)}, bf16[2,4,1,128,256]{4,3,2,1,0:T(8,128)(2,1)}) custom-call(bf16[4,4,4,128,256]{4,3,2,1,0:T(8,128)(2,1)} %feat.5), custom_call_target="tpu_custom_call" | custom-call | bytes 6291456 | tf_op jit(solution)/shard_map/pack/pallas_call | solution.py:88
  2.8 2.5 %collective-permute-start.4 = (bf16[2,4,1,128,256]{4,3,2,1,0:T(8,128)(2,1)}, bf16[2,4,1,128,256]{4,3,2,1,0:T(8,128)(2,1)}, u32[]{:S(2)}, u32[]{:S(2)}) collective-permute-start(bf16[2,4,1,128,256]{4,3,2,1,0:T(8,128)(2,1)} %get-tuple-element.38), channel_id=1, source_target_pairs={{0,8},{8,16},{16,24},{24,0},{1,9},{9,17},{17,25},{25,1},{2,10},{10... | collective-permute-start | bytes 1572872 | tf_op jit(solution)/shard_map/ppermute | solution.py:383
  5.4 2.9 %pack.6 = (bf16[4,1,4,128,256]{4,3,2,1,0:T(8,128)(2,1)}, bf16[4,1,4,128,256]{4,3,2,1,0:T(8,128)(2,1)}) custom-call(bf16[4,4,4,128,256]{4,3,2,1,0:T(8,128)(2,1)} %feat.5), custom_call_target="tpu_custom_call" | custom-call | bytes 6291456 | tf_op jit(solution)/shard_map/pack/pallas_call | solution.py:88
  8.3 3.8 %collective-permute-start = (bf16[4,1,4,128,256]{4,3,2,1,0:T(8,128)(2,1)}, bf16[4,1,4,128,256]{4,3,2,1,0:T(8,128)(2,1)}, u32[]{:S(2)}, u32[]{:S(2)}) collective-permute-start(bf16[4,1,4,128,256]{4,3,2,1,0:T(8,128)(2,1)} %get-tuple-element.41), channel_id=1, source_target_pairs={{0,32},{32,64},{64,96},{96,0},{1,33},{33,65},{65,97},{97,1},{2,34}... | collective-permute-start | bytes 3145736 | tf_op jit(solution)/shard_map/ppermute | solution.py:383
  12.1 0.0 collective-permute-start.1
  12.1 1.9 %collective-permute-start.5 = (bf16[2,4,1,128,256]{4,3,2,1,0:T(8,128)(2,1)}, bf16[2,4,1,128,256]{4,3,2,1,0:T(8,128)(2,1)}, u32[]{:S(2)}, u32[]{:S(2)}) collective-permute-start(bf16[2,4,1,128,256]{4,3,2,1,0:T(8,128)(2,1)} %get-tuple-element.39), channel_id=1, source_target_pairs={{0,24},{8,0},{16,8},{24,16},{1,25},{9,1},{17,9},{25,17},{2,26},{10... | collective-permute-start | bytes 1572872 | tf_op jit(solution)/shard_map/ppermute | solution.py:383
  14.0 2.2 %pack.7 = (bf16[2,4,1,128,256]{4,3,2,1,0:T(8,128)(2,1)}, bf16[2,4,1,128,256]{4,3,2,1,0:T(8,128)(2,1)}) custom-call(bf16[4,4,4,128,256]{4,3,2,1,0:T(8,128)(2,1)} %feat.5), custom_call_target="tpu_custom_call" | custom-call | bytes 6291456 | tf_op jit(solution)/shard_map/pack/pallas_call | solution.py:88
  16.2 0.1 collective-permute-start.2
  16.2 3.2 %collective-permute-done.4.rest_0_ = bf16[2,4,1,128,256]{4,3,2,1,0:T(8,128)(2,1)} collective-permute-done((bf16[2,4,1,128,256]{4,3,2,1,0:T(8,128)(2,1)}, bf16[2,4,1,128,256]{4,3,2,1,0:T(8,128)(2,1)}, u32[]{:S(2)}, u32[]{:S(2)}) %collective-permute-start.4) | collective-permute-done | bytes 524320 | tf_op jit(solution)/shard_map/ppermute | solution.py:383
  19.5 1.1 collective-permute-start.3
  20.6 0.7 reshape.42.codes
  21.3 4.8 %prep.1 = (bf16[16,128,512]{2,1,0:T(8,128)(2,1)}, bf16[768,256]{1,0:T(8,128)(2,1)}) custom-call(s32[16,4,128,128]{3,2,1,0:T(8,128)} %bitcast.25, bf16[256,256]{1,0:T(8,128)(2,1)} %ws_ref.3, bf16[3,256,256]{2,1,0:T(8,128)(2,1)} %wt_ref.3), custom_call_target="tpu_custom_call" | custom-call | flops 100663296 | bytes 8388608 | tf_op jit(solution)/shard_map/prep/pallas_call | solution.py:50
  26.0 0.0 collective-permute-done.5.rest_1_
  26.1 4.3 %aggregate.3 = bf16[2,2,4,128,256]{4,3,2,1,0:T(8,128)(2,1)} custom-call(s32[64]{0:T(128)} %reshape.42.codes, bf16[4,4,4,128,256]{4,3,2,1,0:T(8,128)(2,1)} %feat.5, bf16[2,4,1,128,256]{4,3,2,1,0:T(8,128)(2,1)} %collective-permute-done.4.rest_0_, bf16[2,4,1,128,256]{4,3,2,1,0:T(8,128)(2,1)} %collective-permute-done.5.rest_1_, ...), custom_call_target="tpu_custom_call" | custom-call | flops 536870912 | bytes 8388608 | tf_op jit(solution)/shard_map/aggregate/pallas_call | solution.py:179
  30.4 0.1 collective-permute-done.2.rest_0_
  30.5 6.6 %collective-permute-done.3.rest_1_ = bf16[2,4,1,128,256]{4,3,2,1,0:T(8,128)(2,1)} collective-permute-done((bf16[2,4,1,128,256]{4,3,2,1,0:T(8,128)(2,1)}, bf16[2,4,1,128,256]{4,3,2,1,0:T(8,128)(2,1)}, u32[]{:S(2)}, u32[]{:S(2)}) %collective-permute-start.3) | collective-permute-done | bytes 524320 | tf_op jit(solution)/shard_map/ppermute | solution.py:383
  37.1 0.0 collective-permute-done.refs_0_.rest_2_
  37.1 3.0 %collective-permute-start.11 = (bf16[2,1024,256]{2,1,0:T(8,128)(2,1)}, bf16[2,1024,256]{2,1,0:T(8,128)(2,1)}, u32[]{:S(2)}, u32[]{:S(2)}) collective-permute-start(bf16[2,1024,256]{2,1,0:T(8,128)(2,1)} %bitcast.23), channel_id=1, source_target_pairs={{0,1},{1,2},{2,3},{3,4},{4,5},{5,6},{6,7},{8,9},{9,10},{10,11},{11... | collective-permute-start | bytes 3145736 | tf_op jit(solution)/shard_map/ppermute | solution.py:423
  40.1 1.9 %pack.9 = (bf16[2,2,1,128,256]{4,3,2,1,0:T(8,128)(2,1)}, bf16[2,2,1,128,256]{4,3,2,1,0:T(8,128)(2,1)}) custom-call(bf16[4,1,4,128,256]{4,3,2,1,0:T(8,128)(2,1)} %collective-permute-done.refs_0_.rest_2_, bf16[4,1,4,128,256]{4,3,2,1,0:T(8,128)(2,1)} %collective-permute-done.1.refs_1_.rest_3_), custom_call_target="tpu_custom_call" | custom-call | bytes 6291456 | tf_op jit(solution)/shard_map/pack/pallas_call | solution.py:88
  42.0 1.7 %collective-permute-start.8 = (bf16[2,2,1,128,256]{4,3,2,1,0:T(8,128)(2,1)}, bf16[2,2,1,128,256]{4,3,2,1,0:T(8,128)(2,1)}, u32[]{:S(2)}, u32[]{:S(2)}) collective-permute-start(bf16[2,2,1,128,256]{4,3,2,1,0:T(8,128)(2,1)} %get-tuple-element.52), channel_id=1, source_target_pairs={{0,8},{8,16},{16,24},{24,0},{1,9},{9,17},{17,25},{25,1},{2,10},{10... | collective-permute-start | bytes 786440 | tf_op jit(solution)/shard_map/ppermute | solution.py:383
  43.7 1.0 collective-permute-start.9
  44.7 1.9 %pack.8 = (bf16[2,2,1,128,256]{4,3,2,1,0:T(8,128)(2,1)}, bf16[2,2,1,128,256]{4,3,2,1,0:T(8,128)(2,1)}) custom-call(bf16[4,1,4,128,256]{4,3,2,1,0:T(8,128)(2,1)} %collective-permute-done.refs_0_.rest_2_, bf16[4,1,4,128,256]{4,3,2,1,0:T(8,128)(2,1)} %collective-permute-done.1.refs_1_.rest_3_), custom_call_target="tpu_custom_call" | custom-call | bytes 6291456 | tf_op jit(solution)/shard_map/pack/pallas_call | solution.py:88
  46.7 0.5 collective-permute-start.6
  47.2 2.3 %collective-permute-start.7 = (bf16[2,2,1,128,256]{4,3,2,1,0:T(8,128)(2,1)}, bf16[2,2,1,128,256]{4,3,2,1,0:T(8,128)(2,1)}, u32[]{:S(2)}, u32[]{:S(2)}) collective-permute-start(bf16[2,2,1,128,256]{4,3,2,1,0:T(8,128)(2,1)} %get-tuple-element.51), channel_id=1, source_target_pairs={{0,24},{8,0},{16,8},{24,16},{1,25},{9,1},{17,9},{25,17},{2,26},{10... | collective-permute-start | bytes 786440 | tf_op jit(solution)/shard_map/ppermute | solution.py:383
  49.4 0.3 collective-permute-done.8.rest_4_
  49.7 0.3 collective-permute-done.9.rest_5_
  50.0 4.7 %aggregate.4 = (bf16[2,1,4,128,256]{4,3,2,1,0:T(8,128)(2,1)}, bf16[2,1,4,128,256]{4,3,2,1,0:T(8,128)(2,1)}) custom-call(s32[64]{0:T(128)} %reshape.42.codes, bf16[4,4,4,128,256]{4,3,2,1,0:T(8,128)(2,1)} %feat.5, bf16[2,4,1,128,256]{4,3,2,1,0:T(8,128)(2,1)} %collective-permute-done.4.rest_0_, bf16[2,4,1,128,256]{4,3,2,1,0:T(8,128)(2,1)} %collective-permute-done.5.rest_1_, ...), custom_call_target="tpu_custom_call" | custom-call | flops 536870912 | bytes 8388608 | tf_op jit(solution)/shard_map/aggregate/pallas_call | solution.py:179
  54.8 0.9 collective-permute-done.6.rest_4_
  55.7 0.2 collective-permute-done.7.rest_5_
  55.8 4.3 %collective-permute-start.12 = (bf16[2,512,256]{2,1,0:T(8,128)(2,1)}, bf16[2,512,256]{2,1,0:T(8,128)(2,1)}, u32[]{:S(2)}, u32[]{:S(2)}) collective-permute-start(bf16[2,512,256]{2,1,0:T(8,128)(2,1)} %bitcast.28), channel_id=1, source_target_pairs={{0,1},{1,2},{2,3},{3,4},{4,5},{5,6},{6,7},{8,9},{9,10},{10,11},{11... | collective-permute-start | bytes 1572872 | tf_op jit(solution)/shard_map/ppermute | solution.py:428
  60.1 2.1 %collective-permute-start.10 = (bf16[2,512,256]{2,1,0:T(8,128)(2,1)}, bf16[2,512,256]{2,1,0:T(8,128)(2,1)}, u32[]{:S(2)}, u32[]{:S(2)}) collective-permute-start(bf16[2,512,256]{2,1,0:T(8,128)(2,1)} %bitcast.26), channel_id=1, source_target_pairs={{0,1},{1,2},{2,3},{3,4},{4,5},{5,6},{6,7},{8,9},{9,10},{10,11},{11... | collective-permute-start | bytes 1572872 | tf_op jit(solution)/shard_map/ppermute | solution.py:429
  62.2 5.6 %aggregate.5 = bf16[2,4,4,128,256]{4,3,2,1,0:T(8,128)(2,1)} custom-call(s32[64]{0:T(128)} %reshape.42.codes, bf16[4,4,4,128,256]{4,3,2,1,0:T(8,128)(2,1)} %feat.5, bf16[2,4,1,128,256]{4,3,2,1,0:T(8,128)(2,1)} %collective-permute-done.2.rest_0_, bf16[2,4,1,128,256]{4,3,2,1,0:T(8,128)(2,1)} %collective-permute-done.3.rest_1_, ...), custom_call_target="tpu_custom_call" | custom-call | flops 1073741824 | bytes 8388608 | tf_op jit(solution)/shard_map/aggregate/pallas_call | solution.py:179
  67.8 9.6 %mix.3 = (bf16[4,2048,256]{2,1,0:T(8,128)(2,1)}, f32[768,256]{1,0:T(8,128)}) custom-call(bf16[2,2048,256]{2,1,0:T(8,128)(2,1)} %bitcast.19, bf16[2,1024,256]{2,1,0:T(8,128)(2,1)} %bitcast.24, bf16[2,512,256]{2,1,0:T(8,128)(2,1)} %bitcast.29, bf16[2,512,256]{2,1,0:T(8,128)(2,1)} %bitcast.27, bf16[4,2048,256]{2,1,0:T(8,128)(2,1)} %bitcast.13, ...), custom_call_target="tpu_custom_call" | custom-call | flops 1 | bytes 1 | tf_op jit(solution)/shard_map/mix/pallas_call | solution.py:301
  77.4 0.0 collective-permute-done.11.refs_0_
  77.4 7.9 %mix.4 = (bf16[4,2048,256]{2,1,0:T(8,128)(2,1)}, f32[768,256]{1,0:T(8,128)}) custom-call(bf16[2,1024,256]{2,1,0:T(8,128)(2,1)} %collective-permute-done.11.refs_0_, bf16[2,512,256]{2,1,0:T(8,128)(2,1)} %collective-permute-done.12.refs_1_, bf16[2,2048,256]{2,1,0:T(8,128)(2,1)} %bitcast.20, ...), custom_call_target="tpu_custom_call", output_to_operand_aliasing={{0}: (8, {})} | custom-call | flops 1 | bytes 1 | tf_op jit(solution)/shard_map/mix/pallas_call | solution.py:301
  85.3 4.5 %mix.5 = (bf16[4,2048,256]{2,1,0:T(8,128)(2,1)}, f32[384,256]{1,0:T(8,128)}, f32[384,256]{1,0:T(8,128)}) custom-call(bf16[2,512,256]{2,1,0:T(8,128)(2,1)} %collective-permute-done.10.refs_0_, bf16[2,2048,256]{2,1,0:T(8,128)(2,1)} %bitcast.21, bf16[4,2048,256]{2,1,0:T(8,128)(2,1)} %bitcast.15, ...), custom_call_target="tpu_custom_call", output_to_operand_aliasing={{0}: (7, {})} | custom-call | flops 1 | bytes 1 | tf_op jit(solution)/shard_map/mix/pallas_call | solution.py:301
  89.8 0.0 copy-start
  89.8 0.0 copy-start.1
  89.9 4.1 %collective-permute-start.13 = (f32[384,256]{1,0:T(8,128)}, f32[384,256]{1,0:T(8,128)S(1)}, u32[]{:S(2)}, u32[]{:S(2)}) collective-permute-start(f32[384,256]{1,0:T(8,128)} %get-tuple-element.70), channel_id=1, source_target_pairs={{0,32},{32,0},{1,33},{33,1},{2,34},{34,2},{3,35},{35,3},{4,36},{36... | collective-permute-start | bytes 1179656 | tf_op jit(solution)/shard_map/ppermute | solution.py:358
  93.9 1.6 %collective-permute-done.13 = f32[384,256]{1,0:T(8,128)S(1)} collective-permute-done((f32[384,256]{1,0:T(8,128)}, f32[384,256]{1,0:T(8,128)S(1)}, u32[]{:S(2)}, u32[]{:S(2)}) %collective-permute-start.13) | collective-permute-done | bytes 393248 | tf_op jit(solution)/shard_map/ppermute | solution.py:358
  95.5 1.0 add.5
  96.6 20.3 %all_to_all.10 = f32[64,8,256]{2,1,0:T(8,128)S(1)} all-to-all(f32[64,8,256]{2,1,0:T(8,128)S(1)} %pad_bitcast_fusion), channel_id=1, replica_groups=mesh['yh'=2,'core'=2,'gy'=4,'ta'=8] {'yh','gy','ta'}, dimensions={0} | all-to-all | bytes 1048576 | tf_op jit(solution)/shard_map/all_to_all | solution.py:360
  116.9 0.1 reduce_sum.9
  117.0 15.6 %all_to_all.11 = f32[64,8,256]{2,1,0:T(8,128)S(1)} all-to-all(f32[64,8,256]{2,1,0:T(8,128)S(1)} %broadcast_in_dim.2), channel_id=1, replica_groups=mesh['yh'=2,'core'=2,'gy'=4,'ta'=8] {'yh','gy','ta'}, dimensions={0} | all-to-all | bytes 1048576 | tf_op jit(solution)/shard_map/all_to_all | solution.py:362
  132.7 3.5 %collective-permute-start.14 = (f32[384,256]{1,0:T(8,128)S(1)}, f32[384,256]{1,0:T(8,128)S(1)}, u32[]{:S(2)}, u32[]{:S(2)}) collective-permute-start(f32[384,256]{1,0:T(8,128)S(1)} %slice_bitcast_fusion), channel_id=1, source_target_pairs={{0,32},{32,0},{1,33},{33,1},{2,34},{34,2},{3,35},{35,3},{4,36},{36... | collective-permute-start | bytes 1179656 | tf_op jit(solution)/shard_map/ppermute | solution.py:364
  136.2 1.3 collective-permute-done.14
  137.5 0.1 maximum_select_fusion.g_ref
  137.6 1.6 %finish.1 = (f32[256,256]{1,0:T(8,128)}, f32[3,256,256]{2,1,0:T(8,128)}) custom-call(f32[768,256]{1,0:T(8,128)S(1)} %maximum_select_fusion.g_ref, bf16[256,256]{1,0:T(8,128)(2,1)S(1)} %copy-done.1, bf16[3,256,256]{2,1,0:T(8,128)(2,1)S(1)} %copy-done), custom_call_target="tpu_custom_call" | custom-call | tf_op jit(solution)/shard_map/finish/pallas_call | solution.py:342
  (10 shorter events, 0.1 us)
Async XLA Ops:
  2.8 16.6 %collective-permute-start.4 = (bf16[2,4,1,128,256]{4,3,2,1,0:T(8,128)(2,1)}, bf16[2,4,1,128,256]{4,3,2,1,0:T(8,128)(2,1)}, u32[]{:S(2)}, u32[]{:S(2)}) collective-permute-start(bf16[2,4,1,128,256]{4,3,2,1,0:T(8,128)(2,1)} %get-tuple-element.38), channel_id=1, source_target_pairs={{0,8},{8,16},{16,24},{24,0},{1,9},{9,17},{17,25},{25,1},{2,10},{10... | collective-permute-start | bytes 1572872 | tf_op jit(solution)/shard_map/ppermute | solution.py:383
  5.4 15.2 %copy-start.2 = (s32[4,4,4]{2,1,0:T(4,128)S(1)}, s32[4,4,4]{2,1,0:T(4,128)}, u32[]{:S(2)}) copy-start(s32[4,4,4]{2,1,0:T(4,128)} %param.7) | copy-start | bytes 772
  8.3 28.8 %collective-permute-start = (bf16[4,1,4,128,256]{4,3,2,1,0:T(8,128)(2,1)}, bf16[4,1,4,128,256]{4,3,2,1,0:T(8,128)(2,1)}, u32[]{:S(2)}, u32[]{:S(2)}) collective-permute-start(bf16[4,1,4,128,256]{4,3,2,1,0:T(8,128)(2,1)} %get-tuple-element.41), channel_id=1, source_target_pairs={{0,32},{32,64},{64,96},{96,0},{1,33},{33,65},{65,97},{97,1},{2,34}... | collective-permute-start | bytes 3145736 | tf_op jit(solution)/shard_map/ppermute | solution.py:383
  12.1 25.0 %collective-permute-start.1 = (bf16[4,1,4,128,256]{4,3,2,1,0:T(8,128)(2,1)}, bf16[4,1,4,128,256]{4,3,2,1,0:T(8,128)(2,1)}, u32[]{:S(2)}, u32[]{:S(2)}) collective-permute-start(bf16[4,1,4,128,256]{4,3,2,1,0:T(8,128)(2,1)} %get-tuple-element.42), channel_id=1, source_target_pairs={{0,96},{32,0},{64,32},{96,64},{1,97},{33,1},{65,33},{97,65},{2,98}... | collective-permute-start | bytes 3145736 | tf_op jit(solution)/shard_map/ppermute | solution.py:383
  12.1 13.9 %collective-permute-start.5 = (bf16[2,4,1,128,256]{4,3,2,1,0:T(8,128)(2,1)}, bf16[2,4,1,128,256]{4,3,2,1,0:T(8,128)(2,1)}, u32[]{:S(2)}, u32[]{:S(2)}) collective-permute-start(bf16[2,4,1,128,256]{4,3,2,1,0:T(8,128)(2,1)} %get-tuple-element.39), channel_id=1, source_target_pairs={{0,24},{8,0},{16,8},{24,16},{1,25},{9,1},{17,9},{25,17},{2,26},{10... | collective-permute-start | bytes 1572872 | tf_op jit(solution)/shard_map/ppermute | solution.py:383
  16.2 14.3 %collective-permute-start.2 = (bf16[2,4,1,128,256]{4,3,2,1,0:T(8,128)(2,1)}, bf16[2,4,1,128,256]{4,3,2,1,0:T(8,128)(2,1)}, u32[]{:S(2)}, u32[]{:S(2)}) collective-permute-start(bf16[2,4,1,128,256]{4,3,2,1,0:T(8,128)(2,1)} %get-tuple-element.44), channel_id=1, source_target_pairs={{0,8},{8,16},{16,24},{24,0},{1,9},{9,17},{17,25},{25,1},{2,10},{10... | collective-permute-start | bytes 1572872 | tf_op jit(solution)/shard_map/ppermute | solution.py:383
  19.5 17.6 %collective-permute-start.3 = (bf16[2,4,1,128,256]{4,3,2,1,0:T(8,128)(2,1)}, bf16[2,4,1,128,256]{4,3,2,1,0:T(8,128)(2,1)}, u32[]{:S(2)}, u32[]{:S(2)}) collective-permute-start(bf16[2,4,1,128,256]{4,3,2,1,0:T(8,128)(2,1)} %get-tuple-element.45), channel_id=1, source_target_pairs={{0,24},{8,0},{16,8},{24,16},{1,25},{9,1},{17,9},{25,17},{2,26},{10... | collective-permute-start | bytes 1572872 | tf_op jit(solution)/shard_map/ppermute | solution.py:383
  37.1 40.3 %collective-permute-start.11 = (bf16[2,1024,256]{2,1,0:T(8,128)(2,1)}, bf16[2,1024,256]{2,1,0:T(8,128)(2,1)}, u32[]{:S(2)}, u32[]{:S(2)}) collective-permute-start(bf16[2,1024,256]{2,1,0:T(8,128)(2,1)} %bitcast.23), channel_id=1, source_target_pairs={{0,1},{1,2},{2,3},{3,4},{4,5},{5,6},{6,7},{8,9},{9,10},{10,11},{11... | collective-permute-start | bytes 3145736 | tf_op jit(solution)/shard_map/ppermute | solution.py:423
  42.0 7.7 %collective-permute-start.8 = (bf16[2,2,1,128,256]{4,3,2,1,0:T(8,128)(2,1)}, bf16[2,2,1,128,256]{4,3,2,1,0:T(8,128)(2,1)}, u32[]{:S(2)}, u32[]{:S(2)}) collective-permute-start(bf16[2,2,1,128,256]{4,3,2,1,0:T(8,128)(2,1)} %get-tuple-element.52), channel_id=1, source_target_pairs={{0,8},{8,16},{16,24},{24,0},{1,9},{9,17},{17,25},{25,1},{2,10},{10... | collective-permute-start | bytes 786440 | tf_op jit(solution)/shard_map/ppermute | solution.py:383
  43.7 6.3 %collective-permute-start.9 = (bf16[2,2,1,128,256]{4,3,2,1,0:T(8,128)(2,1)}, bf16[2,2,1,128,256]{4,3,2,1,0:T(8,128)(2,1)}, u32[]{:S(2)}, u32[]{:S(2)}) collective-permute-start(bf16[2,2,1,128,256]{4,3,2,1,0:T(8,128)(2,1)} %get-tuple-element.53), channel_id=1, source_target_pairs={{0,24},{8,0},{16,8},{24,16},{1,25},{9,1},{17,9},{25,17},{2,26},{10... | collective-permute-start | bytes 786440 | tf_op jit(solution)/shard_map/ppermute | solution.py:383
  46.7 9.0 %collective-permute-start.6 = (bf16[2,2,1,128,256]{4,3,2,1,0:T(8,128)(2,1)}, bf16[2,2,1,128,256]{4,3,2,1,0:T(8,128)(2,1)}, u32[]{:S(2)}, u32[]{:S(2)}) collective-permute-start(bf16[2,2,1,128,256]{4,3,2,1,0:T(8,128)(2,1)} %get-tuple-element.50), channel_id=1, source_target_pairs={{0,8},{8,16},{16,24},{24,0},{1,9},{9,17},{17,25},{25,1},{2,10},{10... | collective-permute-start | bytes 786440 | tf_op jit(solution)/shard_map/ppermute | solution.py:383
  47.2 8.7 %collective-permute-start.7 = (bf16[2,2,1,128,256]{4,3,2,1,0:T(8,128)(2,1)}, bf16[2,2,1,128,256]{4,3,2,1,0:T(8,128)(2,1)}, u32[]{:S(2)}, u32[]{:S(2)}) collective-permute-start(bf16[2,2,1,128,256]{4,3,2,1,0:T(8,128)(2,1)} %get-tuple-element.51), channel_id=1, source_target_pairs={{0,24},{8,0},{16,8},{24,16},{1,25},{9,1},{17,9},{25,17},{2,26},{10... | collective-permute-start | bytes 786440 | tf_op jit(solution)/shard_map/ppermute | solution.py:383
  55.8 21.5 %collective-permute-start.12 = (bf16[2,512,256]{2,1,0:T(8,128)(2,1)}, bf16[2,512,256]{2,1,0:T(8,128)(2,1)}, u32[]{:S(2)}, u32[]{:S(2)}) collective-permute-start(bf16[2,512,256]{2,1,0:T(8,128)(2,1)} %bitcast.28), channel_id=1, source_target_pairs={{0,1},{1,2},{2,3},{3,4},{4,5},{5,6},{6,7},{8,9},{9,10},{10,11},{11... | collective-permute-start | bytes 1572872 | tf_op jit(solution)/shard_map/ppermute | solution.py:428
  60.1 25.2 %collective-permute-start.10 = (bf16[2,512,256]{2,1,0:T(8,128)(2,1)}, bf16[2,512,256]{2,1,0:T(8,128)(2,1)}, u32[]{:S(2)}, u32[]{:S(2)}) collective-permute-start(bf16[2,512,256]{2,1,0:T(8,128)(2,1)} %bitcast.26), channel_id=1, source_target_pairs={{0,1},{1,2},{2,3},{3,4},{4,5},{5,6},{6,7},{8,9},{9,10},{10,11},{11... | collective-permute-start | bytes 1572872 | tf_op jit(solution)/shard_map/ppermute | solution.py:429
  89.8 47.8 %copy-start = (bf16[3,256,256]{2,1,0:T(8,128)(2,1)S(1)}, bf16[3,256,256]{2,1,0:T(8,128)(2,1)}, u32[]{:S(2)}) copy-start(bf16[3,256,256]{2,1,0:T(8,128)(2,1)} %wt_ref.3) | copy-start | bytes 1179652
  89.8 47.8 %copy-start.1 = (bf16[256,256]{1,0:T(8,128)(2,1)S(1)}, bf16[256,256]{1,0:T(8,128)(2,1)}, u32[]{:S(2)}) copy-start(bf16[256,256]{1,0:T(8,128)(2,1)} %ws_ref.3) | copy-start | bytes 393220
  89.9 5.6 %collective-permute-start.13 = (f32[384,256]{1,0:T(8,128)}, f32[384,256]{1,0:T(8,128)S(1)}, u32[]{:S(2)}, u32[]{:S(2)}) collective-permute-start(f32[384,256]{1,0:T(8,128)} %get-tuple-element.70), channel_id=1, source_target_pairs={{0,32},{32,0},{1,33},{33,1},{2,34},{34,2},{3,35},{35,3},{4,36},{36... | collective-permute-start | bytes 1179656 | tf_op jit(solution)/shard_map/ppermute | solution.py:358
  132.7 4.9 %collective-permute-start.14 = (f32[384,256]{1,0:T(8,128)S(1)}, f32[384,256]{1,0:T(8,128)S(1)}, u32[]{:S(2)}, u32[]{:S(2)}) collective-permute-start(f32[384,256]{1,0:T(8,128)S(1)} %slice_bitcast_fusion), channel_id=1, source_target_pairs={{0,32},{32,0},{1,33},{33,1},{2,34},{34,2},{3,35},{35,3},{4,36},{36... | collective-permute-start | bytes 1179656 | tf_op jit(solution)/shard_map/ppermute | solution.py:364

commit v6 on v5

--- a/solution.py
+++ b/solution.py
@@ -201,6 +201,26 @@
     return [piece.reshape(frames, -1, width) for piece in out]
 
 
+def chunk_terms(before, features, cotangents, v_ref):
+    lefts, grads, updates = [], [], []
+    for f in range(2):
+        left = jnp.concatenate([before[f + 2], before[f + 1], before[f]], axis=1)
+        mixed = jnp.dot(left, v_ref[...], preferred_element_type=F32)
+        s = 0.5 * jnp.tanh(0.5 * mixed) + 0.5
+        silu = mixed * s
+        updates.append((features[f].astype(F32) + silu).astype(BF16))
+        grad = cotangents[f].astype(F32) * (s + silu * (1.0 - s))
+        lefts.append(left)
+        grads.append(grad.astype(BF16))
+    terms = lax.dot_general(
+        jnp.concatenate(lefts, axis=0),
+        jnp.concatenate(grads, axis=0),
+        (((0,), (0,)), ((), ())),
+        preferred_element_type=F32,
+    )
+    return updates, terms
+
+
 def mix_kernel(half, chunks, sizes, final, *refs):
     n_prev, n_now = sizes
     prevs, nows = refs[:n_prev], refs[n_prev : n_prev + n_now]
@@ -243,23 +263,15 @@
             copy.wait()
         here = slice(c * rows, (c + 1) * rows)
         before = [p_ref[0, here], p_ref[1, here], q_ref[0, here], q_ref[1, here]]
-        lefts, grads = [], []
+        updates, terms = chunk_terms(
+            before,
+            [feat_ref[f, here] for f in range(2)],
+            [cot_ref[f, here] for f in range(2)],
+            v_ref,
+        )
         for f in range(2):
-            left = jnp.concatenate([before[f + 2], before[f + 1], before[f]], axis=1)
-            mixed = jnp.dot(left, v_ref[...], preferred_element_type=F32)
-            s = 0.5 * jnp.tanh(0.5 * mixed) + 0.5
-            silu = mixed * s
-            up_ref[f, here] = (feat_ref[f, here].astype(F32) + silu).astype(BF16)
-            grad = cot_ref[f, here].astype(F32) * (s + silu * (1.0 - s))
-            lefts.append(left)
-            grads.append(grad.astype(BF16))
+            up_ref[f, here] = updates[f]
         stores[c].start()
-        terms = lax.dot_general(
-            jnp.concatenate(lefts, axis=0),
-            jnp.concatenate(grads, axis=0),
-            (((0,), (0,)), ((), ())),
-            preferred_element_type=F32,
-        )
         g_ref[...] = terms if c == 0 else g_ref[...] + terms
     if last is not None:
         last.wait()
@@ -319,6 +331,150 @@
     )(*arrays)
 
 
+def middle_kernel(row, codes, feat, *refs):
+    ins, scratch = refs[:16], refs[16:]
+    halo, mask_hbm, nows = ins[:6], ins[6], ins[7:10]
+    prev_hbm, flat_hbm, cot_hbm, v_hbm, agg_hbm, up_hbm = ins[10:]
+    g_out, ext, mask_ref, agg_ref, q_ref, p_ref, feat_ref, cot_ref, up_ref, v_ref, sems = scratch
+    _, nx, ny, lipids, _ = feat.shape
+    count, rows = nx * ny * lipids, MIX_ROWS
+    end = count - row
+    used = [0]
+
+    def copy(src, dst):
+        used[0] += 1
+        return pltpu.make_async_copy(src, dst, sems.at[used[0] - 1])
+
+    groups = []
+    for f in range(2):
+        moves = [
+            copy(feat.at[f], ext.at[f, 1 : nx + 1, 1 : ny + 1]),
+            copy(halo[0].at[f], ext.at[f, 1 : nx + 1, 0:1]),
+            copy(halo[1].at[f], ext.at[f, 1 : nx + 1, ny + 1 : ny + 2]),
+            copy(halo[2].at[f], ext.at[f, 0:1, 1 : ny + 1]),
+            copy(halo[3].at[f], ext.at[f, nx + 1 : nx + 2, 1 : ny + 1]),
+            copy(halo[4].at[f, 0:1], ext.at[f, 0:1, 0:1]),
+            copy(halo[4].at[f, 1:2], ext.at[f, nx + 1 : nx + 2, 0:1]),
+            copy(halo[5].at[f, 0:1], ext.at[f, 0:1, ny + 1 : ny + 2]),
+            copy(halo[5].at[f, 1:2], ext.at[f, nx + 1 : nx + 2, ny + 1 : ny + 2]),
+        ]
+        groups.append(moves + ([copy(mask_hbm, mask_ref)] if f == 0 else []))
+    load_v = copy(v_hbm, v_ref)
+    work, slot = [], 0
+    for half, first, last in ((1, 0, count), (0, row, end)):
+        pair = slice(2 * half, 2 * half + 2)
+        for r in range(first, last, rows):
+            there, here = slice(r, r + rows), slice(slot, slot + rows)
+            slot += rows
+            if half:
+                n, at = (1, r) if r < row else ((0, r - row) if r < end else (2, r - end))
+                moves = [copy(nows[n].at[:, at : at + rows], q_ref.at[:, there])]
+            else:
+                at = slice(r - row, r - row + rows)
+                moves = [copy(prev_hbm.at[:, at], p_ref.at[:, at])]
+            moves += [
+                copy(flat_hbm.at[pair, there], feat_ref.at[:, here]),
+                copy(cot_hbm.at[pair, there], cot_ref.at[:, here]),
+            ]
+            store = copy(up_ref.at[:, here], up_hbm.at[pair, there])
+            work.append((half, r, here, moves, store))
+    sent = [copy(agg_ref.at[f], agg_hbm.at[f]) for f in range(2)]
+    for moves in groups:
+        for move in moves:
+            move.start()
+    load_v.start()
+    for item in work:
+        for move in item[3]:
+            move.start()
+    slots = mask_ref.shape[2] // lipids
+    for f in range(2):
+        for move in groups[f]:
+            move.wait()
+        for x in range(nx):
+            for y in range(ny):
+                tile = x * ny + y
+                parts = []
+                for k in range(slots):
+                    code = codes[tile * slots + k]
+                    parts.append(ext[f, x + lax.div(code, 3), y + lax.rem(code, 3)])
+                summed = jnp.dot(
+                    mask_ref[tile],
+                    jnp.concatenate(parts, axis=0),
+                    preferred_element_type=F32,
+                )
+                agg_ref[f, tile * lipids : (tile + 1) * lipids] = (0.18 * summed).astype(BF16)
+        sent[f].start()
+    load_v.wait()
+    for n, (half, r, here, moves, store) in enumerate(work):
+        for move in moves:
+            move.wait()
+        there = slice(r, r + rows)
+        mid = [agg_ref[0, there], agg_ref[1, there]]
+        if half:
+            before = mid + [q_ref[0, there], q_ref[1, there]]
+        else:
+            at = slice(r - row, r - row + rows)
+            before = [p_ref[0, at], p_ref[1, at]] + mid
+        updates, terms = chunk_terms(
+            before,
+            [feat_ref[f, here] for f in range(2)],
+            [cot_ref[f, here] for f in range(2)],
+            v_ref,
+        )
+        for f in range(2):
+            up_ref[f, here] = updates[f]
+        store.start()
+        g_out[...] = terms if n == 0 else g_out[...] + terms
+    for move in sent:
+        move.wait()
+    for item in work:
+        item[4].wait()
+
+
+def middle(row, codes, features, halo, mask, nows, prev, cotangent, v):
+    frames, nx, ny, lipids, width = features.shape
+    count = nx * ny * lipids
+    flat = (frames, count, width)
+    anywhere = pl.BlockSpec(memory_space=pl.ANY)
+    some = 2 * count - 2 * row
+    chunks = some // MIX_ROWS
+    return pl.pallas_call(
+        functools.partial(middle_kernel, row),
+        in_specs=[pl.BlockSpec(memory_space=pltpu.SMEM)] + [anywhere] * 15,
+        out_specs=[anywhere, anywhere, whole_vmem()],
+        out_shape=[
+            jax.ShapeDtypeStruct((2, count, width), BF16),
+            jax.ShapeDtypeStruct(flat, BF16),
+            jax.ShapeDtypeStruct(v.shape, F32),
+        ],
+        scratch_shapes=[
+            pltpu.VMEM((2, nx + 2, ny + 2, lipids, width), BF16),
+            pltpu.VMEM(mask.shape, BF16),
+            pltpu.VMEM((2, count, width), BF16),
+            pltpu.VMEM((2, count, width), BF16),
+            pltpu.VMEM((2, count - 2 * row, width), BF16),
+            pltpu.VMEM((2, some, width), BF16),
+            pltpu.VMEM((2, some, width), BF16),
+            pltpu.VMEM((2, some, width), BF16),
+            pltpu.VMEM(v.shape, BF16),
+            pltpu.SemaphoreType.DMA((22 + 4 * chunks,)),
+        ],
+        compiler_params=pltpu.CompilerParams(vmem_limit_bytes=VMEM),
+        cost_estimate=pl.CostEstimate(flops=1, bytes_accessed=1, transcendentals=0),
+        name="middle",
+    )(
+        codes,
+        features,
+        *halo,
+        mask,
+        *nows,
+        prev,
+        features.reshape(flat),
+        cotangent,
+        v,
+    )
+
+
 def finish_kernel(scale, g_ref, ws_ref, wt_ref, space_ref, time_ref):
     width = ws_ref.shape[0]
     space = jnp.zeros((width, width), F32)
@@ -393,62 +549,57 @@
         moves = [(0, (pair, every, side), o, ()) for o, side in enumerate((high, low))]
         return pack([source], [edge, edge], moves)
 
-    def corners(first, x_halo):
+    def corner_edges(x_halo):
         corner = (2, 2, 1, lipids, width)
-        pair = slice(first, first + 2)
-        ends = pack(
-            x_halo,
-            [corner, corner],
-            [
-                (i, (pair, every, side), o, (every, slice(i, i + 1)))
-                for i in range(2)
-                for o, side in enumerate((high, low))
-            ],
-        )
-        return exchange("gy", *ends)
-
-    edges_b = y_edges(2, features)
+        moves = [
+            (i, (slice(2 * p, 2 * p + 2), every, side), 2 * p + o, (every, slice(i, i + 1)))
+            for i in range(2)
+            for p in range(2)
+            for o, side in enumerate((high, low))
+        ]
+        return pack(x_halo, [corner] * 4, moves)
+
+    edges_x = x_edges(features)
+    x_halo = exchange(GX, *edges_x)
+    later, _ = lax.optimization_barrier((features, edges_x))
+    edges_b = y_edges(2, later)
     y_b = exchange("gy", *edges_b)
     later, _ = lax.optimization_barrier((features, edges_b))
-    edges_x = x_edges(later)
-    x_halo = exchange(GX, *edges_x)
-    later, _ = lax.optimization_barrier((features, edges_x))
     edges_a = y_edges(0, later)
     y_a = exchange("gy", *edges_a)
     contacts = adjacency.reshape(nx * ny, -1, lipids, lipids)
-    contacts, _ = lax.optimization_barrier((contacts, edges_x))
+    contacts, _ = lax.optimization_barrier((contacts, edges_b))
     mask, v = prep(contacts, w_space, w_time)
     (inner_b,) = aggregate(2, inner, codes, features, y_b, mask)
-    x_halo, y_a, sent = lax.optimization_barrier((x_halo, y_a, inner_b))
+    x_halo, sent = lax.optimization_barrier((x_halo, inner_b))
     prev_inner = lax.ppermute(sent, "ta", onward)
-    c_b = corners(2, x_halo)
-    c_a = corners(0, x_halo)
+    ends = corner_edges(x_halo)
+    c_b = exchange("gy", *ends[2:])
+    c_a = exchange("gy", *ends[:2])
+    c_b, y_a = lax.optimization_barrier((c_b, y_a))
     outer_b = aggregate(2, outer, codes, features, (*y_b, *x_halo, *c_b), mask, 2)
     c_a, sent = lax.optimization_barrier((c_a, outer_b))
     prev_first = lax.ppermute(sent[0], "ta", onward)
     prev_last = lax.ppermute(sent[1], "ta", onward)
-    every_x = tuple(range(nx))
-    (agg_a,) = aggregate(0, every_x, codes, features, (*y_a, *x_halo, *c_a), mask)
     feat = features.reshape(frames, count, width)
     cot = cotangent.reshape(frames, count, width)
     a_row = ny * lipids
     end = count - a_row
-    updated, total = mix(
-        1,
-        [(0, r, 0, r - a_row, r) for r in range(a_row, end, MIX_ROWS)]
-        + [(0, r, 1, r, r) for r in range(0, a_row, MIX_ROWS)]
-        + [(0, r, 2, r - end, r) for r in range(end, count, MIX_ROWS)],
-        [agg_a],
-        [inner_b, *outer_b],
-        feat,
+    agg_a, updated, total = middle(
+        a_row,
+        codes,
+        features,
+        (*y_a, *x_halo, *c_a),
+        mask,
+        (inner_b, *outer_b),
+        prev_inner,
         cot,
         v,
     )
     updated, total = mix(
         0,
-        [(0, r - a_row, 0, r, r) for r in range(a_row, end, MIX_ROWS)]
-        + [(1, r, 0, r, r) for r in range(0, a_row, MIX_ROWS)],
-        [prev_inner, prev_first],
+        [(0, r, 0, r, r) for r in range(0, a_row, MIX_ROWS)],
+        [prev_first],
         [agg_a],
         feat,
         cot,

time: 140 us -> 139 us (level)
  Pallas kernels: 54.1 us -> 50.2 us
  starting transfers between devices: 31.9 us -> 34.4 us
    pallas_call x0 -> x1, Pallas kernels: none -> 16.2 us  [middle(): pl.pallas_call(functools.partial(middle_kernel, row), in_specs=[pl.BlockS...]
    pallas_call x3 -> x2, Pallas kernels: 22 us -> 8.93 us  [mix(): pl.pallas_call(functools.partial(mix_kernel, half, chunks, (len(prevs), l...]
    ppermute x5, waiting for transfers between devices: 7.07 us -> 0.01 us  [exchange(): lax.ppermute(low_edge, axis, down)]
    ppermute x5, waiting for transfers between devices: 4.54 us -> 11.2 us  [exchange(): lax.ppermute(high_edge, axis, up)]
    pallas_call x3 -> x2, Pallas kernels: 14.6 us -> 9.05 us  [aggregate(): pl.pallas_call(functools.partial(agg_kernel, first, xs, edge, pieces), in...]
    ppermute x5, starting transfers between devices: 8.64 us -> 6.52 us  [exchange(): lax.ppermute(high_edge, axis, up)]
    ppermute x5, starting transfers between devices: 6.29 us -> 8.4 us  [exchange(): lax.ppermute(low_edge, axis, down)]
    ppermute x1, starting transfers between devices: 4.09 us -> 6.09 us  [all_sum(): mine = keep + lax.ppermute(give, 'core', ring(2, 1))]
  transfers between devices with their start and end apart: 15 -> 15, of which waited for: 9 -> 4; matrix products, arithmetic and copies ran while one was open for 0% -> 0% of each run, Pallas kernels for 33% -> 30%
where the time goes in v6:
time: 139 us
  Pallas kernels  50.2 us (36%)
  blocking collectives  37 us (27%)
  starting transfers between devices  34.4 us (25%)
  waiting for transfers between devices  14.2 us (10%)
    all_to_all x1, blocking collectives, all_sum(): lax.all_to_all(mine.reshape(count, block, width), REST, 0, 0, tiled=True)  21.3 us
    pallas_call x1, Pallas kernels, middle(): pl.pallas_call(functools.partial(middle_kernel, row), in_specs=[pl.BlockS...  16.2 us
    all_to_all x1, blocking collectives, all_sum(): back = lax.all_to_all(spread, REST, 0, 0, tiled=True)  15.6 us
    ppermute x5, waiting for transfers between devices, exchange(): lax.ppermute(high_edge, axis, up)  11.2 us
    pallas_call x4, Pallas kernels, pack(): pl.pallas_call(functools.partial(pack_kernel, moves, len(arrays)), in_spe...  9.63 us
    pallas_call x2, Pallas kernels, aggregate(): pl.pallas_call(functools.partial(agg_kernel, first, xs, edge, pieces), in...  9.05 us
    pallas_call x2, Pallas kernels, mix(): pl.pallas_call(functools.partial(mix_kernel, half, chunks, (len(prevs), l...  8.93 us
    ppermute x5, starting transfers between devices, exchange(): lax.ppermute(low_edge, axis, down)  8.4 us
  transfers between devices with their start and end apart: 15, of which 4 were waited for; matrix products, arithmetic and copies ran while one was open for 0% of the time, Pallas kernels for 30%

profile of v6, /device:TPU:1, one launch (start us, length us, event | category | flops | bytes accessed | tf_op | source)
XLA Modules:
  0.0 138.5 jit_solution(2209420143486927350)
XLA Ops:
  0.6 2.9 %pack.4 = (bf16[4,1,4,128,256]{4,3,2,1,0:T(8,128)(2,1)}, bf16[4,1,4,128,256]{4,3,2,1,0:T(8,128)(2,1)}) custom-call(bf16[4,4,4,128,256]{4,3,2,1,0:T(8,128)(2,1)} %feat.5), custom_call_target="tpu_custom_call" | custom-call | bytes 6291456 | tf_op jit(solution)/shard_map/pack/pallas_call | solution.py:88
  3.5 4.4 %collective-permute-start = (bf16[4,1,4,128,256]{4,3,2,1,0:T(8,128)(2,1)}, bf16[4,1,4,128,256]{4,3,2,1,0:T(8,128)(2,1)}, u32[]{:S(2)}, u32[]{:S(2)}) collective-permute-start(bf16[4,1,4,128,256]{4,3,2,1,0:T(8,128)(2,1)} %get-tuple-element.41), channel_id=1, source_target_pairs={{0,32},{32,64},{64,96},{96,0},{1,33},{33,65},{65,97},{97,1},{2,34}... | collective-permute-start | bytes 3145736 | tf_op jit(solution)/shard_map/ppermute | solution.py:539
  7.9 0.0 collective-permute-start.1
  7.9 2.2 %pack.5 = (bf16[2,4,1,128,256]{4,3,2,1,0:T(8,128)(2,1)}, bf16[2,4,1,128,256]{4,3,2,1,0:T(8,128)(2,1)}) custom-call(bf16[4,4,4,128,256]{4,3,2,1,0:T(8,128)(2,1)} %feat.5), custom_call_target="tpu_custom_call" | custom-call | bytes 6291456 | tf_op jit(solution)/shard_map/pack/pallas_call | solution.py:88
  10.1 1.7 %collective-permute-start.2 = (bf16[2,4,1,128,256]{4,3,2,1,0:T(8,128)(2,1)}, bf16[2,4,1,128,256]{4,3,2,1,0:T(8,128)(2,1)}, u32[]{:S(2)}, u32[]{:S(2)}) collective-permute-start(bf16[2,4,1,128,256]{4,3,2,1,0:T(8,128)(2,1)} %get-tuple-element.44), channel_id=1, source_target_pairs={{0,8},{8,16},{16,24},{24,0},{1,9},{9,17},{17,25},{25,1},{2,10},{10... | collective-permute-start | bytes 1572872 | tf_op jit(solution)/shard_map/ppermute | solution.py:539
  11.8 2.2 %collective-permute-start.3 = (bf16[2,4,1,128,256]{4,3,2,1,0:T(8,128)(2,1)}, bf16[2,4,1,128,256]{4,3,2,1,0:T(8,128)(2,1)}, u32[]{:S(2)}, u32[]{:S(2)}) collective-permute-start(bf16[2,4,1,128,256]{4,3,2,1,0:T(8,128)(2,1)} %get-tuple-element.45), channel_id=1, source_target_pairs={{0,24},{8,0},{16,8},{24,16},{1,25},{9,1},{17,9},{25,17},{2,26},{10... | collective-permute-start | bytes 1572872 | tf_op jit(solution)/shard_map/ppermute | solution.py:539
  14.0 2.2 %pack.7 = (bf16[2,4,1,128,256]{4,3,2,1,0:T(8,128)(2,1)}, bf16[2,4,1,128,256]{4,3,2,1,0:T(8,128)(2,1)}) custom-call(bf16[4,4,4,128,256]{4,3,2,1,0:T(8,128)(2,1)} %feat.5), custom_call_target="tpu_custom_call" | custom-call | bytes 6291456 | tf_op jit(solution)/shard_map/pack/pallas_call | solution.py:88
  16.2 0.1 collective-permute-start.8
  16.3 9.9 %collective-permute-done.2.rest_0_ = bf16[2,4,1,128,256]{4,3,2,1,0:T(8,128)(2,1)} collective-permute-done((bf16[2,4,1,128,256]{4,3,2,1,0:T(8,128)(2,1)}, bf16[2,4,1,128,256]{4,3,2,1,0:T(8,128)(2,1)}, u32[]{:S(2)}, u32[]{:S(2)}) %collective-permute-start.2) | collective-permute-done | bytes 524320 | tf_op jit(solution)/shard_map/ppermute | solution.py:539
  26.2 1.1 collective-permute-start.9
  27.3 0.7 reshape.40.codes
  28.0 4.8 %prep.1 = (bf16[16,128,512]{2,1,0:T(8,128)(2,1)}, bf16[768,256]{1,0:T(8,128)(2,1)}) custom-call(s32[16,4,128,128]{3,2,1,0:T(8,128)} %bitcast.21, bf16[256,256]{1,0:T(8,128)(2,1)} %ws_ref.3, bf16[3,256,256]{2,1,0:T(8,128)(2,1)} %wt_ref.3), custom_call_target="tpu_custom_call" | custom-call | flops 100663296 | bytes 8388608 | tf_op jit(solution)/shard_map/prep/pallas_call | solution.py:50
  32.8 0.0 collective-permute-done.3.rest_1_
  32.8 4.3 %aggregate.2 = bf16[2,2,4,128,256]{4,3,2,1,0:T(8,128)(2,1)} custom-call(s32[64]{0:T(128)} %reshape.40.codes, bf16[4,4,4,128,256]{4,3,2,1,0:T(8,128)(2,1)} %feat.5, bf16[2,4,1,128,256]{4,3,2,1,0:T(8,128)(2,1)} %collective-permute-done.2.rest_0_, bf16[2,4,1,128,256]{4,3,2,1,0:T(8,128)(2,1)} %collective-permute-done.3.rest_1_, ...), custom_call_target="tpu_custom_call" | custom-call | flops 536870912 | bytes 8388608 | tf_op jit(solution)/shard_map/aggregate/pallas_call | solution.py:179
  37.1 0.0 collective-permute-done.refs_0_.rest_2_.refs_2_
  37.2 0.0 collective-permute-done.1.refs_1_.rest_3_.refs_3_
  37.2 2.4 %collective-permute-start.11 = (bf16[2,1024,256]{2,1,0:T(8,128)(2,1)}, bf16[2,1024,256]{2,1,0:T(8,128)(2,1)}, u32[]{:S(2)}, u32[]{:S(2)}) collective-permute-start(bf16[2,1024,256]{2,1,0:T(8,128)(2,1)} %bitcast.19), channel_id=1, source_target_pairs={{0,1},{1,2},{2,3},{3,4},{4,5},{5,6},{6,7},{8,9},{9,10},{10,11},{11... | collective-permute-start | bytes 3145736 | tf_op jit(solution)/shard_map/ppermute | solution.py:575
  39.6 2.3 %pack.6 = (bf16[2,2,1,128,256]{4,3,2,1,0:T(8,128)(2,1)}, bf16[2,2,1,128,256]{4,3,2,1,0:T(8,128)(2,1)}, bf16[2,2,1,128,256]{4,3,2,1,0:T(8,128)(2,1)}, bf16[2,2,1,128,256]{4,3,2,1,0:T(8,128)(2,1)}) custom-call(bf16[4,1,4,128,256]{4,3,2,1,0:T(8,128)(2,1)} %collective-permute-done.refs_0_.rest_2_.refs_2_, ...), custom_call_target="tpu_custom_call" | custom-call | bytes 6291456 | tf_op jit(solution)/shard_map/pack/pallas_call | solution.py:88
  41.9 0.4 collective-permute-start.6
  42.3 2.4 %collective-permute-start.7 = (bf16[2,2,1,128,256]{4,3,2,1,0:T(8,128)(2,1)}, bf16[2,2,1,128,256]{4,3,2,1,0:T(8,128)(2,1)}, u32[]{:S(2)}, u32[]{:S(2)}) collective-permute-start(bf16[2,2,1,128,256]{4,3,2,1,0:T(8,128)(2,1)} %get-tuple-element.53), channel_id=1, source_target_pairs={{0,24},{8,0},{16,8},{24,16},{1,25},{9,1},{17,9},{25,17},{2,26},{10... | collective-permute-start | bytes 786440 | tf_op jit(solution)/shard_map/ppermute | solution.py:539
  44.6 0.0 collective-permute-done.8.refs_0_
  44.6 0.0 collective-permute-start.4
  44.6 0.0 collective-permute-done.9.refs_1_
  44.7 2.7 %collective-permute-start.5 = (bf16[2,2,1,128,256]{4,3,2,1,0:T(8,128)(2,1)}, bf16[2,2,1,128,256]{4,3,2,1,0:T(8,128)(2,1)}, u32[]{:S(2)}, u32[]{:S(2)}) collective-permute-start(bf16[2,2,1,128,256]{4,3,2,1,0:T(8,128)(2,1)} %get-tuple-element.51), channel_id=1, source_target_pairs={{0,24},{8,0},{16,8},{24,16},{1,25},{9,1},{17,9},{25,17},{2,26},{10... | collective-permute-start | bytes 786440 | tf_op jit(solution)/shard_map/ppermute | solution.py:539
  47.3 1.4 %collective-permute-done.6.rest_4_ = bf16[2,2,1,128,256]{4,3,2,1,0:T(8,128)(2,1)} collective-permute-done((bf16[2,2,1,128,256]{4,3,2,1,0:T(8,128)(2,1)}, bf16[2,2,1,128,256]{4,3,2,1,0:T(8,128)(2,1)}, u32[]{:S(2)}, u32[]{:S(2)}) %collective-permute-start.6) | collective-permute-done | bytes 262176 | tf_op jit(solution)/shard_map/ppermute | solution.py:539
  48.7 0.0 collective-permute-done.7.rest_5_
  48.7 4.7 %aggregate.3 = (bf16[2,1,4,128,256]{4,3,2,1,0:T(8,128)(2,1)}, bf16[2,1,4,128,256]{4,3,2,1,0:T(8,128)(2,1)}) custom-call(s32[64]{0:T(128)} %reshape.40.codes, bf16[4,4,4,128,256]{4,3,2,1,0:T(8,128)(2,1)} %feat.5, bf16[2,4,1,128,256]{4,3,2,1,0:T(8,128)(2,1)} %collective-permute-done.2.rest_0_, bf16[2,4,1,128,256]{4,3,2,1,0:T(8,128)(2,1)} %collective-permute-done.3.rest_1_, ...), custom_call_target="tpu_custom_call" | custom-call | flops 536870912 | bytes 8388608 | tf_op jit(solution)/shard_map/aggregate/pallas_call | solution.py:179
  53.5 0.0 collective-permute-done.5.refs_5_
  53.5 5.3 %collective-permute-start.12 = (bf16[2,512,256]{2,1,0:T(8,128)(2,1)}, bf16[2,512,256]{2,1,0:T(8,128)(2,1)}, u32[]{:S(2)}, u32[]{:S(2)}) collective-permute-start(bf16[2,512,256]{2,1,0:T(8,128)(2,1)} %bitcast.24), channel_id=1, source_target_pairs={{0,1},{1,2},{2,3},{3,4},{4,5},{5,6},{6,7},{8,9},{9,10},{10,11},{11... | collective-permute-start | bytes 1572872 | tf_op jit(solution)/shard_map/ppermute | solution.py:582
  58.8 2.1 %collective-permute-start.10 = (bf16[2,512,256]{2,1,0:T(8,128)(2,1)}, bf16[2,512,256]{2,1,0:T(8,128)(2,1)}, u32[]{:S(2)}, u32[]{:S(2)}) collective-permute-start(bf16[2,512,256]{2,1,0:T(8,128)(2,1)} %bitcast.22), channel_id=1, source_target_pairs={{0,1},{1,2},{2,3},{3,4},{4,5},{5,6},{6,7},{8,9},{9,10},{10,11},{11... | collective-permute-start | bytes 1572872 | tf_op jit(solution)/shard_map/ppermute | solution.py:583
  60.9 0.0 collective-permute-done.11.refs_10_
  60.9 16.2 %middle.1 = (bf16[2,2048,256]{2,1,0:T(8,128)(2,1)}, bf16[4,2048,256]{2,1,0:T(8,128)(2,1)}, f32[768,256]{1,0:T(8,128)}) custom-call(s32[64]{0:T(128)} %reshape.40.codes, bf16[4,4,4,128,256]{4,3,2,1,0:T(8,128)(2,1)} %feat.5, bf16[2,4,1,128,256]{4,3,2,1,0:T(8,128)(2,1)} %collective-permute-done.8.refs_0_, ...), custom_call_target="tpu_custom_call" | custom-call | flops 1 | bytes 1 | tf_op jit(solution)/shard_map/middle/pallas_call | solution.py:441
  77.1 0.0 collective-permute-done.12.refs_0_
  77.2 4.5 %mix.2 = (bf16[4,2048,256]{2,1,0:T(8,128)(2,1)}, f32[768,256]{1,0:T(8,128)}) custom-call(bf16[2,512,256]{2,1,0:T(8,128)(2,1)} %collective-permute-done.12.refs_0_, bf16[2,2048,256]{2,1,0:T(8,128)(2,1)} %get-tuple-element.68.refs_1_, bf16[4,2048,256]{2,1,0:T(8,128)(2,1)} %bitcast.13, bf16[4,2048,256]{2,1,0:T(8,128)(2,1)} %bitcast.16, ...), custom_call_target="tpu_custom_call", output_to_operand_aliasing={{0}: (7, {})} | custom-call | flops 1 | bytes 1 | tf_op jit(solution)/shard_map/mix/pallas_call | solution.py:313
  81.6 0.0 collective-permute-done.10.refs_0_
  81.6 4.5 %mix.3 = (bf16[4,2048,256]{2,1,0:T(8,128)(2,1)}, f32[384,256]{1,0:T(8,128)}, f32[384,256]{1,0:T(8,128)}) custom-call(bf16[2,512,256]{2,1,0:T(8,128)(2,1)} %collective-permute-done.10.refs_0_, bf16[2,2048,256]{2,1,0:T(8,128)(2,1)} %get-tuple-element.68.refs_1_, bf16[4,2048,256]{2,1,0:T(8,128)(2,1)} %bitcast.14, ...), custom_call_target="tpu_custom_call", output_to_operand_aliasing={{0}: (7, {})} | custom-call | flops 1 | bytes 1 | tf_op jit(solution)/shard_map/mix/pallas_call | solution.py:313
  86.1 0.0 copy-start
  86.1 0.0 copy-start.1
  86.1 6.1 %collective-permute-start.13 = (f32[384,256]{1,0:T(8,128)}, f32[384,256]{1,0:T(8,128)S(1)}, u32[]{:S(2)}, u32[]{:S(2)}) collective-permute-start(f32[384,256]{1,0:T(8,128)} %get-tuple-element.76), channel_id=1, source_target_pairs={{0,32},{32,0},{1,33},{33,1},{2,34},{34,2},{3,35},{35,3},{4,36},{36... | collective-permute-start | bytes 1179656 | tf_op jit(solution)/shard_map/ppermute | solution.py:514
  92.2 1.6 %collective-permute-done.13 = f32[384,256]{1,0:T(8,128)S(1)} collective-permute-done((f32[384,256]{1,0:T(8,128)}, f32[384,256]{1,0:T(8,128)S(1)}, u32[]{:S(2)}, u32[]{:S(2)}) %collective-permute-start.13) | collective-permute-done | bytes 393248 | tf_op jit(solution)/shard_map/ppermute | solution.py:514
  93.8 1.0 add.5
  94.9 21.3 %all_to_all.10 = f32[64,8,256]{2,1,0:T(8,128)S(1)} all-to-all(f32[64,8,256]{2,1,0:T(8,128)S(1)} %pad_bitcast_fusion), channel_id=1, replica_groups=mesh['yh'=2,'core'=2,'gy'=4,'ta'=8] {'yh','gy','ta'}, dimensions={0} | all-to-all | bytes 1048576 | tf_op jit(solution)/shard_map/all_to_all | solution.py:516
  116.2 0.1 reduce_sum.9
  116.3 15.6 %all_to_all.11 = f32[64,8,256]{2,1,0:T(8,128)S(1)} all-to-all(f32[64,8,256]{2,1,0:T(8,128)S(1)} %broadcast_in_dim.2), channel_id=1, replica_groups=mesh['yh'=2,'core'=2,'gy'=4,'ta'=8] {'yh','gy','ta'}, dimensions={0} | all-to-all | bytes 1048576 | tf_op jit(solution)/shard_map/all_to_all | solution.py:518
  132.0 3.5 %collective-permute-start.14 = (f32[384,256]{1,0:T(8,128)S(1)}, f32[384,256]{1,0:T(8,128)S(1)}, u32[]{:S(2)}, u32[]{:S(2)}) collective-permute-start(f32[384,256]{1,0:T(8,128)S(1)} %slice_bitcast_fusion), channel_id=1, source_target_pairs={{0,32},{32,0},{1,33},{33,1},{2,34},{34,2},{3,35},{35,3},{4,36},{36... | collective-permute-start | bytes 1179656 | tf_op jit(solution)/shard_map/ppermute | solution.py:520
  135.5 1.3 collective-permute-done.14
  136.9 0.1 maximum_select_fusion.g_ref
  137.0 1.6 %finish.1 = (f32[256,256]{1,0:T(8,128)}, f32[3,256,256]{2,1,0:T(8,128)}) custom-call(f32[768,256]{1,0:T(8,128)S(1)} %maximum_select_fusion.g_ref, bf16[256,256]{1,0:T(8,128)(2,1)S(1)} %copy-done.1, bf16[3,256,256]{2,1,0:T(8,128)(2,1)S(1)} %copy-done), custom_call_target="tpu_custom_call" | custom-call | tf_op jit(solution)/shard_map/finish/pallas_call | solution.py:498
  (8 shorter events, 0.1 us)
Async XLA Ops:
  3.5 33.6 %collective-permute-start = (bf16[4,1,4,128,256]{4,3,2,1,0:T(8,128)(2,1)}, bf16[4,1,4,128,256]{4,3,2,1,0:T(8,128)(2,1)}, u32[]{:S(2)}, u32[]{:S(2)}) collective-permute-start(bf16[4,1,4,128,256]{4,3,2,1,0:T(8,128)(2,1)} %get-tuple-element.41), channel_id=1, source_target_pairs={{0,32},{32,64},{64,96},{96,0},{1,33},{33,65},{65,97},{97,1},{2,34}... | collective-permute-start | bytes 3145736 | tf_op jit(solution)/shard_map/ppermute | solution.py:539
  7.9 19.4 %copy-start.2 = (s32[4,4,4]{2,1,0:T(4,128)S(1)}, s32[4,4,4]{2,1,0:T(4,128)}, u32[]{:S(2)}) copy-start(s32[4,4,4]{2,1,0:T(4,128)} %param.7) | copy-start | bytes 772
  7.9 29.2 %collective-permute-start.1 = (bf16[4,1,4,128,256]{4,3,2,1,0:T(8,128)(2,1)}, bf16[4,1,4,128,256]{4,3,2,1,0:T(8,128)(2,1)}, u32[]{:S(2)}, u32[]{:S(2)}) collective-permute-start(bf16[4,1,4,128,256]{4,3,2,1,0:T(8,128)(2,1)} %get-tuple-element.42), channel_id=1, source_target_pairs={{0,96},{32,0},{64,32},{96,64},{1,97},{33,1},{65,33},{97,65},{2,98}... | collective-permute-start | bytes 3145736 | tf_op jit(solution)/shard_map/ppermute | solution.py:539
  10.1 16.0 %collective-permute-start.2 = (bf16[2,4,1,128,256]{4,3,2,1,0:T(8,128)(2,1)}, bf16[2,4,1,128,256]{4,3,2,1,0:T(8,128)(2,1)}, u32[]{:S(2)}, u32[]{:S(2)}) collective-permute-start(bf16[2,4,1,128,256]{4,3,2,1,0:T(8,128)(2,1)} %get-tuple-element.44), channel_id=1, source_target_pairs={{0,8},{8,16},{16,24},{24,0},{1,9},{9,17},{17,25},{25,1},{2,10},{10... | collective-permute-start | bytes 1572872 | tf_op jit(solution)/shard_map/ppermute | solution.py:539
  11.8 21.0 %collective-permute-start.3 = (bf16[2,4,1,128,256]{4,3,2,1,0:T(8,128)(2,1)}, bf16[2,4,1,128,256]{4,3,2,1,0:T(8,128)(2,1)}, u32[]{:S(2)}, u32[]{:S(2)}) collective-permute-start(bf16[2,4,1,128,256]{4,3,2,1,0:T(8,128)(2,1)} %get-tuple-element.45), channel_id=1, source_target_pairs={{0,24},{8,0},{16,8},{24,16},{1,25},{9,1},{17,9},{25,17},{2,26},{10... | collective-permute-start | bytes 1572872 | tf_op jit(solution)/shard_map/ppermute | solution.py:539
  16.2 28.4 %collective-permute-start.8 = (bf16[2,4,1,128,256]{4,3,2,1,0:T(8,128)(2,1)}, bf16[2,4,1,128,256]{4,3,2,1,0:T(8,128)(2,1)}, u32[]{:S(2)}, u32[]{:S(2)}) collective-permute-start(bf16[2,4,1,128,256]{4,3,2,1,0:T(8,128)(2,1)} %get-tuple-element.55), channel_id=1, source_target_pairs={{0,8},{8,16},{16,24},{24,0},{1,9},{9,17},{17,25},{25,1},{2,10},{10... | collective-permute-start | bytes 1572872 | tf_op jit(solution)/shard_map/ppermute | solution.py:539
  26.2 18.5 %collective-permute-start.9 = (bf16[2,4,1,128,256]{4,3,2,1,0:T(8,128)(2,1)}, bf16[2,4,1,128,256]{4,3,2,1,0:T(8,128)(2,1)}, u32[]{:S(2)}, u32[]{:S(2)}) collective-permute-start(bf16[2,4,1,128,256]{4,3,2,1,0:T(8,128)(2,1)} %get-tuple-element.56), channel_id=1, source_target_pairs={{0,24},{8,0},{16,8},{24,16},{1,25},{9,1},{17,9},{25,17},{2,26},{10... | collective-permute-start | bytes 1572872 | tf_op jit(solution)/shard_map/ppermute | solution.py:539
  37.2 23.7 %collective-permute-start.11 = (bf16[2,1024,256]{2,1,0:T(8,128)(2,1)}, bf16[2,1024,256]{2,1,0:T(8,128)(2,1)}, u32[]{:S(2)}, u32[]{:S(2)}) collective-permute-start(bf16[2,1024,256]{2,1,0:T(8,128)(2,1)} %bitcast.19), channel_id=1, source_target_pairs={{0,1},{1,2},{2,3},{3,4},{4,5},{5,6},{6,7},{8,9},{9,10},{10,11},{11... | collective-permute-start | bytes 3145736 | tf_op jit(solution)/shard_map/ppermute | solution.py:575
  41.9 6.8 %collective-permute-start.6 = (bf16[2,2,1,128,256]{4,3,2,1,0:T(8,128)(2,1)}, bf16[2,2,1,128,256]{4,3,2,1,0:T(8,128)(2,1)}, u32[]{:S(2)}, u32[]{:S(2)}) collective-permute-start(bf16[2,2,1,128,256]{4,3,2,1,0:T(8,128)(2,1)} %get-tuple-element.52), channel_id=1, source_target_pairs={{0,8},{8,16},{16,24},{24,0},{1,9},{9,17},{17,25},{25,1},{2,10},{10... | collective-permute-start | bytes 786440 | tf_op jit(solution)/shard_map/ppermute | solution.py:539
  42.3 6.5 %collective-permute-start.7 = (bf16[2,2,1,128,256]{4,3,2,1,0:T(8,128)(2,1)}, bf16[2,2,1,128,256]{4,3,2,1,0:T(8,128)(2,1)}, u32[]{:S(2)}, u32[]{:S(2)}) collective-permute-start(bf16[2,2,1,128,256]{4,3,2,1,0:T(8,128)(2,1)} %get-tuple-element.53), channel_id=1, source_target_pairs={{0,24},{8,0},{16,8},{24,16},{1,25},{9,1},{17,9},{25,17},{2,26},{10... | collective-permute-start | bytes 786440 | tf_op jit(solution)/shard_map/ppermute | solution.py:539
  44.6 8.8 %collective-permute-start.4 = (bf16[2,2,1,128,256]{4,3,2,1,0:T(8,128)(2,1)}, bf16[2,2,1,128,256]{4,3,2,1,0:T(8,128)(2,1)}, u32[]{:S(2)}, u32[]{:S(2)}) collective-permute-start(bf16[2,2,1,128,256]{4,3,2,1,0:T(8,128)(2,1)} %get-tuple-element.50), channel_id=1, source_target_pairs={{0,8},{8,16},{16,24},{24,0},{1,9},{9,17},{17,25},{25,1},{2,10},{10... | collective-permute-start | bytes 786440 | tf_op jit(solution)/shard_map/ppermute | solution.py:539
  44.7 8.8 %collective-permute-start.5 = (bf16[2,2,1,128,256]{4,3,2,1,0:T(8,128)(2,1)}, bf16[2,2,1,128,256]{4,3,2,1,0:T(8,128)(2,1)}, u32[]{:S(2)}, u32[]{:S(2)}) collective-permute-start(bf16[2,2,1,128,256]{4,3,2,1,0:T(8,128)(2,1)} %get-tuple-element.51), channel_id=1, source_target_pairs={{0,24},{8,0},{16,8},{24,16},{1,25},{9,1},{17,9},{25,17},{2,26},{10... | collective-permute-start | bytes 786440 | tf_op jit(solution)/shard_map/ppermute | solution.py:539
  53.5 23.7 %collective-permute-start.12 = (bf16[2,512,256]{2,1,0:T(8,128)(2,1)}, bf16[2,512,256]{2,1,0:T(8,128)(2,1)}, u32[]{:S(2)}, u32[]{:S(2)}) collective-permute-start(bf16[2,512,256]{2,1,0:T(8,128)(2,1)} %bitcast.24), channel_id=1, source_target_pairs={{0,1},{1,2},{2,3},{3,4},{4,5},{5,6},{6,7},{8,9},{9,10},{10,11},{11... | collective-permute-start | bytes 1572872 | tf_op jit(solution)/shard_map/ppermute | solution.py:582
  58.8 22.8 %collective-permute-start.10 = (bf16[2,512,256]{2,1,0:T(8,128)(2,1)}, bf16[2,512,256]{2,1,0:T(8,128)(2,1)}, u32[]{:S(2)}, u32[]{:S(2)}) collective-permute-start(bf16[2,512,256]{2,1,0:T(8,128)(2,1)} %bitcast.22), channel_id=1, source_target_pairs={{0,1},{1,2},{2,3},{3,4},{4,5},{5,6},{6,7},{8,9},{9,10},{10,11},{11... | collective-permute-start | bytes 1572872 | tf_op jit(solution)/shard_map/ppermute | solution.py:583
  86.1 50.8 %copy-start = (bf16[3,256,256]{2,1,0:T(8,128)(2,1)S(1)}, bf16[3,256,256]{2,1,0:T(8,128)(2,1)}, u32[]{:S(2)}) copy-start(bf16[3,256,256]{2,1,0:T(8,128)(2,1)} %wt_ref.3) | copy-start | bytes 1179652
  86.1 50.8 %copy-start.1 = (bf16[256,256]{1,0:T(8,128)(2,1)S(1)}, bf16[256,256]{1,0:T(8,128)(2,1)}, u32[]{:S(2)}) copy-start(bf16[256,256]{1,0:T(8,128)(2,1)} %ws_ref.3) | copy-start | bytes 393220
  86.1 7.7 %collective-permute-start.13 = (f32[384,256]{1,0:T(8,128)}, f32[384,256]{1,0:T(8,128)S(1)}, u32[]{:S(2)}, u32[]{:S(2)}) collective-permute-start(f32[384,256]{1,0:T(8,128)} %get-tuple-element.76), channel_id=1, source_target_pairs={{0,32},{32,0},{1,33},{33,1},{2,34},{34,2},{3,35},{35,3},{4,36},{36... | collective-permute-start | bytes 1179656 | tf_op jit(solution)/shard_map/ppermute | solution.py:514
  132.0 4.9 %collective-permute-start.14 = (f32[384,256]{1,0:T(8,128)S(1)}, f32[384,256]{1,0:T(8,128)S(1)}, u32[]{:S(2)}, u32[]{:S(2)}) collective-permute-start(f32[384,256]{1,0:T(8,128)S(1)} %slice_bitcast_fusion), channel_id=1, source_target_pairs={{0,32},{32,0},{1,33},{33,1},{2,34},{34,2},{3,35},{35,3},{4,36},{36... | collective-permute-start | bytes 1179656 | tf_op jit(solution)/shard_map/ppermute | solution.py:520

commit v7 on v6

--- a/solution.py
+++ b/solution.py
@@ -358,7 +358,11 @@
             copy(halo[5].at[f, 0:1], ext.at[f, 0:1, ny + 1 : ny + 2]),
             copy(halo[5].at[f, 1:2], ext.at[f, nx + 1 : nx + 2, ny + 1 : ny + 2]),
         ]
-        groups.append(moves + ([copy(mask_hbm, mask_ref)] if f == 0 else []))
+        groups.append(moves)
+    masks = [
+        copy(mask_hbm.at[x * ny : (x + 1) * ny], mask_ref.at[x * ny : (x + 1) * ny])
+        for x in range(nx)
+    ]
     load_v = copy(v_hbm, v_ref)
     work, slot = [], 0
     for half, first, last in ((1, 0, count), (0, row, end)):
@@ -372,14 +376,13 @@
             else:
                 at = slice(r - row, r - row + rows)
                 moves = [copy(prev_hbm.at[:, at], p_ref.at[:, at])]
-            moves += [
-                copy(flat_hbm.at[pair, there], feat_ref.at[:, here]),
-                copy(cot_hbm.at[pair, there], cot_ref.at[:, here]),
-            ]
+            moves.append(copy(cot_hbm.at[pair, there], cot_ref.at[:, here]))
+            if half:
+                moves.append(copy(flat_hbm.at[pair, there], feat_ref.at[:, there]))
             store = copy(up_ref.at[:, here], up_hbm.at[pair, there])
             work.append((half, r, here, moves, store))
     sent = [copy(agg_ref.at[f], agg_hbm.at[f]) for f in range(2)]
-    for moves in groups:
+    for moves in (groups[0], masks, groups[1]):
         for move in moves:
             move.start()
     load_v.start()
@@ -391,6 +394,8 @@
         for move in groups[f]:
             move.wait()
         for x in range(nx):
+            if f == 0:
+                masks[x].wait()
             for y in range(ny):
                 tile = x * ny + y
                 parts = []
@@ -412,14 +417,17 @@
         mid = [agg_ref[0, there], agg_ref[1, there]]
         if half:
             before = mid + [q_ref[0, there], q_ref[1, there]]
+            own = [feat_ref[f, there] for f in range(2)]
         else:
+            tiles = [divmod(t // lipids, ny) for t in range(r, r + rows, lipids)]
+            own = [
+                jnp.concatenate([ext[f, x + 1, y + 1] for x, y in tiles], axis=0)
+                for f in range(2)
+            ]
             at = slice(r - row, r - row + rows)
             before = [p_ref[0, at], p_ref[1, at]] + mid
         updates, terms = chunk_terms(
-            before,
-            [feat_ref[f, here] for f in range(2)],
-            [cot_ref[f, here] for f in range(2)],
-            v_ref,
+            before, own, [cot_ref[f, here] for f in range(2)], v_ref
         )
         for f in range(2):
             up_ref[f, here] = updates[f]
@@ -453,11 +461,11 @@
             pltpu.VMEM((2, count, width), BF16),
             pltpu.VMEM((2, count, width), BF16),
             pltpu.VMEM((2, count - 2 * row, width), BF16),
-            pltpu.VMEM((2, some, width), BF16),
+            pltpu.VMEM((2, count, width), BF16),
             pltpu.VMEM((2, some, width), BF16),
             pltpu.VMEM((2, some, width), BF16),
             pltpu.VMEM(v.shape, BF16),
-            pltpu.SemaphoreType.DMA((22 + 4 * chunks,)),
+            pltpu.SemaphoreType.DMA((25 + 4 * chunks,)),
         ],
         compiler_params=pltpu.CompilerParams(vmem_limit_bytes=VMEM),
         cost_estimate=pl.CostEstimate(flops=1, bytes_accessed=1, transcendentals=0),
@@ -564,12 +572,12 @@
     later, _ = lax.optimization_barrier((features, edges_x))
     edges_b = y_edges(2, later)
     y_b = exchange("gy", *edges_b)
-    later, _ = lax.optimization_barrier((features, edges_b))
-    edges_a = y_edges(0, later)
-    y_a = exchange("gy", *edges_a)
     contacts = adjacency.reshape(nx * ny, -1, lipids, lipids)
     contacts, _ = lax.optimization_barrier((contacts, edges_b))
     mask, v = prep(contacts, w_space, w_time)
+    later, _ = lax.optimization_barrier((features, mask))
+    edges_a = y_edges(0, later)
+    y_a = exchange("gy", *edges_a)
     (inner_b,) = aggregate(2, inner, codes, features, y_b, mask)
     x_halo, sent = lax.optimization_barrier((x_halo, inner_b))
     prev_inner = lax.ppermute(sent, "ta", onward)

time: 139 us -> 136 us (0.978)
  waiting for transfers between devices: 14.2 us -> 10.6 us
    ppermute x5, waiting for transfers between devices: 11.2 us -> 7.69 us  [exchange(): lax.ppermute(high_edge, axis, up)]
    ppermute x1, starting transfers between devices: 5.33 us -> 2.38 us  [shards(): prev_first = lax.ppermute(sent[0], 'ta', onward)]
    ppermute x1, starting transfers between devices: 2.39 us -> 3.92 us  [shards(): prev_inner = lax.ppermute(sent, 'ta', onward)]
    ppermute x1, starting transfers between devices: 2.09 us -> 3.58 us  [shards(): prev_last = lax.ppermute(sent[1], 'ta', onward)]
  transfers between devices with their start and end apart: 15 -> 15, of which waited for: 4 -> 5; matrix products, arithmetic and copies ran while one was open for 0% -> 1% of each run, Pallas kernels for 30% -> 30%
where the time goes in v7:
time: 136 us
  Pallas kernels  50.2 us (37%)
  blocking collectives  36.9 us (27%)
  starting transfers between devices  35.1 us (26%)
  waiting for transfers between devices  10.6 us (8%)
    all_to_all x1, blocking collectives, all_sum(): lax.all_to_all(mine.reshape(count, block, width), REST, 0, 0, tiled=True)  21.3 us
    pallas_call x1, Pallas kernels, middle(): pl.pallas_call(functools.partial(middle_kernel, row), in_specs=[pl.BlockS...  16.2 us
    all_to_all x1, blocking collectives, all_sum(): back = lax.all_to_all(spread, REST, 0, 0, tiled=True)  15.6 us
    pallas_call x4, Pallas kernels, pack(): pl.pallas_call(functools.partial(pack_kernel, moves, len(arrays)), in_spe...  9.62 us
    pallas_call x2, Pallas kernels, aggregate(): pl.pallas_call(functools.partial(agg_kernel, first, xs, edge, pieces), in...  9.05 us
    pallas_call x2, Pallas kernels, mix(): pl.pallas_call(functools.partial(mix_kernel, half, chunks, (len(prevs), l...  8.93 us
    ppermute x5, starting transfers between devices, exchange(): lax.ppermute(low_edge, axis, down)  8.52 us
    ppermute x5, waiting for transfers between devices, exchange(): lax.ppermute(high_edge, axis, up)  7.69 us
  transfers between devices with their start and end apart: 15, of which 5 were waited for; matrix products, arithmetic and copies ran while one was open for 1% of the time, Pallas kernels for 30%

profile of v7, /device:TPU:1, one launch (start us, length us, event | category | flops | bytes accessed | tf_op | source)
XLA Modules:
  0.0 135.7 jit_solution(3792006511371353875)
XLA Ops:
  0.6 2.9 %pack.4 = (bf16[4,1,4,128,256]{4,3,2,1,0:T(8,128)(2,1)}, bf16[4,1,4,128,256]{4,3,2,1,0:T(8,128)(2,1)}) custom-call(bf16[4,4,4,128,256]{4,3,2,1,0:T(8,128)(2,1)} %feat.5), custom_call_target="tpu_custom_call" | custom-call | bytes 6291456 | tf_op jit(solution)/shard_map/pack/pallas_call | solution.py:88
  3.5 4.4 %collective-permute-start = (bf16[4,1,4,128,256]{4,3,2,1,0:T(8,128)(2,1)}, bf16[4,1,4,128,256]{4,3,2,1,0:T(8,128)(2,1)}, u32[]{:S(2)}, u32[]{:S(2)}) collective-permute-start(bf16[4,1,4,128,256]{4,3,2,1,0:T(8,128)(2,1)} %get-tuple-element.41), channel_id=1, source_target_pairs={{0,32},{32,64},{64,96},{96,0},{1,33},{33,65},{65,97},{97,1},{2,34}... | collective-permute-start | bytes 3145736 | tf_op jit(solution)/shard_map/ppermute | solution.py:547
  7.9 0.0 collective-permute-start.1
  7.9 2.2 %pack.5 = (bf16[2,4,1,128,256]{4,3,2,1,0:T(8,128)(2,1)}, bf16[2,4,1,128,256]{4,3,2,1,0:T(8,128)(2,1)}) custom-call(bf16[4,4,4,128,256]{4,3,2,1,0:T(8,128)(2,1)} %feat.5), custom_call_target="tpu_custom_call" | custom-call | bytes 6291456 | tf_op jit(solution)/shard_map/pack/pallas_call | solution.py:88
  10.1 1.7 %collective-permute-start.2 = (bf16[2,4,1,128,256]{4,3,2,1,0:T(8,128)(2,1)}, bf16[2,4,1,128,256]{4,3,2,1,0:T(8,128)(2,1)}, u32[]{:S(2)}, u32[]{:S(2)}) collective-permute-start(bf16[2,4,1,128,256]{4,3,2,1,0:T(8,128)(2,1)} %get-tuple-element.44), channel_id=1, source_target_pairs={{0,8},{8,16},{16,24},{24,0},{1,9},{9,17},{17,25},{25,1},{2,10},{10... | collective-permute-start | bytes 1572872 | tf_op jit(solution)/shard_map/ppermute | solution.py:547
  11.8 2.2 %collective-permute-start.3 = (bf16[2,4,1,128,256]{4,3,2,1,0:T(8,128)(2,1)}, bf16[2,4,1,128,256]{4,3,2,1,0:T(8,128)(2,1)}, u32[]{:S(2)}, u32[]{:S(2)}) collective-permute-start(bf16[2,4,1,128,256]{4,3,2,1,0:T(8,128)(2,1)} %get-tuple-element.45), channel_id=1, source_target_pairs={{0,24},{8,0},{16,8},{24,16},{1,25},{9,1},{17,9},{25,17},{2,26},{10... | collective-permute-start | bytes 1572872 | tf_op jit(solution)/shard_map/ppermute | solution.py:547
  14.0 4.8 %prep.1 = (bf16[16,128,512]{2,1,0:T(8,128)(2,1)}, bf16[768,256]{1,0:T(8,128)(2,1)}) custom-call(s32[16,4,128,128]{3,2,1,0:T(8,128)} %bitcast.21, bf16[256,256]{1,0:T(8,128)(2,1)} %ws_ref.3, bf16[3,256,256]{2,1,0:T(8,128)(2,1)} %wt_ref.3), custom_call_target="tpu_custom_call" | custom-call | flops 100663296 | bytes 8388608 | tf_op jit(solution)/shard_map/prep/pallas_call | solution.py:50
  18.8 2.2 %pack.7 = (bf16[2,4,1,128,256]{4,3,2,1,0:T(8,128)(2,1)}, bf16[2,4,1,128,256]{4,3,2,1,0:T(8,128)(2,1)}) custom-call(bf16[4,4,4,128,256]{4,3,2,1,0:T(8,128)(2,1)} %feat.5), custom_call_target="tpu_custom_call" | custom-call | bytes 6291456 | tf_op jit(solution)/shard_map/pack/pallas_call | solution.py:88
  21.1 0.1 collective-permute-start.8
  21.1 5.0 %collective-permute-done.2.rest_0_ = bf16[2,4,1,128,256]{4,3,2,1,0:T(8,128)(2,1)} collective-permute-done((bf16[2,4,1,128,256]{4,3,2,1,0:T(8,128)(2,1)}, bf16[2,4,1,128,256]{4,3,2,1,0:T(8,128)(2,1)}, u32[]{:S(2)}, u32[]{:S(2)}) %collective-permute-start.2) | collective-permute-done | bytes 524320 | tf_op jit(solution)/shard_map/ppermute | solution.py:547
  26.2 1.1 collective-permute-start.9
  27.3 0.7 reshape.40.codes
  28.0 0.0 collective-permute-done.3.rest_1_
  28.0 4.3 %aggregate.2 = bf16[2,2,4,128,256]{4,3,2,1,0:T(8,128)(2,1)} custom-call(s32[64]{0:T(128)} %reshape.40.codes, bf16[4,4,4,128,256]{4,3,2,1,0:T(8,128)(2,1)} %feat.5, bf16[2,4,1,128,256]{4,3,2,1,0:T(8,128)(2,1)} %collective-permute-done.2.rest_0_, bf16[2,4,1,128,256]{4,3,2,1,0:T(8,128)(2,1)} %collective-permute-done.3.rest_1_, ...), custom_call_target="tpu_custom_call" | custom-call | flops 536870912 | bytes 8388608 | tf_op jit(solution)/shard_map/aggregate/pallas_call | solution.py:179
  32.3 0.0 collective-permute-done.refs_0_.rest_2_.refs_2_
  32.3 0.0 collective-permute-done.1.refs_1_.rest_3_.refs_3_
  32.3 3.9 %collective-permute-start.11 = (bf16[2,1024,256]{2,1,0:T(8,128)(2,1)}, bf16[2,1024,256]{2,1,0:T(8,128)(2,1)}, u32[]{:S(2)}, u32[]{:S(2)}) collective-permute-start(bf16[2,1024,256]{2,1,0:T(8,128)(2,1)} %bitcast.19), channel_id=1, source_target_pairs={{0,1},{1,2},{2,3},{3,4},{4,5},{5,6},{6,7},{8,9},{9,10},{10,11},{11... | collective-permute-start | bytes 3145736 | tf_op jit(solution)/shard_map/ppermute | solution.py:583
  36.3 2.3 %pack.6 = (bf16[2,2,1,128,256]{4,3,2,1,0:T(8,128)(2,1)}, bf16[2,2,1,128,256]{4,3,2,1,0:T(8,128)(2,1)}, bf16[2,2,1,128,256]{4,3,2,1,0:T(8,128)(2,1)}, bf16[2,2,1,128,256]{4,3,2,1,0:T(8,128)(2,1)}) custom-call(bf16[4,1,4,128,256]{4,3,2,1,0:T(8,128)(2,1)} %collective-permute-done.refs_0_.rest_2_.refs_2_, ...), custom_call_target="tpu_custom_call" | custom-call | bytes 6291456 | tf_op jit(solution)/shard_map/pack/pallas_call | solution.py:88
  38.6 1.4 %collective-permute-start.6 = (bf16[2,2,1,128,256]{4,3,2,1,0:T(8,128)(2,1)}, bf16[2,2,1,128,256]{4,3,2,1,0:T(8,128)(2,1)}, u32[]{:S(2)}, u32[]{:S(2)}) collective-permute-start(bf16[2,2,1,128,256]{4,3,2,1,0:T(8,128)(2,1)} %get-tuple-element.52), channel_id=1, source_target_pairs={{0,8},{8,16},{16,24},{24,0},{1,9},{9,17},{17,25},{25,1},{2,10},{10... | collective-permute-start | bytes 786440 | tf_op jit(solution)/shard_map/ppermute | solution.py:547
  40.0 2.5 %collective-permute-start.7 = (bf16[2,2,1,128,256]{4,3,2,1,0:T(8,128)(2,1)}, bf16[2,2,1,128,256]{4,3,2,1,0:T(8,128)(2,1)}, u32[]{:S(2)}, u32[]{:S(2)}) collective-permute-start(bf16[2,2,1,128,256]{4,3,2,1,0:T(8,128)(2,1)} %get-tuple-element.53), channel_id=1, source_target_pairs={{0,24},{8,0},{16,8},{24,16},{1,25},{9,1},{17,9},{25,17},{2,26},{10... | collective-permute-start | bytes 786440 | tf_op jit(solution)/shard_map/ppermute | solution.py:547
  42.5 0.0 collective-permute-done.8.refs_0_
  42.5 0.0 collective-permute-start.4
  42.5 0.0 collective-permute-done.9.refs_1_
  42.5 2.7 %collective-permute-start.5 = (bf16[2,2,1,128,256]{4,3,2,1,0:T(8,128)(2,1)}, bf16[2,2,1,128,256]{4,3,2,1,0:T(8,128)(2,1)}, u32[]{:S(2)}, u32[]{:S(2)}) collective-permute-start(bf16[2,2,1,128,256]{4,3,2,1,0:T(8,128)(2,1)} %get-tuple-element.51), channel_id=1, source_target_pairs={{0,24},{8,0},{16,8},{24,16},{1,25},{9,1},{17,9},{25,17},{2,26},{10... | collective-permute-start | bytes 786440 | tf_op jit(solution)/shard_map/ppermute | solution.py:547
  45.2 1.8 %collective-permute-done.6.rest_4_ = bf16[2,2,1,128,256]{4,3,2,1,0:T(8,128)(2,1)} collective-permute-done((bf16[2,2,1,128,256]{4,3,2,1,0:T(8,128)(2,1)}, bf16[2,2,1,128,256]{4,3,2,1,0:T(8,128)(2,1)}, u32[]{:S(2)}, u32[]{:S(2)}) %collective-permute-start.6) | collective-permute-done | bytes 262176 | tf_op jit(solution)/shard_map/ppermute | solution.py:547
  47.0 0.0 collective-permute-done.7.rest_5_
  47.0 4.7 %aggregate.3 = (bf16[2,1,4,128,256]{4,3,2,1,0:T(8,128)(2,1)}, bf16[2,1,4,128,256]{4,3,2,1,0:T(8,128)(2,1)}) custom-call(s32[64]{0:T(128)} %reshape.40.codes, bf16[4,4,4,128,256]{4,3,2,1,0:T(8,128)(2,1)} %feat.5, bf16[2,4,1,128,256]{4,3,2,1,0:T(8,128)(2,1)} %collective-permute-done.2.rest_0_, bf16[2,4,1,128,256]{4,3,2,1,0:T(8,128)(2,1)} %collective-permute-done.3.rest_1_, ...), custom_call_target="tpu_custom_call" | custom-call | flops 536870912 | bytes 8388608 | tf_op jit(solution)/shard_map/aggregate/pallas_call | solution.py:179
  51.7 0.9 collective-permute-done.4.refs_4_
  52.6 0.0 collective-permute-done.5.refs_5_
  52.6 2.4 %collective-permute-start.12 = (bf16[2,512,256]{2,1,0:T(8,128)(2,1)}, bf16[2,512,256]{2,1,0:T(8,128)(2,1)}, u32[]{:S(2)}, u32[]{:S(2)}) collective-permute-start(bf16[2,512,256]{2,1,0:T(8,128)(2,1)} %bitcast.24), channel_id=1, source_target_pairs={{0,1},{1,2},{2,3},{3,4},{4,5},{5,6},{6,7},{8,9},{9,10},{10,11},{11... | collective-permute-start | bytes 1572872 | tf_op jit(solution)/shard_map/ppermute | solution.py:590
  55.0 3.6 %collective-permute-start.10 = (bf16[2,512,256]{2,1,0:T(8,128)(2,1)}, bf16[2,512,256]{2,1,0:T(8,128)(2,1)}, u32[]{:S(2)}, u32[]{:S(2)}) collective-permute-start(bf16[2,512,256]{2,1,0:T(8,128)(2,1)} %bitcast.22), channel_id=1, source_target_pairs={{0,1},{1,2},{2,3},{3,4},{4,5},{5,6},{6,7},{8,9},{9,10},{10,11},{11... | collective-permute-start | bytes 1572872 | tf_op jit(solution)/shard_map/ppermute | solution.py:591
  58.6 0.0 collective-permute-done.11.refs_10_
  58.6 16.2 %middle.1 = (bf16[2,2048,256]{2,1,0:T(8,128)(2,1)}, bf16[4,2048,256]{2,1,0:T(8,128)(2,1)}, f32[768,256]{1,0:T(8,128)}) custom-call(s32[64]{0:T(128)} %reshape.40.codes, bf16[4,4,4,128,256]{4,3,2,1,0:T(8,128)(2,1)} %feat.5, bf16[2,4,1,128,256]{4,3,2,1,0:T(8,128)(2,1)} %collective-permute-done.8.refs_0_, ...), custom_call_target="tpu_custom_call" | custom-call | flops 1 | bytes 1 | tf_op jit(solution)/shard_map/middle/pallas_call | solution.py:449
  74.8 0.0 collective-permute-done.12.refs_0_
  74.8 4.5 %mix.2 = (bf16[4,2048,256]{2,1,0:T(8,128)(2,1)}, f32[768,256]{1,0:T(8,128)}) custom-call(bf16[2,512,256]{2,1,0:T(8,128)(2,1)} %collective-permute-done.12.refs_0_, bf16[2,2048,256]{2,1,0:T(8,128)(2,1)} %get-tuple-element.68.refs_1_, bf16[4,2048,256]{2,1,0:T(8,128)(2,1)} %bitcast.13, bf16[4,2048,256]{2,1,0:T(8,128)(2,1)} %bitcast.16, ...), custom_call_target="tpu_custom_call", output_to_operand_aliasing={{0}: (7, {})} | custom-call | flops 1 | bytes 1 | tf_op jit(solution)/shard_map/mix/pallas_call | solution.py:313
  79.3 4.5 %mix.3 = (bf16[4,2048,256]{2,1,0:T(8,128)(2,1)}, f32[384,256]{1,0:T(8,128)}, f32[384,256]{1,0:T(8,128)}) custom-call(bf16[2,512,256]{2,1,0:T(8,128)(2,1)} %collective-permute-done.10.refs_0_, bf16[2,2048,256]{2,1,0:T(8,128)(2,1)} %get-tuple-element.68.refs_1_, bf16[4,2048,256]{2,1,0:T(8,128)(2,1)} %bitcast.14, ...), custom_call_target="tpu_custom_call", output_to_operand_aliasing={{0}: (7, {})} | custom-call | flops 1 | bytes 1 | tf_op jit(solution)/shard_map/mix/pallas_call | solution.py:313
  83.7 0.0 copy-start
  83.8 0.0 copy-start.1
  83.8 5.6 %collective-permute-start.13 = (f32[384,256]{1,0:T(8,128)}, f32[384,256]{1,0:T(8,128)S(1)}, u32[]{:S(2)}, u32[]{:S(2)}) collective-permute-start(f32[384,256]{1,0:T(8,128)} %get-tuple-element.76), channel_id=1, source_target_pairs={{0,32},{32,0},{1,33},{33,1},{2,34},{34,2},{3,35},{35,3},{4,36},{36... | collective-permute-start | bytes 1179656 | tf_op jit(solution)/shard_map/ppermute | solution.py:522
  89.4 1.6 %collective-permute-done.13 = f32[384,256]{1,0:T(8,128)S(1)} collective-permute-done((f32[384,256]{1,0:T(8,128)}, f32[384,256]{1,0:T(8,128)S(1)}, u32[]{:S(2)}, u32[]{:S(2)}) %collective-permute-start.13) | collective-permute-done | bytes 393248 | tf_op jit(solution)/shard_map/ppermute | solution.py:522
  91.0 1.0 add.5
  92.1 21.3 %all_to_all.10 = f32[64,8,256]{2,1,0:T(8,128)S(1)} all-to-all(f32[64,8,256]{2,1,0:T(8,128)S(1)} %pad_bitcast_fusion), channel_id=1, replica_groups=mesh['yh'=2,'core'=2,'gy'=4,'ta'=8] {'yh','gy','ta'}, dimensions={0} | all-to-all | bytes 1048576 | tf_op jit(solution)/shard_map/all_to_all | solution.py:524
  113.4 0.1 reduce_sum.9
  113.5 15.6 %all_to_all.11 = f32[64,8,256]{2,1,0:T(8,128)S(1)} all-to-all(f32[64,8,256]{2,1,0:T(8,128)S(1)} %broadcast_in_dim.2), channel_id=1, replica_groups=mesh['yh'=2,'core'=2,'gy'=4,'ta'=8] {'yh','gy','ta'}, dimensions={0} | all-to-all | bytes 1048576 | tf_op jit(solution)/shard_map/all_to_all | solution.py:526
  129.1 3.5 %collective-permute-start.14 = (f32[384,256]{1,0:T(8,128)S(1)}, f32[384,256]{1,0:T(8,128)S(1)}, u32[]{:S(2)}, u32[]{:S(2)}) collective-permute-start(f32[384,256]{1,0:T(8,128)S(1)} %slice_bitcast_fusion), channel_id=1, source_target_pairs={{0,32},{32,0},{1,33},{33,1},{2,34},{34,2},{3,35},{35,3},{4,36},{36... | collective-permute-start | bytes 1179656 | tf_op jit(solution)/shard_map/ppermute | solution.py:528
  132.7 1.3 collective-permute-done.14
  134.0 0.1 maximum_select_fusion.g_ref
  134.1 1.6 %finish.1 = (f32[256,256]{1,0:T(8,128)}, f32[3,256,256]{2,1,0:T(8,128)}) custom-call(f32[768,256]{1,0:T(8,128)S(1)} %maximum_select_fusion.g_ref, bf16[256,256]{1,0:T(8,128)(2,1)S(1)} %copy-done.1, bf16[3,256,256]{2,1,0:T(8,128)(2,1)S(1)} %copy-done), custom_call_target="tpu_custom_call" | custom-call | tf_op jit(solution)/shard_map/finish/pallas_call | solution.py:506
  (8 shorter events, 0.1 us)
Async XLA Ops:
  3.5 28.8 %collective-permute-start = (bf16[4,1,4,128,256]{4,3,2,1,0:T(8,128)(2,1)}, bf16[4,1,4,128,256]{4,3,2,1,0:T(8,128)(2,1)}, u32[]{:S(2)}, u32[]{:S(2)}) collective-permute-start(bf16[4,1,4,128,256]{4,3,2,1,0:T(8,128)(2,1)} %get-tuple-element.41), channel_id=1, source_target_pairs={{0,32},{32,64},{64,96},{96,0},{1,33},{33,65},{65,97},{97,1},{2,34}... | collective-permute-start | bytes 3145736 | tf_op jit(solution)/shard_map/ppermute | solution.py:547
  7.9 24.4 %collective-permute-start.1 = (bf16[4,1,4,128,256]{4,3,2,1,0:T(8,128)(2,1)}, bf16[4,1,4,128,256]{4,3,2,1,0:T(8,128)(2,1)}, u32[]{:S(2)}, u32[]{:S(2)}) collective-permute-start(bf16[4,1,4,128,256]{4,3,2,1,0:T(8,128)(2,1)} %get-tuple-element.42), channel_id=1, source_target_pairs={{0,96},{32,0},{64,32},{96,64},{1,97},{33,1},{65,33},{97,65},{2,98}... | collective-permute-start | bytes 3145736 | tf_op jit(solution)/shard_map/ppermute | solution.py:547
  10.1 16.0 %collective-permute-start.2 = (bf16[2,4,1,128,256]{4,3,2,1,0:T(8,128)(2,1)}, bf16[2,4,1,128,256]{4,3,2,1,0:T(8,128)(2,1)}, u32[]{:S(2)}, u32[]{:S(2)}) collective-permute-start(bf16[2,4,1,128,256]{4,3,2,1,0:T(8,128)(2,1)} %get-tuple-element.44), channel_id=1, source_target_pairs={{0,8},{8,16},{16,24},{24,0},{1,9},{9,17},{17,25},{25,1},{2,10},{10... | collective-permute-start | bytes 1572872 | tf_op jit(solution)/shard_map/ppermute | solution.py:547
  11.8 16.2 %collective-permute-start.3 = (bf16[2,4,1,128,256]{4,3,2,1,0:T(8,128)(2,1)}, bf16[2,4,1,128,256]{4,3,2,1,0:T(8,128)(2,1)}, u32[]{:S(2)}, u32[]{:S(2)}) collective-permute-start(bf16[2,4,1,128,256]{4,3,2,1,0:T(8,128)(2,1)} %get-tuple-element.45), channel_id=1, source_target_pairs={{0,24},{8,0},{16,8},{24,16},{1,25},{9,1},{17,9},{25,17},{2,26},{10... | collective-permute-start | bytes 1572872 | tf_op jit(solution)/shard_map/ppermute | solution.py:547
  14.0 13.3 %copy-start.2 = (s32[4,4,4]{2,1,0:T(4,128)S(1)}, s32[4,4,4]{2,1,0:T(4,128)}, u32[]{:S(2)}) copy-start(s32[4,4,4]{2,1,0:T(4,128)} %param.7) | copy-start | bytes 772
  21.1 21.4 %collective-permute-start.8 = (bf16[2,4,1,128,256]{4,3,2,1,0:T(8,128)(2,1)}, bf16[2,4,1,128,256]{4,3,2,1,0:T(8,128)(2,1)}, u32[]{:S(2)}, u32[]{:S(2)}) collective-permute-start(bf16[2,4,1,128,256]{4,3,2,1,0:T(8,128)(2,1)} %get-tuple-element.55), channel_id=1, source_target_pairs={{0,8},{8,16},{16,24},{24,0},{1,9},{9,17},{17,25},{25,1},{2,10},{10... | collective-permute-start | bytes 1572872 | tf_op jit(solution)/shard_map/ppermute | solution.py:547
  26.2 16.3 %collective-permute-start.9 = (bf16[2,4,1,128,256]{4,3,2,1,0:T(8,128)(2,1)}, bf16[2,4,1,128,256]{4,3,2,1,0:T(8,128)(2,1)}, u32[]{:S(2)}, u32[]{:S(2)}) collective-permute-start(bf16[2,4,1,128,256]{4,3,2,1,0:T(8,128)(2,1)} %get-tuple-element.56), channel_id=1, source_target_pairs={{0,24},{8,0},{16,8},{24,16},{1,25},{9,1},{17,9},{25,17},{2,26},{10... | collective-permute-start | bytes 1572872 | tf_op jit(solution)/shard_map/ppermute | solution.py:547
  32.3 26.2 %collective-permute-start.11 = (bf16[2,1024,256]{2,1,0:T(8,128)(2,1)}, bf16[2,1024,256]{2,1,0:T(8,128)(2,1)}, u32[]{:S(2)}, u32[]{:S(2)}) collective-permute-start(bf16[2,1024,256]{2,1,0:T(8,128)(2,1)} %bitcast.19), channel_id=1, source_target_pairs={{0,1},{1,2},{2,3},{3,4},{4,5},{5,6},{6,7},{8,9},{9,10},{10,11},{11... | collective-permute-start | bytes 3145736 | tf_op jit(solution)/shard_map/ppermute | solution.py:583
  38.6 8.4 %collective-permute-start.6 = (bf16[2,2,1,128,256]{4,3,2,1,0:T(8,128)(2,1)}, bf16[2,2,1,128,256]{4,3,2,1,0:T(8,128)(2,1)}, u32[]{:S(2)}, u32[]{:S(2)}) collective-permute-start(bf16[2,2,1,128,256]{4,3,2,1,0:T(8,128)(2,1)} %get-tuple-element.52), channel_id=1, source_target_pairs={{0,8},{8,16},{16,24},{24,0},{1,9},{9,17},{17,25},{25,1},{2,10},{10... | collective-permute-start | bytes 786440 | tf_op jit(solution)/shard_map/ppermute | solution.py:547
  40.0 7.0 %collective-permute-start.7 = (bf16[2,2,1,128,256]{4,3,2,1,0:T(8,128)(2,1)}, bf16[2,2,1,128,256]{4,3,2,1,0:T(8,128)(2,1)}, u32[]{:S(2)}, u32[]{:S(2)}) collective-permute-start(bf16[2,2,1,128,256]{4,3,2,1,0:T(8,128)(2,1)} %get-tuple-element.53), channel_id=1, source_target_pairs={{0,24},{8,0},{16,8},{24,16},{1,25},{9,1},{17,9},{25,17},{2,26},{10... | collective-permute-start | bytes 786440 | tf_op jit(solution)/shard_map/ppermute | solution.py:547
  42.5 10.1 %collective-permute-start.4 = (bf16[2,2,1,128,256]{4,3,2,1,0:T(8,128)(2,1)}, bf16[2,2,1,128,256]{4,3,2,1,0:T(8,128)(2,1)}, u32[]{:S(2)}, u32[]{:S(2)}) collective-permute-start(bf16[2,2,1,128,256]{4,3,2,1,0:T(8,128)(2,1)} %get-tuple-element.50), channel_id=1, source_target_pairs={{0,8},{8,16},{16,24},{24,0},{1,9},{9,17},{17,25},{25,1},{2,10},{10... | collective-permute-start | bytes 786440 | tf_op jit(solution)/shard_map/ppermute | solution.py:547
  42.5 10.1 %collective-permute-start.5 = (bf16[2,2,1,128,256]{4,3,2,1,0:T(8,128)(2,1)}, bf16[2,2,1,128,256]{4,3,2,1,0:T(8,128)(2,1)}, u32[]{:S(2)}, u32[]{:S(2)}) collective-permute-start(bf16[2,2,1,128,256]{4,3,2,1,0:T(8,128)(2,1)} %get-tuple-element.51), channel_id=1, source_target_pairs={{0,24},{8,0},{16,8},{24,16},{1,25},{9,1},{17,9},{25,17},{2,26},{10... | collective-permute-start | bytes 786440 | tf_op jit(solution)/shard_map/ppermute | solution.py:547
  52.6 22.2 %collective-permute-start.12 = (bf16[2,512,256]{2,1,0:T(8,128)(2,1)}, bf16[2,512,256]{2,1,0:T(8,128)(2,1)}, u32[]{:S(2)}, u32[]{:S(2)}) collective-permute-start(bf16[2,512,256]{2,1,0:T(8,128)(2,1)} %bitcast.24), channel_id=1, source_target_pairs={{0,1},{1,2},{2,3},{3,4},{4,5},{5,6},{6,7},{8,9},{9,10},{10,11},{11... | collective-permute-start | bytes 1572872 | tf_op jit(solution)/shard_map/ppermute | solution.py:590
  55.0 24.3 %collective-permute-start.10 = (bf16[2,512,256]{2,1,0:T(8,128)(2,1)}, bf16[2,512,256]{2,1,0:T(8,128)(2,1)}, u32[]{:S(2)}, u32[]{:S(2)}) collective-permute-start(bf16[2,512,256]{2,1,0:T(8,128)(2,1)} %bitcast.22), channel_id=1, source_target_pairs={{0,1},{1,2},{2,3},{3,4},{4,5},{5,6},{6,7},{8,9},{9,10},{10,11},{11... | collective-permute-start | bytes 1572872 | tf_op jit(solution)/shard_map/ppermute | solution.py:591
  83.7 50.3 %copy-start = (bf16[3,256,256]{2,1,0:T(8,128)(2,1)S(1)}, bf16[3,256,256]{2,1,0:T(8,128)(2,1)}, u32[]{:S(2)}) copy-start(bf16[3,256,256]{2,1,0:T(8,128)(2,1)} %wt_ref.3) | copy-start | bytes 1179652
  83.8 50.3 %copy-start.1 = (bf16[256,256]{1,0:T(8,128)(2,1)S(1)}, bf16[256,256]{1,0:T(8,128)(2,1)}, u32[]{:S(2)}) copy-start(bf16[256,256]{1,0:T(8,128)(2,1)} %ws_ref.3) | copy-start | bytes 393220
  83.8 7.2 %collective-permute-start.13 = (f32[384,256]{1,0:T(8,128)}, f32[384,256]{1,0:T(8,128)S(1)}, u32[]{:S(2)}, u32[]{:S(2)}) collective-permute-start(f32[384,256]{1,0:T(8,128)} %get-tuple-element.76), channel_id=1, source_target_pairs={{0,32},{32,0},{1,33},{33,1},{2,34},{34,2},{3,35},{35,3},{4,36},{36... | collective-permute-start | bytes 1179656 | tf_op jit(solution)/shard_map/ppermute | solution.py:522
  129.1 4.9 %collective-permute-start.14 = (f32[384,256]{1,0:T(8,128)S(1)}, f32[384,256]{1,0:T(8,128)S(1)}, u32[]{:S(2)}, u32[]{:S(2)}) collective-permute-start(f32[384,256]{1,0:T(8,128)S(1)} %slice_bitcast_fusion), channel_id=1, source_target_pairs={{0,32},{32,0},{1,33},{33,1},{2,34},{34,2},{3,35},{35,3},{4,36},{36... | collective-permute-start | bytes 1179656 | tf_op jit(solution)/shard_map/ppermute | solution.py:528

commit v8 on v7

--- a/solution.py
+++ b/solution.py
@@ -546,11 +546,6 @@
     def exchange(axis, high_edge, low_edge):
         return lax.ppermute(high_edge, axis, up), lax.ppermute(low_edge, axis, down)
 
-    def x_edges(source):
-        edge = (frames, 1, ny, lipids, width)
-        moves = [(0, (every, slice(nx - 1, nx)), 0, ()), (0, (every, low), 1, ())]
-        return pack([source], [edge, edge], moves)
-
     def y_edges(first, source):
         edge = (2, nx, 1, lipids, width)
         pair = slice(first, first + 2)
@@ -567,7 +562,7 @@
         ]
         return pack(x_halo, [corner] * 4, moves)
 
-    edges_x = x_edges(features)
+    edges_x = (features[:, nx - 1 :], features[:, :1])
     x_halo = exchange(GX, *edges_x)
     later, _ = lax.optimization_barrier((features, edges_x))
     edges_b = y_edges(2, later)

time: 136 us -> 136 us (level)
  local copies, waits for them, and re-layouts: 0.8 us -> 3.9 us
  Pallas kernels: 50.2 us -> 47.3 us
    slice x0 -> x1, local copies, waits for them, and re-layouts: none -> 3.1 us  [shards(): edges_x = (features[:, nx - 1:], features[:, :1])]
    pallas_call x4 -> x3, Pallas kernels: 9.62 us -> 6.72 us  [pack(): pl.pallas_call(functools.partial(pack_kernel, moves, len(arrays)), in_spe...]
where the time goes in v8:
time: 136 us
  Pallas kernels  47.3 us (35%)
  blocking collectives  36.9 us (27%)
  starting transfers between devices  35.1 us (26%)
  waiting for transfers between devices  10.6 us (8%)
  local copies, waits for them, and re-layouts  3.9 us (3%)
    all_to_all x1, blocking collectives, all_sum(): lax.all_to_all(mine.reshape(count, block, width), REST, 0, 0, tiled=True)  21.3 us
    pallas_call x1, Pallas kernels, middle(): pl.pallas_call(functools.partial(middle_kernel, row), in_specs=[pl.BlockS...  16.2 us
    all_to_all x1, blocking collectives, all_sum(): back = lax.all_to_all(spread, REST, 0, 0, tiled=True)  15.6 us
    pallas_call x2, Pallas kernels, aggregate(): pl.pallas_call(functools.partial(agg_kernel, first, xs, edge, pieces), in...  9.05 us
    pallas_call x2, Pallas kernels, mix(): pl.pallas_call(functools.partial(mix_kernel, half, chunks, (len(prevs), l...  8.93 us
    ppermute x5, starting transfers between devices, exchange(): lax.ppermute(low_edge, axis, down)  8.52 us
    ppermute x5, waiting for transfers between devices, exchange(): lax.ppermute(high_edge, axis, up)  7.69 us
    ppermute x5, starting transfers between devices, exchange(): lax.ppermute(high_edge, axis, up)  7.5 us
  transfers between devices with their start and end apart: 15, of which 5 were waited for; matrix products, arithmetic and copies ran while one was open for 1% of the time, Pallas kernels for 30%

profile of v8, /device:TPU:1, one launch (start us, length us, event | category | flops | bytes accessed | tf_op | source)
XLA Modules:
  0.0 135.8 jit_solution(4796359188493665184)
XLA Ops:
  0.6 3.1 %fusion = (bf16[4,1,4,128,256]{4,3,2,1,0:T(8,128)(2,1)}, bf16[4,1,4,128,256]{4,3,2,1,0:T(8,128)(2,1)}) fusion(bf16[4,4,4,128,256]{4,3,2,1,0:T(8,128)(2,1)} %feat.5), kind=kLoop, calls=%fused_computation.3 | loop fusion | bytes 4194304 | tf_op jit(solution)/shard_map/slice | solution.py:565
  3.7 4.3 %collective-permute-start = (bf16[4,1,4,128,256]{4,3,2,1,0:T(8,128)(2,1)}, bf16[4,1,4,128,256]{4,3,2,1,0:T(8,128)(2,1)}, u32[]{:S(2)}, u32[]{:S(2)}) collective-permute-start(bf16[4,1,4,128,256]{4,3,2,1,0:T(8,128)(2,1)} %get-tuple-element.76), channel_id=1, source_target_pairs={{0,32},{32,64},{64,96},{96,0},{1,33},{33,65},{65,97},{97,1},{2,34}... | collective-permute-start | bytes 3145736 | tf_op jit(solution)/shard_map/ppermute | solution.py:547
  8.0 0.0 collective-permute-start.1
  8.1 2.2 %pack.3 = (bf16[2,4,1,128,256]{4,3,2,1,0:T(8,128)(2,1)}, bf16[2,4,1,128,256]{4,3,2,1,0:T(8,128)(2,1)}) custom-call(bf16[4,4,4,128,256]{4,3,2,1,0:T(8,128)(2,1)} %feat.5), custom_call_target="tpu_custom_call" | custom-call | bytes 6291456 | tf_op jit(solution)/shard_map/pack/pallas_call | solution.py:88
  10.3 1.7 %collective-permute-start.2 = (bf16[2,4,1,128,256]{4,3,2,1,0:T(8,128)(2,1)}, bf16[2,4,1,128,256]{4,3,2,1,0:T(8,128)(2,1)}, u32[]{:S(2)}, u32[]{:S(2)}) collective-permute-start(bf16[2,4,1,128,256]{4,3,2,1,0:T(8,128)(2,1)} %get-tuple-element.40), channel_id=1, source_target_pairs={{0,8},{8,16},{16,24},{24,0},{1,9},{9,17},{17,25},{25,1},{2,10},{10... | collective-permute-start | bytes 1572872 | tf_op jit(solution)/shard_map/ppermute | solution.py:547
  11.9 2.2 %collective-permute-start.3 = (bf16[2,4,1,128,256]{4,3,2,1,0:T(8,128)(2,1)}, bf16[2,4,1,128,256]{4,3,2,1,0:T(8,128)(2,1)}, u32[]{:S(2)}, u32[]{:S(2)}) collective-permute-start(bf16[2,4,1,128,256]{4,3,2,1,0:T(8,128)(2,1)} %get-tuple-element.41), channel_id=1, source_target_pairs={{0,24},{8,0},{16,8},{24,16},{1,25},{9,1},{17,9},{25,17},{2,26},{10... | collective-permute-start | bytes 1572872 | tf_op jit(solution)/shard_map/ppermute | solution.py:547
  14.2 4.8 %prep.1 = (bf16[16,128,512]{2,1,0:T(8,128)(2,1)}, bf16[768,256]{1,0:T(8,128)(2,1)}) custom-call(s32[16,4,128,128]{3,2,1,0:T(8,128)} %bitcast.21, bf16[256,256]{1,0:T(8,128)(2,1)} %ws_ref.3, bf16[3,256,256]{2,1,0:T(8,128)(2,1)} %wt_ref.3), custom_call_target="tpu_custom_call" | custom-call | flops 100663296 | bytes 8388608 | tf_op jit(solution)/shard_map/prep/pallas_call | solution.py:50
  19.0 2.2 %pack.5 = (bf16[2,4,1,128,256]{4,3,2,1,0:T(8,128)(2,1)}, bf16[2,4,1,128,256]{4,3,2,1,0:T(8,128)(2,1)}) custom-call(bf16[4,4,4,128,256]{4,3,2,1,0:T(8,128)(2,1)} %feat.5), custom_call_target="tpu_custom_call" | custom-call | bytes 6291456 | tf_op jit(solution)/shard_map/pack/pallas_call | solution.py:88
  21.2 0.1 collective-permute-start.8
  21.3 5.0 %collective-permute-done.2.rest_0_ = bf16[2,4,1,128,256]{4,3,2,1,0:T(8,128)(2,1)} collective-permute-done((bf16[2,4,1,128,256]{4,3,2,1,0:T(8,128)(2,1)}, bf16[2,4,1,128,256]{4,3,2,1,0:T(8,128)(2,1)}, u32[]{:S(2)}, u32[]{:S(2)}) %collective-permute-start.2) | collective-permute-done | bytes 524320 | tf_op jit(solution)/shard_map/ppermute | solution.py:547
  26.3 1.1 collective-permute-start.9
  27.4 0.7 reshape.40.codes
  28.1 0.0 collective-permute-done.3.rest_1_
  28.1 4.3 %aggregate.2 = bf16[2,2,4,128,256]{4,3,2,1,0:T(8,128)(2,1)} custom-call(s32[64]{0:T(128)} %reshape.40.codes, bf16[4,4,4,128,256]{4,3,2,1,0:T(8,128)(2,1)} %feat.5, bf16[2,4,1,128,256]{4,3,2,1,0:T(8,128)(2,1)} %collective-permute-done.2.rest_0_, bf16[2,4,1,128,256]{4,3,2,1,0:T(8,128)(2,1)} %collective-permute-done.3.rest_1_, ...), custom_call_target="tpu_custom_call" | custom-call | flops 536870912 | bytes 8388608 | tf_op jit(solution)/shard_map/aggregate/pallas_call | solution.py:179
  32.4 0.0 collective-permute-done.refs_0_.rest_2_.refs_2_
  32.5 0.0 collective-permute-done.1.refs_1_.rest_3_.refs_3_
  32.5 3.9 %collective-permute-start.11 = (bf16[2,1024,256]{2,1,0:T(8,128)(2,1)}, bf16[2,1024,256]{2,1,0:T(8,128)(2,1)}, u32[]{:S(2)}, u32[]{:S(2)}) collective-permute-start(bf16[2,1024,256]{2,1,0:T(8,128)(2,1)} %bitcast.19), channel_id=1, source_target_pairs={{0,1},{1,2},{2,3},{3,4},{4,5},{5,6},{6,7},{8,9},{9,10},{10,11},{11... | collective-permute-start | bytes 3145736 | tf_op jit(solution)/shard_map/ppermute | solution.py:578
  36.4 2.3 %pack.4 = (bf16[2,2,1,128,256]{4,3,2,1,0:T(8,128)(2,1)}, bf16[2,2,1,128,256]{4,3,2,1,0:T(8,128)(2,1)}, bf16[2,2,1,128,256]{4,3,2,1,0:T(8,128)(2,1)}, bf16[2,2,1,128,256]{4,3,2,1,0:T(8,128)(2,1)}) custom-call(bf16[4,1,4,128,256]{4,3,2,1,0:T(8,128)(2,1)} %collective-permute-done.refs_0_.rest_2_.refs_2_, ...), custom_call_target="tpu_custom_call" | custom-call | bytes 6291456 | tf_op jit(solution)/shard_map/pack/pallas_call | solution.py:88
  38.7 1.4 %collective-permute-start.6 = (bf16[2,2,1,128,256]{4,3,2,1,0:T(8,128)(2,1)}, bf16[2,2,1,128,256]{4,3,2,1,0:T(8,128)(2,1)}, u32[]{:S(2)}, u32[]{:S(2)}) collective-permute-start(bf16[2,2,1,128,256]{4,3,2,1,0:T(8,128)(2,1)} %get-tuple-element.48), channel_id=1, source_target_pairs={{0,8},{8,16},{16,24},{24,0},{1,9},{9,17},{17,25},{25,1},{2,10},{10... | collective-permute-start | bytes 786440 | tf_op jit(solution)/shard_map/ppermute | solution.py:547
  40.1 2.5 %collective-permute-start.7 = (bf16[2,2,1,128,256]{4,3,2,1,0:T(8,128)(2,1)}, bf16[2,2,1,128,256]{4,3,2,1,0:T(8,128)(2,1)}, u32[]{:S(2)}, u32[]{:S(2)}) collective-permute-start(bf16[2,2,1,128,256]{4,3,2,1,0:T(8,128)(2,1)} %get-tuple-element.49), channel_id=1, source_target_pairs={{0,24},{8,0},{16,8},{24,16},{1,25},{9,1},{17,9},{25,17},{2,26},{10... | collective-permute-start | bytes 786440 | tf_op jit(solution)/shard_map/ppermute | solution.py:547
  42.6 0.0 collective-permute-done.8.refs_0_
  42.6 0.0 collective-permute-start.4
  42.6 0.0 collective-permute-done.9.refs_1_
  42.6 2.7 %collective-permute-start.5 = (bf16[2,2,1,128,256]{4,3,2,1,0:T(8,128)(2,1)}, bf16[2,2,1,128,256]{4,3,2,1,0:T(8,128)(2,1)}, u32[]{:S(2)}, u32[]{:S(2)}) collective-permute-start(bf16[2,2,1,128,256]{4,3,2,1,0:T(8,128)(2,1)} %get-tuple-element.47), channel_id=1, source_target_pairs={{0,24},{8,0},{16,8},{24,16},{1,25},{9,1},{17,9},{25,17},{2,26},{10... | collective-permute-start | bytes 786440 | tf_op jit(solution)/shard_map/ppermute | solution.py:547
  45.3 1.8 %collective-permute-done.6.rest_4_ = bf16[2,2,1,128,256]{4,3,2,1,0:T(8,128)(2,1)} collective-permute-done((bf16[2,2,1,128,256]{4,3,2,1,0:T(8,128)(2,1)}, bf16[2,2,1,128,256]{4,3,2,1,0:T(8,128)(2,1)}, u32[]{:S(2)}, u32[]{:S(2)}) %collective-permute-start.6) | collective-permute-done | bytes 262176 | tf_op jit(solution)/shard_map/ppermute | solution.py:547
  47.1 0.0 collective-permute-done.7.rest_5_
  47.1 4.7 %aggregate.3 = (bf16[2,1,4,128,256]{4,3,2,1,0:T(8,128)(2,1)}, bf16[2,1,4,128,256]{4,3,2,1,0:T(8,128)(2,1)}) custom-call(s32[64]{0:T(128)} %reshape.40.codes, bf16[4,4,4,128,256]{4,3,2,1,0:T(8,128)(2,1)} %feat.5, bf16[2,4,1,128,256]{4,3,2,1,0:T(8,128)(2,1)} %collective-permute-done.2.rest_0_, bf16[2,4,1,128,256]{4,3,2,1,0:T(8,128)(2,1)} %collective-permute-done.3.rest_1_, ...), custom_call_target="tpu_custom_call" | custom-call | flops 536870912 | bytes 8388608 | tf_op jit(solution)/shard_map/aggregate/pallas_call | solution.py:179
  51.9 0.9 collective-permute-done.4.refs_4_
  52.7 0.0 collective-permute-done.5.refs_5_
  52.7 2.4 %collective-permute-start.12 = (bf16[2,512,256]{2,1,0:T(8,128)(2,1)}, bf16[2,512,256]{2,1,0:T(8,128)(2,1)}, u32[]{:S(2)}, u32[]{:S(2)}) collective-permute-start(bf16[2,512,256]{2,1,0:T(8,128)(2,1)} %bitcast.24), channel_id=1, source_target_pairs={{0,1},{1,2},{2,3},{3,4},{4,5},{5,6},{6,7},{8,9},{9,10},{10,11},{11... | collective-permute-start | bytes 1572872 | tf_op jit(solution)/shard_map/ppermute | solution.py:585
  55.1 3.6 %collective-permute-start.10 = (bf16[2,512,256]{2,1,0:T(8,128)(2,1)}, bf16[2,512,256]{2,1,0:T(8,128)(2,1)}, u32[]{:S(2)}, u32[]{:S(2)}) collective-permute-start(bf16[2,512,256]{2,1,0:T(8,128)(2,1)} %bitcast.22), channel_id=1, source_target_pairs={{0,1},{1,2},{2,3},{3,4},{4,5},{5,6},{6,7},{8,9},{9,10},{10,11},{11... | collective-permute-start | bytes 1572872 | tf_op jit(solution)/shard_map/ppermute | solution.py:586
  58.7 0.0 collective-permute-done.11.refs_10_
  58.7 16.2 %middle.1 = (bf16[2,2048,256]{2,1,0:T(8,128)(2,1)}, bf16[4,2048,256]{2,1,0:T(8,128)(2,1)}, f32[768,256]{1,0:T(8,128)}) custom-call(s32[64]{0:T(128)} %reshape.40.codes, bf16[4,4,4,128,256]{4,3,2,1,0:T(8,128)(2,1)} %feat.5, bf16[2,4,1,128,256]{4,3,2,1,0:T(8,128)(2,1)} %collective-permute-done.8.refs_0_, ...), custom_call_target="tpu_custom_call" | custom-call | flops 1 | bytes 1 | tf_op jit(solution)/shard_map/middle/pallas_call | solution.py:449
  74.9 0.0 collective-permute-done.12.refs_0_
  74.9 4.5 %mix.2 = (bf16[4,2048,256]{2,1,0:T(8,128)(2,1)}, f32[768,256]{1,0:T(8,128)}) custom-call(bf16[2,512,256]{2,1,0:T(8,128)(2,1)} %collective-permute-done.12.refs_0_, bf16[2,2048,256]{2,1,0:T(8,128)(2,1)} %get-tuple-element.64.refs_1_, bf16[4,2048,256]{2,1,0:T(8,128)(2,1)} %bitcast.13, bf16[4,2048,256]{2,1,0:T(8,128)(2,1)} %bitcast.16, ...), custom_call_target="tpu_custom_call", output_to_operand_aliasing={{0}: (7, {})} | custom-call | flops 1 | bytes 1 | tf_op jit(solution)/shard_map/mix/pallas_call | solution.py:313
  79.4 4.5 %mix.3 = (bf16[4,2048,256]{2,1,0:T(8,128)(2,1)}, f32[384,256]{1,0:T(8,128)}, f32[384,256]{1,0:T(8,128)}) custom-call(bf16[2,512,256]{2,1,0:T(8,128)(2,1)} %collective-permute-done.10.refs_0_, bf16[2,2048,256]{2,1,0:T(8,128)(2,1)} %get-tuple-element.64.refs_1_, bf16[4,2048,256]{2,1,0:T(8,128)(2,1)} %bitcast.14, ...), custom_call_target="tpu_custom_call", output_to_operand_aliasing={{0}: (7, {})} | custom-call | flops 1 | bytes 1 | tf_op jit(solution)/shard_map/mix/pallas_call | solution.py:313
  83.9 0.0 copy-start
  83.9 0.0 copy-start.1
  83.9 5.6 %collective-permute-start.13 = (f32[384,256]{1,0:T(8,128)}, f32[384,256]{1,0:T(8,128)S(1)}, u32[]{:S(2)}, u32[]{:S(2)}) collective-permute-start(f32[384,256]{1,0:T(8,128)} %get-tuple-element.72), channel_id=1, source_target_pairs={{0,32},{32,0},{1,33},{33,1},{2,34},{34,2},{3,35},{35,3},{4,36},{36... | collective-permute-start | bytes 1179656 | tf_op jit(solution)/shard_map/ppermute | solution.py:522
  89.5 1.6 %collective-permute-done.13 = f32[384,256]{1,0:T(8,128)S(1)} collective-permute-done((f32[384,256]{1,0:T(8,128)}, f32[384,256]{1,0:T(8,128)S(1)}, u32[]{:S(2)}, u32[]{:S(2)}) %collective-permute-start.13) | collective-permute-done | bytes 393248 | tf_op jit(solution)/shard_map/ppermute | solution.py:522
  91.1 1.0 add.5
  92.2 21.3 %all_to_all.10 = f32[64,8,256]{2,1,0:T(8,128)S(1)} all-to-all(f32[64,8,256]{2,1,0:T(8,128)S(1)} %pad_bitcast_fusion), channel_id=1, replica_groups=mesh['yh'=2,'core'=2,'gy'=4,'ta'=8] {'yh','gy','ta'}, dimensions={0} | all-to-all | bytes 1048576 | tf_op jit(solution)/shard_map/all_to_all | solution.py:524
  113.5 0.1 reduce_sum.9
  113.6 15.6 %all_to_all.11 = f32[64,8,256]{2,1,0:T(8,128)S(1)} all-to-all(f32[64,8,256]{2,1,0:T(8,128)S(1)} %broadcast_in_dim.2), channel_id=1, replica_groups=mesh['yh'=2,'core'=2,'gy'=4,'ta'=8] {'yh','gy','ta'}, dimensions={0} | all-to-all | bytes 1048576 | tf_op jit(solution)/shard_map/all_to_all | solution.py:526
  129.3 3.5 %collective-permute-start.14 = (f32[384,256]{1,0:T(8,128)S(1)}, f32[384,256]{1,0:T(8,128)S(1)}, u32[]{:S(2)}, u32[]{:S(2)}) collective-permute-start(f32[384,256]{1,0:T(8,128)S(1)} %slice_bitcast_fusion), channel_id=1, source_target_pairs={{0,32},{32,0},{1,33},{33,1},{2,34},{34,2},{3,35},{35,3},{4,36},{36... | collective-permute-start | bytes 1179656 | tf_op jit(solution)/shard_map/ppermute | solution.py:528
  132.8 1.3 collective-permute-done.14
  134.1 0.1 maximum_select_fusion.g_ref
  134.2 1.6 %finish.1 = (f32[256,256]{1,0:T(8,128)}, f32[3,256,256]{2,1,0:T(8,128)}) custom-call(f32[768,256]{1,0:T(8,128)S(1)} %maximum_select_fusion.g_ref, bf16[256,256]{1,0:T(8,128)(2,1)S(1)} %copy-done.1, bf16[3,256,256]{2,1,0:T(8,128)(2,1)S(1)} %copy-done), custom_call_target="tpu_custom_call" | custom-call | tf_op jit(solution)/shard_map/finish/pallas_call | solution.py:506
  (8 shorter events, 0.1 us)
Async XLA Ops:
  3.7 28.7 %collective-permute-start = (bf16[4,1,4,128,256]{4,3,2,1,0:T(8,128)(2,1)}, bf16[4,1,4,128,256]{4,3,2,1,0:T(8,128)(2,1)}, u32[]{:S(2)}, u32[]{:S(2)}) collective-permute-start(bf16[4,1,4,128,256]{4,3,2,1,0:T(8,128)(2,1)} %get-tuple-element.76), channel_id=1, source_target_pairs={{0,32},{32,64},{64,96},{96,0},{1,33},{33,65},{65,97},{97,1},{2,34}... | collective-permute-start | bytes 3145736 | tf_op jit(solution)/shard_map/ppermute | solution.py:547
  8.0 24.4 %collective-permute-start.1 = (bf16[4,1,4,128,256]{4,3,2,1,0:T(8,128)(2,1)}, bf16[4,1,4,128,256]{4,3,2,1,0:T(8,128)(2,1)}, u32[]{:S(2)}, u32[]{:S(2)}) collective-permute-start(bf16[4,1,4,128,256]{4,3,2,1,0:T(8,128)(2,1)} %get-tuple-element.75), channel_id=1, source_target_pairs={{0,96},{32,0},{64,32},{96,64},{1,97},{33,1},{65,33},{97,65},{2,98}... | collective-permute-start | bytes 3145736 | tf_op jit(solution)/shard_map/ppermute | solution.py:547
  10.3 16.0 %collective-permute-start.2 = (bf16[2,4,1,128,256]{4,3,2,1,0:T(8,128)(2,1)}, bf16[2,4,1,128,256]{4,3,2,1,0:T(8,128)(2,1)}, u32[]{:S(2)}, u32[]{:S(2)}) collective-permute-start(bf16[2,4,1,128,256]{4,3,2,1,0:T(8,128)(2,1)} %get-tuple-element.40), channel_id=1, source_target_pairs={{0,8},{8,16},{16,24},{24,0},{1,9},{9,17},{17,25},{25,1},{2,10},{10... | collective-permute-start | bytes 1572872 | tf_op jit(solution)/shard_map/ppermute | solution.py:547
  11.9 16.2 %collective-permute-start.3 = (bf16[2,4,1,128,256]{4,3,2,1,0:T(8,128)(2,1)}, bf16[2,4,1,128,256]{4,3,2,1,0:T(8,128)(2,1)}, u32[]{:S(2)}, u32[]{:S(2)}) collective-permute-start(bf16[2,4,1,128,256]{4,3,2,1,0:T(8,128)(2,1)} %get-tuple-element.41), channel_id=1, source_target_pairs={{0,24},{8,0},{16,8},{24,16},{1,25},{9,1},{17,9},{25,17},{2,26},{10... | collective-permute-start | bytes 1572872 | tf_op jit(solution)/shard_map/ppermute | solution.py:547
  14.1 13.3 %copy-start.2 = (s32[4,4,4]{2,1,0:T(4,128)S(1)}, s32[4,4,4]{2,1,0:T(4,128)}, u32[]{:S(2)}) copy-start(s32[4,4,4]{2,1,0:T(4,128)} %param.7) | copy-start | bytes 772
  21.2 21.4 %collective-permute-start.8 = (bf16[2,4,1,128,256]{4,3,2,1,0:T(8,128)(2,1)}, bf16[2,4,1,128,256]{4,3,2,1,0:T(8,128)(2,1)}, u32[]{:S(2)}, u32[]{:S(2)}) collective-permute-start(bf16[2,4,1,128,256]{4,3,2,1,0:T(8,128)(2,1)} %get-tuple-element.51), channel_id=1, source_target_pairs={{0,8},{8,16},{16,24},{24,0},{1,9},{9,17},{17,25},{25,1},{2,10},{10... | collective-permute-start | bytes 1572872 | tf_op jit(solution)/shard_map/ppermute | solution.py:547
  26.3 16.3 %collective-permute-start.9 = (bf16[2,4,1,128,256]{4,3,2,1,0:T(8,128)(2,1)}, bf16[2,4,1,128,256]{4,3,2,1,0:T(8,128)(2,1)}, u32[]{:S(2)}, u32[]{:S(2)}) collective-permute-start(bf16[2,4,1,128,256]{4,3,2,1,0:T(8,128)(2,1)} %get-tuple-element.52), channel_id=1, source_target_pairs={{0,24},{8,0},{16,8},{24,16},{1,25},{9,1},{17,9},{25,17},{2,26},{10... | collective-permute-start | bytes 1572872 | tf_op jit(solution)/shard_map/ppermute | solution.py:547
  32.5 26.2 %collective-permute-start.11 = (bf16[2,1024,256]{2,1,0:T(8,128)(2,1)}, bf16[2,1024,256]{2,1,0:T(8,128)(2,1)}, u32[]{:S(2)}, u32[]{:S(2)}) collective-permute-start(bf16[2,1024,256]{2,1,0:T(8,128)(2,1)} %bitcast.19), channel_id=1, source_target_pairs={{0,1},{1,2},{2,3},{3,4},{4,5},{5,6},{6,7},{8,9},{9,10},{10,11},{11... | collective-permute-start | bytes 3145736 | tf_op jit(solution)/shard_map/ppermute | solution.py:578
  38.7 8.4 %collective-permute-start.6 = (bf16[2,2,1,128,256]{4,3,2,1,0:T(8,128)(2,1)}, bf16[2,2,1,128,256]{4,3,2,1,0:T(8,128)(2,1)}, u32[]{:S(2)}, u32[]{:S(2)}) collective-permute-start(bf16[2,2,1,128,256]{4,3,2,1,0:T(8,128)(2,1)} %get-tuple-element.48), channel_id=1, source_target_pairs={{0,8},{8,16},{16,24},{24,0},{1,9},{9,17},{17,25},{25,1},{2,10},{10... | collective-permute-start | bytes 786440 | tf_op jit(solution)/shard_map/ppermute | solution.py:547
  40.1 7.0 %collective-permute-start.7 = (bf16[2,2,1,128,256]{4,3,2,1,0:T(8,128)(2,1)}, bf16[2,2,1,128,256]{4,3,2,1,0:T(8,128)(2,1)}, u32[]{:S(2)}, u32[]{:S(2)}) collective-permute-start(bf16[2,2,1,128,256]{4,3,2,1,0:T(8,128)(2,1)} %get-tuple-element.49), channel_id=1, source_target_pairs={{0,24},{8,0},{16,8},{24,16},{1,25},{9,1},{17,9},{25,17},{2,26},{10... | collective-permute-start | bytes 786440 | tf_op jit(solution)/shard_map/ppermute | solution.py:547
  42.6 10.1 %collective-permute-start.4 = (bf16[2,2,1,128,256]{4,3,2,1,0:T(8,128)(2,1)}, bf16[2,2,1,128,256]{4,3,2,1,0:T(8,128)(2,1)}, u32[]{:S(2)}, u32[]{:S(2)}) collective-permute-start(bf16[2,2,1,128,256]{4,3,2,1,0:T(8,128)(2,1)} %get-tuple-element.46), channel_id=1, source_target_pairs={{0,8},{8,16},{16,24},{24,0},{1,9},{9,17},{17,25},{25,1},{2,10},{10... | collective-permute-start | bytes 786440 | tf_op jit(solution)/shard_map/ppermute | solution.py:547
  42.6 10.1 %collective-permute-start.5 = (bf16[2,2,1,128,256]{4,3,2,1,0:T(8,128)(2,1)}, bf16[2,2,1,128,256]{4,3,2,1,0:T(8,128)(2,1)}, u32[]{:S(2)}, u32[]{:S(2)}) collective-permute-start(bf16[2,2,1,128,256]{4,3,2,1,0:T(8,128)(2,1)} %get-tuple-element.47), channel_id=1, source_target_pairs={{0,24},{8,0},{16,8},{24,16},{1,25},{9,1},{17,9},{25,17},{2,26},{10... | collective-permute-start | bytes 786440 | tf_op jit(solution)/shard_map/ppermute | solution.py:547
  52.7 22.2 %collective-permute-start.12 = (bf16[2,512,256]{2,1,0:T(8,128)(2,1)}, bf16[2,512,256]{2,1,0:T(8,128)(2,1)}, u32[]{:S(2)}, u32[]{:S(2)}) collective-permute-start(bf16[2,512,256]{2,1,0:T(8,128)(2,1)} %bitcast.24), channel_id=1, source_target_pairs={{0,1},{1,2},{2,3},{3,4},{4,5},{5,6},{6,7},{8,9},{9,10},{10,11},{11... | collective-permute-start | bytes 1572872 | tf_op jit(solution)/shard_map/ppermute | solution.py:585
  55.1 24.3 %collective-permute-start.10 = (bf16[2,512,256]{2,1,0:T(8,128)(2,1)}, bf16[2,512,256]{2,1,0:T(8,128)(2,1)}, u32[]{:S(2)}, u32[]{:S(2)}) collective-permute-start(bf16[2,512,256]{2,1,0:T(8,128)(2,1)} %bitcast.22), channel_id=1, source_target_pairs={{0,1},{1,2},{2,3},{3,4},{4,5},{5,6},{6,7},{8,9},{9,10},{10,11},{11... | collective-permute-start | bytes 1572872 | tf_op jit(solution)/shard_map/ppermute | solution.py:586
  83.9 50.3 %copy-start = (bf16[3,256,256]{2,1,0:T(8,128)(2,1)S(1)}, bf16[3,256,256]{2,1,0:T(8,128)(2,1)}, u32[]{:S(2)}) copy-start(bf16[3,256,256]{2,1,0:T(8,128)(2,1)} %wt_ref.3) | copy-start | bytes 1179652
  83.9 50.3 %copy-start.1 = (bf16[256,256]{1,0:T(8,128)(2,1)S(1)}, bf16[256,256]{1,0:T(8,128)(2,1)}, u32[]{:S(2)}) copy-start(bf16[256,256]{1,0:T(8,128)(2,1)} %ws_ref.3) | copy-start | bytes 393220
  83.9 7.2 %collective-permute-start.13 = (f32[384,256]{1,0:T(8,128)}, f32[384,256]{1,0:T(8,128)S(1)}, u32[]{:S(2)}, u32[]{:S(2)}) collective-permute-start(f32[384,256]{1,0:T(8,128)} %get-tuple-element.72), channel_id=1, source_target_pairs={{0,32},{32,0},{1,33},{33,1},{2,34},{34,2},{3,35},{35,3},{4,36},{36... | collective-permute-start | bytes 1179656 | tf_op jit(solution)/shard_map/ppermute | solution.py:522
  129.3 4.9 %collective-permute-start.14 = (f32[384,256]{1,0:T(8,128)S(1)}, f32[384,256]{1,0:T(8,128)S(1)}, u32[]{:S(2)}, u32[]{:S(2)}) collective-permute-start(f32[384,256]{1,0:T(8,128)S(1)} %slice_bitcast_fusion), channel_id=1, source_target_pairs={{0,32},{32,0},{1,33},{33,1},{2,34},{34,2},{3,35},{35,3},{4,36},{36... | collective-permute-start | bytes 1179656 | tf_op jit(solution)/shard_map/ppermute | solution.py:528

commit v9 on v7

--- a/solution.py
+++ b/solution.py
@@ -13,7 +13,7 @@
 BF16 = jnp.bfloat16
 F32 = jnp.float32
 GX = ("yh", "core")
-MIX_ROWS = 256
+MIX_ROWS = 512
 VMEM = 65300 << 10
 EVERY = ("yh", "core", "gy", "ta")
 REST = ("yh", "gy", "ta")
@@ -147,7 +147,7 @@
             for y in range(ny):
                 places = []
                 for k in range(slots):
-                    code = codes[(x * ny + y) * slots + k]
+                    code = codes[x, y, k]
                     places.append(
                         (x - 1 + edge + lax.div(code, 3), y + lax.rem(code, 3))
                     )
@@ -400,7 +400,7 @@
                 tile = x * ny + y
                 parts = []
                 for k in range(slots):
-                    code = codes[tile * slots + k]
+                    code = codes[x, y, k]
                     parts.append(ext[f, x + lax.div(code, 3), y + lax.rem(code, 3)])
                 summed = jnp.dot(
                     mask_ref[tile],
@@ -535,7 +535,7 @@
 def shards(features, neighbours, adjacency, w_space, w_time, cotangent):
     frames, nx, ny, lipids, width = features.shape
     count = nx * ny * lipids
-    codes = neighbours.reshape(-1)
+    codes = neighbours
     up, down = ring(4, 1), ring(4, -1)
     onward = [(i, i + 1) for i in range(7)]
     inner, outer = tuple(range(1, nx - 1)), (0, nx - 1)

time: 136 us -> 136 us (level)
  blocking collectives: 36.9 us -> 39.3 us
  Pallas kernels: 50.2 us -> 48.3 us
    all_to_all x1, blocking collectives: 21.3 us -> 23.6 us  [all_sum(): lax.all_to_all(mine.reshape(count, block, width), REST, 0, 0, tiled=True)]
    pallas_call x1, Pallas kernels: 16.2 us -> 14.5 us  [middle(): pl.pallas_call(functools.partial(middle_kernel, row), in_specs=[pl.BlockS...]
    ppermute x1, starting transfers between devices: 5.64 us -> 4.27 us  [all_sum(): mine = keep + lax.ppermute(give, 'core', ring(2, 1))]
  transfers between devices with their start and end apart: 15 -> 15, of which waited for: 5 -> 6; matrix products, arithmetic and copies ran while one was open for 1% -> 0% of each run, Pallas kernels for 30% -> 29%
where the time goes in v9:
time: 136 us; the launch traced here: 135 us
  Pallas kernels  48.3 us (36%)
  blocking collectives  39.3 us (29%)
  starting transfers between devices  34.3 us (25%)
  waiting for transfers between devices  11.2 us (8%)
    all_to_all x1, blocking collectives, all_sum(): lax.all_to_all(mine.reshape(count, block, width), REST, 0, 0, tiled=True)  23.6 us
    all_to_all x1, blocking collectives, all_sum(): back = lax.all_to_all(spread, REST, 0, 0, tiled=True)  15.6 us
    pallas_call x1, Pallas kernels, middle(): pl.pallas_call(functools.partial(middle_kernel, row), in_specs=[pl.BlockS...  14.5 us
    pallas_call x4, Pallas kernels, pack(): pl.pallas_call(functools.partial(pack_kernel, moves, len(arrays)), in_spe...  9.63 us
    pallas_call x2, Pallas kernels, aggregate(): pl.pallas_call(functools.partial(agg_kernel, first, xs, edge, pieces), in...  9.3 us
    pallas_call x2, Pallas kernels, mix(): pl.pallas_call(functools.partial(mix_kernel, half, chunks, (len(prevs), l...  8.55 us
    ppermute x5, starting transfers between devices, exchange(): lax.ppermute(low_edge, axis, down)  8.52 us
    ppermute x5, waiting for transfers between devices, exchange(): lax.ppermute(high_edge, axis, up)  8.11 us
  transfers between devices with their start and end apart: 15, of which 6 were waited for; matrix products, arithmetic and copies ran while one was open for 0% of the time, Pallas kernels for 29%

profile of v9, /device:TPU:1, one launch (start us, length us, event | category | flops | bytes accessed | tf_op | source)
XLA Modules:
  0.0 135.3 jit_solution(1616630850494330440)
XLA Ops:
  0.6 2.9 %pack.4 = (bf16[4,1,4,128,256]{4,3,2,1,0:T(8,128)(2,1)}, bf16[4,1,4,128,256]{4,3,2,1,0:T(8,128)(2,1)}) custom-call(bf16[4,4,4,128,256]{4,3,2,1,0:T(8,128)(2,1)} %feat.5), custom_call_target="tpu_custom_call" | custom-call | bytes 6291456 | tf_op jit(solution)/shard_map/pack/pallas_call | solution.py:88
  3.5 4.4 %collective-permute-start = (bf16[4,1,4,128,256]{4,3,2,1,0:T(8,128)(2,1)}, bf16[4,1,4,128,256]{4,3,2,1,0:T(8,128)(2,1)}, u32[]{:S(2)}, u32[]{:S(2)}) collective-permute-start(bf16[4,1,4,128,256]{4,3,2,1,0:T(8,128)(2,1)} %get-tuple-element.41), channel_id=1, source_target_pairs={{0,32},{32,64},{64,96},{96,0},{1,33},{33,65},{65,97},{97,1},{2,34}... | collective-permute-start | bytes 3145736 | tf_op jit(solution)/shard_map/ppermute | solution.py:547
  7.9 0.0 collective-permute-start.1
  7.9 2.2 %pack.5 = (bf16[2,4,1,128,256]{4,3,2,1,0:T(8,128)(2,1)}, bf16[2,4,1,128,256]{4,3,2,1,0:T(8,128)(2,1)}) custom-call(bf16[4,4,4,128,256]{4,3,2,1,0:T(8,128)(2,1)} %feat.5), custom_call_target="tpu_custom_call" | custom-call | bytes 6291456 | tf_op jit(solution)/shard_map/pack/pallas_call | solution.py:88
  10.1 1.7 %collective-permute-start.2 = (bf16[2,4,1,128,256]{4,3,2,1,0:T(8,128)(2,1)}, bf16[2,4,1,128,256]{4,3,2,1,0:T(8,128)(2,1)}, u32[]{:S(2)}, u32[]{:S(2)}) collective-permute-start(bf16[2,4,1,128,256]{4,3,2,1,0:T(8,128)(2,1)} %get-tuple-element.44), channel_id=1, source_target_pairs={{0,8},{8,16},{16,24},{24,0},{1,9},{9,17},{17,25},{25,1},{2,10},{10... | collective-permute-start | bytes 1572872 | tf_op jit(solution)/shard_map/ppermute | solution.py:547
  11.8 2.2 %collective-permute-start.3 = (bf16[2,4,1,128,256]{4,3,2,1,0:T(8,128)(2,1)}, bf16[2,4,1,128,256]{4,3,2,1,0:T(8,128)(2,1)}, u32[]{:S(2)}, u32[]{:S(2)}) collective-permute-start(bf16[2,4,1,128,256]{4,3,2,1,0:T(8,128)(2,1)} %get-tuple-element.45), channel_id=1, source_target_pairs={{0,24},{8,0},{16,8},{24,16},{1,25},{9,1},{17,9},{25,17},{2,26},{10... | collective-permute-start | bytes 1572872 | tf_op jit(solution)/shard_map/ppermute | solution.py:547
  14.0 4.8 %prep.1 = (bf16[16,128,512]{2,1,0:T(8,128)(2,1)}, bf16[768,256]{1,0:T(8,128)(2,1)}) custom-call(s32[16,4,128,128]{3,2,1,0:T(8,128)} %bitcast.21, bf16[256,256]{1,0:T(8,128)(2,1)} %ws_ref.3, bf16[3,256,256]{2,1,0:T(8,128)(2,1)} %wt_ref.3), custom_call_target="tpu_custom_call" | custom-call | flops 100663296 | bytes 8388608 | tf_op jit(solution)/shard_map/prep/pallas_call | solution.py:50
  18.9 2.2 %pack.7 = (bf16[2,4,1,128,256]{4,3,2,1,0:T(8,128)(2,1)}, bf16[2,4,1,128,256]{4,3,2,1,0:T(8,128)(2,1)}) custom-call(bf16[4,4,4,128,256]{4,3,2,1,0:T(8,128)(2,1)} %feat.5), custom_call_target="tpu_custom_call" | custom-call | bytes 6291456 | tf_op jit(solution)/shard_map/pack/pallas_call | solution.py:88
  21.1 0.1 collective-permute-start.8
  21.2 5.0 %collective-permute-done.2.rest_0_ = bf16[2,4,1,128,256]{4,3,2,1,0:T(8,128)(2,1)} collective-permute-done((bf16[2,4,1,128,256]{4,3,2,1,0:T(8,128)(2,1)}, bf16[2,4,1,128,256]{4,3,2,1,0:T(8,128)(2,1)}, u32[]{:S(2)}, u32[]{:S(2)}) %collective-permute-start.2) | collective-permute-done | bytes 524320 | tf_op jit(solution)/shard_map/ppermute | solution.py:547
  26.2 1.1 collective-permute-start.9
  27.3 0.0 collective-permute-done.3.rest_1_
  27.3 4.4 %aggregate.2 = bf16[2,2,4,128,256]{4,3,2,1,0:T(8,128)(2,1)} custom-call(s32[4,4,4]{2,1,0:T(4,128)} %codes.5, bf16[4,4,4,128,256]{4,3,2,1,0:T(8,128)(2,1)} %feat.5, bf16[2,4,1,128,256]{4,3,2,1,0:T(8,128)(2,1)} %collective-permute-done.2.rest_0_, bf16[2,4,1,128,256]{4,3,2,1,0:T(8,128)(2,1)} %collective-permute-done.3.rest_1_, ...), custom_call_target="tpu_custom_call" | custom-call | flops 536870912 | bytes 8388608 | tf_op jit(solution)/shard_map/aggregate/pallas_call | solution.py:179
  31.7 0.0 collective-permute-done.refs_0_.rest_2_.refs_2_
  31.8 0.0 collective-permute-done.1.refs_1_.rest_3_.refs_3_
  31.8 4.5 %collective-permute-start.11 = (bf16[2,1024,256]{2,1,0:T(8,128)(2,1)}, bf16[2,1024,256]{2,1,0:T(8,128)(2,1)}, u32[]{:S(2)}, u32[]{:S(2)}) collective-permute-start(bf16[2,1024,256]{2,1,0:T(8,128)(2,1)} %bitcast.19), channel_id=1, source_target_pairs={{0,1},{1,2},{2,3},{3,4},{4,5},{5,6},{6,7},{8,9},{9,10},{10,11},{11... | collective-permute-start | bytes 3145736 | tf_op jit(solution)/shard_map/ppermute | solution.py:583
  36.2 2.3 %pack.6 = (bf16[2,2,1,128,256]{4,3,2,1,0:T(8,128)(2,1)}, bf16[2,2,1,128,256]{4,3,2,1,0:T(8,128)(2,1)}, bf16[2,2,1,128,256]{4,3,2,1,0:T(8,128)(2,1)}, bf16[2,2,1,128,256]{4,3,2,1,0:T(8,128)(2,1)}) custom-call(bf16[4,1,4,128,256]{4,3,2,1,0:T(8,128)(2,1)} %collective-permute-done.refs_0_.rest_2_.refs_2_, ...), custom_call_target="tpu_custom_call" | custom-call | bytes 6291456 | tf_op jit(solution)/shard_map/pack/pallas_call | solution.py:88
  38.6 1.4 %collective-permute-start.6 = (bf16[2,2,1,128,256]{4,3,2,1,0:T(8,128)(2,1)}, bf16[2,2,1,128,256]{4,3,2,1,0:T(8,128)(2,1)}, u32[]{:S(2)}, u32[]{:S(2)}) collective-permute-start(bf16[2,2,1,128,256]{4,3,2,1,0:T(8,128)(2,1)} %get-tuple-element.52), channel_id=1, source_target_pairs={{0,8},{8,16},{16,24},{24,0},{1,9},{9,17},{17,25},{25,1},{2,10},{10... | collective-permute-start | bytes 786440 | tf_op jit(solution)/shard_map/ppermute | solution.py:547
  40.0 2.5 %collective-permute-start.7 = (bf16[2,2,1,128,256]{4,3,2,1,0:T(8,128)(2,1)}, bf16[2,2,1,128,256]{4,3,2,1,0:T(8,128)(2,1)}, u32[]{:S(2)}, u32[]{:S(2)}) collective-permute-start(bf16[2,2,1,128,256]{4,3,2,1,0:T(8,128)(2,1)} %get-tuple-element.53), channel_id=1, source_target_pairs={{0,24},{8,0},{16,8},{24,16},{1,25},{9,1},{17,9},{25,17},{2,26},{10... | collective-permute-start | bytes 786440 | tf_op jit(solution)/shard_map/ppermute | solution.py:547
  42.5 0.0 collective-permute-done.8.refs_0_
  42.5 0.0 collective-permute-start.4
  42.5 0.0 collective-permute-done.9.refs_1_
  42.5 2.7 %collective-permute-start.5 = (bf16[2,2,1,128,256]{4,3,2,1,0:T(8,128)(2,1)}, bf16[2,2,1,128,256]{4,3,2,1,0:T(8,128)(2,1)}, u32[]{:S(2)}, u32[]{:S(2)}) collective-permute-start(bf16[2,2,1,128,256]{4,3,2,1,0:T(8,128)(2,1)} %get-tuple-element.51), channel_id=1, source_target_pairs={{0,24},{8,0},{16,8},{24,16},{1,25},{9,1},{17,9},{25,17},{2,26},{10... | collective-permute-start | bytes 786440 | tf_op jit(solution)/shard_map/ppermute | solution.py:547
  45.2 2.4 %collective-permute-done.6.rest_4_ = bf16[2,2,1,128,256]{4,3,2,1,0:T(8,128)(2,1)} collective-permute-done((bf16[2,2,1,128,256]{4,3,2,1,0:T(8,128)(2,1)}, bf16[2,2,1,128,256]{4,3,2,1,0:T(8,128)(2,1)}, u32[]{:S(2)}, u32[]{:S(2)}) %collective-permute-start.6) | collective-permute-done | bytes 262176 | tf_op jit(solution)/shard_map/ppermute | solution.py:547
  47.5 0.0 collective-permute-done.7.rest_5_
  47.5 4.9 %aggregate.3 = (bf16[2,1,4,128,256]{4,3,2,1,0:T(8,128)(2,1)}, bf16[2,1,4,128,256]{4,3,2,1,0:T(8,128)(2,1)}) custom-call(s32[4,4,4]{2,1,0:T(4,128)} %codes.5, bf16[4,4,4,128,256]{4,3,2,1,0:T(8,128)(2,1)} %feat.5, bf16[2,4,1,128,256]{4,3,2,1,0:T(8,128)(2,1)} %collective-permute-done.2.rest_0_, bf16[2,4,1,128,256]{4,3,2,1,0:T(8,128)(2,1)} %collective-permute-done.3.rest_1_, ...), custom_call_target="tpu_custom_call" | custom-call | flops 536870912 | bytes 8388608 | tf_op jit(solution)/shard_map/aggregate/pallas_call | solution.py:179
  52.4 0.7 collective-permute-done.4.refs_4_
  53.2 0.0 collective-permute-done.5.refs_5_
  53.2 2.4 %collective-permute-start.12 = (bf16[2,512,256]{2,1,0:T(8,128)(2,1)}, bf16[2,512,256]{2,1,0:T(8,128)(2,1)}, u32[]{:S(2)}, u32[]{:S(2)}) collective-permute-start(bf16[2,512,256]{2,1,0:T(8,128)(2,1)} %bitcast.24), channel_id=1, source_target_pairs={{0,1},{1,2},{2,3},{3,4},{4,5},{5,6},{6,7},{8,9},{9,10},{10,11},{11... | collective-permute-start | bytes 1572872 | tf_op jit(solution)/shard_map/ppermute | solution.py:590
  55.5 3.6 %collective-permute-start.10 = (bf16[2,512,256]{2,1,0:T(8,128)(2,1)}, bf16[2,512,256]{2,1,0:T(8,128)(2,1)}, u32[]{:S(2)}, u32[]{:S(2)}) collective-permute-start(bf16[2,512,256]{2,1,0:T(8,128)(2,1)} %bitcast.22), channel_id=1, source_target_pairs={{0,1},{1,2},{2,3},{3,4},{4,5},{5,6},{6,7},{8,9},{9,10},{10,11},{11... | collective-permute-start | bytes 1572872 | tf_op jit(solution)/shard_map/ppermute | solution.py:591
  59.1 0.0 collective-permute-done.11.refs_10_
  59.1 14.5 %middle.1 = (bf16[2,2048,256]{2,1,0:T(8,128)(2,1)}, bf16[4,2048,256]{2,1,0:T(8,128)(2,1)}, f32[768,256]{1,0:T(8,128)}) custom-call(s32[4,4,4]{2,1,0:T(4,128)} %codes.5, bf16[4,4,4,128,256]{4,3,2,1,0:T(8,128)(2,1)} %feat.5, bf16[2,4,1,128,256]{4,3,2,1,0:T(8,128)(2,1)} %collective-permute-done.8.refs_0_, ...), custom_call_target="tpu_custom_call" | custom-call | flops 1 | bytes 1 | tf_op jit(solution)/shard_map/middle/pallas_call | solution.py:449
  73.6 0.0 collective-permute-done.12.refs_0_
  73.6 4.3 %mix.2 = (bf16[4,2048,256]{2,1,0:T(8,128)(2,1)}, f32[768,256]{1,0:T(8,128)}) custom-call(bf16[2,512,256]{2,1,0:T(8,128)(2,1)} %collective-permute-done.12.refs_0_, bf16[2,2048,256]{2,1,0:T(8,128)(2,1)} %get-tuple-element.68.refs_1_, bf16[4,2048,256]{2,1,0:T(8,128)(2,1)} %bitcast.13, bf16[4,2048,256]{2,1,0:T(8,128)(2,1)} %bitcast.16, ...), custom_call_target="tpu_custom_call", output_to_operand_aliasing={{0}: (7, {})} | custom-call | flops 1 | bytes 1 | tf_op jit(solution)/shard_map/mix/pallas_call | solution.py:313
  77.9 0.2 collective-permute-done.10.refs_0_
  78.1 4.3 %mix.3 = (bf16[4,2048,256]{2,1,0:T(8,128)(2,1)}, f32[384,256]{1,0:T(8,128)}, f32[384,256]{1,0:T(8,128)}) custom-call(bf16[2,512,256]{2,1,0:T(8,128)(2,1)} %collective-permute-done.10.refs_0_, bf16[2,2048,256]{2,1,0:T(8,128)(2,1)} %get-tuple-element.68.refs_1_, bf16[4,2048,256]{2,1,0:T(8,128)(2,1)} %bitcast.14, ...), custom_call_target="tpu_custom_call", output_to_operand_aliasing={{0}: (7, {})} | custom-call | flops 1 | bytes 1 | tf_op jit(solution)/shard_map/mix/pallas_call | solution.py:313
  82.4 0.0 copy-start
  82.4 0.0 copy-start.1
  82.4 4.3 %collective-permute-start.13 = (f32[384,256]{1,0:T(8,128)}, f32[384,256]{1,0:T(8,128)S(1)}, u32[]{:S(2)}, u32[]{:S(2)}) collective-permute-start(f32[384,256]{1,0:T(8,128)} %get-tuple-element.76), channel_id=1, source_target_pairs={{0,32},{32,0},{1,33},{33,1},{2,34},{34,2},{3,35},{35,3},{4,36},{36... | collective-permute-start | bytes 1179656 | tf_op jit(solution)/shard_map/ppermute | solution.py:522
  86.7 1.6 %collective-permute-done.13 = f32[384,256]{1,0:T(8,128)S(1)} collective-permute-done((f32[384,256]{1,0:T(8,128)}, f32[384,256]{1,0:T(8,128)S(1)}, u32[]{:S(2)}, u32[]{:S(2)}) %collective-permute-start.13) | collective-permute-done | bytes 393248 | tf_op jit(solution)/shard_map/ppermute | solution.py:522
  88.2 1.0 add.5
  89.3 23.6 %all_to_all.10 = f32[64,8,256]{2,1,0:T(8,128)S(1)} all-to-all(f32[64,8,256]{2,1,0:T(8,128)S(1)} %pad_bitcast_fusion), channel_id=1, replica_groups=mesh['yh'=2,'core'=2,'gy'=4,'ta'=8] {'yh','gy','ta'}, dimensions={0} | all-to-all | bytes 1048576 | tf_op jit(solution)/shard_map/all_to_all | solution.py:524
  113.0 0.1 reduce_sum.9
  113.1 15.6 %all_to_all.11 = f32[64,8,256]{2,1,0:T(8,128)S(1)} all-to-all(f32[64,8,256]{2,1,0:T(8,128)S(1)} %broadcast_in_dim.2), channel_id=1, replica_groups=mesh['yh'=2,'core'=2,'gy'=4,'ta'=8] {'yh','gy','ta'}, dimensions={0} | all-to-all | bytes 1048576 | tf_op jit(solution)/shard_map/all_to_all | solution.py:526
  128.7 3.5 %collective-permute-start.14 = (f32[384,256]{1,0:T(8,128)S(1)}, f32[384,256]{1,0:T(8,128)S(1)}, u32[]{:S(2)}, u32[]{:S(2)}) collective-permute-start(f32[384,256]{1,0:T(8,128)S(1)} %slice_bitcast_fusion), channel_id=1, source_target_pairs={{0,32},{32,0},{1,33},{33,1},{2,34},{34,2},{3,35},{35,3},{4,36},{36... | collective-permute-start | bytes 1179656 | tf_op jit(solution)/shard_map/ppermute | solution.py:528
  132.3 1.3 collective-permute-done.14
  133.6 0.1 maximum_select_fusion.g_ref
  133.7 1.6 %finish.1 = (f32[256,256]{1,0:T(8,128)}, f32[3,256,256]{2,1,0:T(8,128)}) custom-call(f32[768,256]{1,0:T(8,128)S(1)} %maximum_select_fusion.g_ref, bf16[256,256]{1,0:T(8,128)(2,1)S(1)} %copy-done.1, bf16[3,256,256]{2,1,0:T(8,128)(2,1)S(1)} %copy-done), custom_call_target="tpu_custom_call" | custom-call | tf_op jit(solution)/shard_map/finish/pallas_call | solution.py:506
  (5 shorter events, 0.1 us)
Async XLA Ops:
  3.5 28.2 %collective-permute-start = (bf16[4,1,4,128,256]{4,3,2,1,0:T(8,128)(2,1)}, bf16[4,1,4,128,256]{4,3,2,1,0:T(8,128)(2,1)}, u32[]{:S(2)}, u32[]{:S(2)}) collective-permute-start(bf16[4,1,4,128,256]{4,3,2,1,0:T(8,128)(2,1)} %get-tuple-element.41), channel_id=1, source_target_pairs={{0,32},{32,64},{64,96},{96,0},{1,33},{33,65},{65,97},{97,1},{2,34}... | collective-permute-start | bytes 3145736 | tf_op jit(solution)/shard_map/ppermute | solution.py:547
  7.9 23.8 %collective-permute-start.1 = (bf16[4,1,4,128,256]{4,3,2,1,0:T(8,128)(2,1)}, bf16[4,1,4,128,256]{4,3,2,1,0:T(8,128)(2,1)}, u32[]{:S(2)}, u32[]{:S(2)}) collective-permute-start(bf16[4,1,4,128,256]{4,3,2,1,0:T(8,128)(2,1)} %get-tuple-element.42), channel_id=1, source_target_pairs={{0,96},{32,0},{64,32},{96,64},{1,97},{33,1},{65,33},{97,65},{2,98}... | collective-permute-start | bytes 3145736 | tf_op jit(solution)/shard_map/ppermute | solution.py:547
  10.1 16.0 %collective-permute-start.2 = (bf16[2,4,1,128,256]{4,3,2,1,0:T(8,128)(2,1)}, bf16[2,4,1,128,256]{4,3,2,1,0:T(8,128)(2,1)}, u32[]{:S(2)}, u32[]{:S(2)}) collective-permute-start(bf16[2,4,1,128,256]{4,3,2,1,0:T(8,128)(2,1)} %get-tuple-element.44), channel_id=1, source_target_pairs={{0,8},{8,16},{16,24},{24,0},{1,9},{9,17},{17,25},{25,1},{2,10},{10... | collective-permute-start | bytes 1572872 | tf_op jit(solution)/shard_map/ppermute | solution.py:547
  11.8 15.5 %collective-permute-start.3 = (bf16[2,4,1,128,256]{4,3,2,1,0:T(8,128)(2,1)}, bf16[2,4,1,128,256]{4,3,2,1,0:T(8,128)(2,1)}, u32[]{:S(2)}, u32[]{:S(2)}) collective-permute-start(bf16[2,4,1,128,256]{4,3,2,1,0:T(8,128)(2,1)} %get-tuple-element.45), channel_id=1, source_target_pairs={{0,24},{8,0},{16,8},{24,16},{1,25},{9,1},{17,9},{25,17},{2,26},{10... | collective-permute-start | bytes 1572872 | tf_op jit(solution)/shard_map/ppermute | solution.py:547
  21.1 21.4 %collective-permute-start.8 = (bf16[2,4,1,128,256]{4,3,2,1,0:T(8,128)(2,1)}, bf16[2,4,1,128,256]{4,3,2,1,0:T(8,128)(2,1)}, u32[]{:S(2)}, u32[]{:S(2)}) collective-permute-start(bf16[2,4,1,128,256]{4,3,2,1,0:T(8,128)(2,1)} %get-tuple-element.55), channel_id=1, source_target_pairs={{0,8},{8,16},{16,24},{24,0},{1,9},{9,17},{17,25},{25,1},{2,10},{10... | collective-permute-start | bytes 1572872 | tf_op jit(solution)/shard_map/ppermute | solution.py:547
  26.2 16.3 %collective-permute-start.9 = (bf16[2,4,1,128,256]{4,3,2,1,0:T(8,128)(2,1)}, bf16[2,4,1,128,256]{4,3,2,1,0:T(8,128)(2,1)}, u32[]{:S(2)}, u32[]{:S(2)}) collective-permute-start(bf16[2,4,1,128,256]{4,3,2,1,0:T(8,128)(2,1)} %get-tuple-element.56), channel_id=1, source_target_pairs={{0,24},{8,0},{16,8},{24,16},{1,25},{9,1},{17,9},{25,17},{2,26},{10... | collective-permute-start | bytes 1572872 | tf_op jit(solution)/shard_map/ppermute | solution.py:547
  31.8 27.4 %collective-permute-start.11 = (bf16[2,1024,256]{2,1,0:T(8,128)(2,1)}, bf16[2,1024,256]{2,1,0:T(8,128)(2,1)}, u32[]{:S(2)}, u32[]{:S(2)}) collective-permute-start(bf16[2,1024,256]{2,1,0:T(8,128)(2,1)} %bitcast.19), channel_id=1, source_target_pairs={{0,1},{1,2},{2,3},{3,4},{4,5},{5,6},{6,7},{8,9},{9,10},{10,11},{11... | collective-permute-start | bytes 3145736 | tf_op jit(solution)/shard_map/ppermute | solution.py:583
  38.6 9.0 %collective-permute-start.6 = (bf16[2,2,1,128,256]{4,3,2,1,0:T(8,128)(2,1)}, bf16[2,2,1,128,256]{4,3,2,1,0:T(8,128)(2,1)}, u32[]{:S(2)}, u32[]{:S(2)}) collective-permute-start(bf16[2,2,1,128,256]{4,3,2,1,0:T(8,128)(2,1)} %get-tuple-element.52), channel_id=1, source_target_pairs={{0,8},{8,16},{16,24},{24,0},{1,9},{9,17},{17,25},{25,1},{2,10},{10... | collective-permute-start | bytes 786440 | tf_op jit(solution)/shard_map/ppermute | solution.py:547
  40.0 7.6 %collective-permute-start.7 = (bf16[2,2,1,128,256]{4,3,2,1,0:T(8,128)(2,1)}, bf16[2,2,1,128,256]{4,3,2,1,0:T(8,128)(2,1)}, u32[]{:S(2)}, u32[]{:S(2)}) collective-permute-start(bf16[2,2,1,128,256]{4,3,2,1,0:T(8,128)(2,1)} %get-tuple-element.53), channel_id=1, source_target_pairs={{0,24},{8,0},{16,8},{24,16},{1,25},{9,1},{17,9},{25,17},{2,26},{10... | collective-permute-start | bytes 786440 | tf_op jit(solution)/shard_map/ppermute | solution.py:547
  42.5 10.7 %collective-permute-start.4 = (bf16[2,2,1,128,256]{4,3,2,1,0:T(8,128)(2,1)}, bf16[2,2,1,128,256]{4,3,2,1,0:T(8,128)(2,1)}, u32[]{:S(2)}, u32[]{:S(2)}) collective-permute-start(bf16[2,2,1,128,256]{4,3,2,1,0:T(8,128)(2,1)} %get-tuple-element.50), channel_id=1, source_target_pairs={{0,8},{8,16},{16,24},{24,0},{1,9},{9,17},{17,25},{25,1},{2,10},{10... | collective-permute-start | bytes 786440 | tf_op jit(solution)/shard_map/ppermute | solution.py:547
  42.5 10.7 %collective-permute-start.5 = (bf16[2,2,1,128,256]{4,3,2,1,0:T(8,128)(2,1)}, bf16[2,2,1,128,256]{4,3,2,1,0:T(8,128)(2,1)}, u32[]{:S(2)}, u32[]{:S(2)}) collective-permute-start(bf16[2,2,1,128,256]{4,3,2,1,0:T(8,128)(2,1)} %get-tuple-element.51), channel_id=1, source_target_pairs={{0,24},{8,0},{16,8},{24,16},{1,25},{9,1},{17,9},{25,17},{2,26},{10... | collective-permute-start | bytes 786440 | tf_op jit(solution)/shard_map/ppermute | solution.py:547
  53.2 20.5 %collective-permute-start.12 = (bf16[2,512,256]{2,1,0:T(8,128)(2,1)}, bf16[2,512,256]{2,1,0:T(8,128)(2,1)}, u32[]{:S(2)}, u32[]{:S(2)}) collective-permute-start(bf16[2,512,256]{2,1,0:T(8,128)(2,1)} %bitcast.24), channel_id=1, source_target_pairs={{0,1},{1,2},{2,3},{3,4},{4,5},{5,6},{6,7},{8,9},{9,10},{10,11},{11... | collective-permute-start | bytes 1572872 | tf_op jit(solution)/shard_map/ppermute | solution.py:590
  55.5 22.5 %collective-permute-start.10 = (bf16[2,512,256]{2,1,0:T(8,128)(2,1)}, bf16[2,512,256]{2,1,0:T(8,128)(2,1)}, u32[]{:S(2)}, u32[]{:S(2)}) collective-permute-start(bf16[2,512,256]{2,1,0:T(8,128)(2,1)} %bitcast.22), channel_id=1, source_target_pairs={{0,1},{1,2},{2,3},{3,4},{4,5},{5,6},{6,7},{8,9},{9,10},{10,11},{11... | collective-permute-start | bytes 1572872 | tf_op jit(solution)/shard_map/ppermute | solution.py:591
  82.4 51.3 %copy-start = (bf16[3,256,256]{2,1,0:T(8,128)(2,1)S(1)}, bf16[3,256,256]{2,1,0:T(8,128)(2,1)}, u32[]{:S(2)}) copy-start(bf16[3,256,256]{2,1,0:T(8,128)(2,1)} %wt_ref.3) | copy-start | bytes 1179652
  82.4 51.3 %copy-start.1 = (bf16[256,256]{1,0:T(8,128)(2,1)S(1)}, bf16[256,256]{1,0:T(8,128)(2,1)}, u32[]{:S(2)}) copy-start(bf16[256,256]{1,0:T(8,128)(2,1)} %ws_ref.3) | copy-start | bytes 393220
  82.4 5.8 %collective-permute-start.13 = (f32[384,256]{1,0:T(8,128)}, f32[384,256]{1,0:T(8,128)S(1)}, u32[]{:S(2)}, u32[]{:S(2)}) collective-permute-start(f32[384,256]{1,0:T(8,128)} %get-tuple-element.76), channel_id=1, source_target_pairs={{0,32},{32,0},{1,33},{33,1},{2,34},{34,2},{3,35},{35,3},{4,36},{36... | collective-permute-start | bytes 1179656 | tf_op jit(solution)/shard_map/ppermute | solution.py:522
  128.7 4.9 %collective-permute-start.14 = (f32[384,256]{1,0:T(8,128)S(1)}, f32[384,256]{1,0:T(8,128)S(1)}, u32[]{:S(2)}, u32[]{:S(2)}) collective-permute-start(f32[384,256]{1,0:T(8,128)S(1)} %slice_bitcast_fusion), channel_id=1, source_target_pairs={{0,32},{32,0},{1,33},{33,1},{2,34},{34,2},{3,35},{35,3},{4,36},{36... | collective-permute-start | bytes 1179656 | tf_op jit(solution)/shard_map/ppermute | solution.py:528
